TPU v7x, 256 devices: a whole 4x4x8 slice. The times are simulated.
256 devices in a mesh: tm: 4 (over y), row: 4 (over x), col: 16 (over z, core).
Axes of the slice: x: 4, y: 4, z: 8, core: 2. Of those that a mesh axis runs over, the one named last changes fastest.
Arguments:
- features: bfloat16 [16, 8, 160, 512], P('tm', 'row', 'col'), may hold values from -4200 to 4200, as said below
- gain_low: float32 [512], replicated, may hold values from 0.1 to 1.9
- bias_low: float32 [512], replicated, may hold values from -3 to 3
- w_up: bfloat16 [3, 3, 3, 512, 256], replicated, may hold values from -0.0546875 to 0.0546875
- b_up: float32 [256], replicated, may hold values from -3 to 3
- gain_high: float32 [256], replicated, may hold values from 0.1 to 1.9
- bias_high: float32 [256], replicated, may hold values from -3 to 3
- w_res: bfloat16 [3, 3, 3, 256, 256], replicated, may hold values from -0.078125 to 0.078125
- b_res: float32 [256], replicated, may hold values from -3 to 3
Outputs:
- decoded: bfloat16 [16, 16, 320, 256], P('tm', 'row', 'col')
Inputs may be any that keep to these rules, and one draw needn't show every extreme that they name: Decoder features of order one to a few thousand.
All inputs are finite; a program needn't handle non-finite values.
Results may differ from a plain program's by a relative error of at most 0.013.
Values may be sent and summed in bfloat16 or wider, within the bound.
No kernel may reach another device: no remote copies, remote signals or barrier semaphores. Data moves between devices by JAX's collectives and lax.ppermute only.
A program may use at most 64 MiB of HBM per device.

v0:
```python
import jax
import jax.numpy as jnp
from jax import lax
from jax.sharding import PartitionSpec as P

GROUPS = 32


def entering(value, axis, join, neutral):
    count, mine = (lax.axis_size(axis), lax.axis_index(axis))
    pieces = lax.all_gather(value, axis)
    total = jnp.full_like(value, 0) + jnp.asarray(neutral, value.dtype)

    def step(position, total):
        longer = join(total, pieces[position])
        return jnp.where(position < mine, longer, total)

    return lax.fori_loop(0, count - 1, step, total)


def passed_along(block, axis, distance):
    devices = range(lax.axis_size(axis))
    route = [(i - distance, i) for i in devices if i - distance in devices]
    return lax.ppermute(block, axis, route)


def extended(cells, sides, width):
    for axis, dim in sides:
        count = lax.axis_size(axis)
        ends = count - 1
        head = lax.slice_in_dim(cells, 0, width, axis=dim)
        tail = lax.slice_in_dim(cells, cells.shape[dim] - width, cells.shape[dim], axis=dim)
        cells = jnp.concatenate(
            [
                lax.ppermute(tail, axis, [(i, (i + 1) % count) for i in range(ends)]),
                cells,
                lax.ppermute(head, axis, [((i + 1) % count, i) for i in range(ends)]),
            ],
            axis=dim,
        )
    return cells


def add_sums(earlier, later):
    return earlier + later


def activate(field_in, gain, bias):
    frames, height, across, channels = field_in.shape
    per_group = channels // GROUPS
    grouped = field_in.reshape(frames, height, across, GROUPS, per_group)
    partial_value = jnp.stack(
        [jnp.sum(grouped, axis=(0, 1, 2, 4)), jnp.sum(grouped * grouped, axis=(0, 1, 2, 4))]
    )
    totals = lax.psum(partial_value, ("row", "col"))
    before = entering(totals, "tm", add_sums, jnp.zeros_like(totals))
    running = before + totals
    spread_cells = (
        frames * height * across * per_group * lax.axis_size("row") * lax.axis_size("col")
    )
    cells_seen = (lax.axis_index("tm") + 1).astype(jnp.float32) * float(spread_cells)
    group_mean = running[0] / cells_seen
    group_var = running[1] / cells_seen - group_mean * group_mean
    inv_std = lax.rsqrt(group_var + 1e-06)
    normed = (field_in - jnp.repeat(group_mean, per_group)) * jnp.repeat(
        inv_std, per_group
    ) * gain + bias
    return jax.nn.silu(normed).astype(jnp.bfloat16)


def conv_taps(padded, weight):
    frames = padded.shape[0] - 2
    height = padded.shape[1] - 2
    across = padded.shape[2] - 2
    summed = jnp.zeros((frames * height * across, weight.shape[-1]), jnp.float32)
    for tap_t in range(3):
        for tap_r in range(3):
            for tap_c in range(3):
                tapped = padded[
                    tap_t : tap_t + frames, tap_r : tap_r + height, tap_c : tap_c + across
                ]
                summed = summed + jnp.dot(
                    tapped.reshape(-1, padded.shape[-1]),
                    weight[tap_t, tap_r, tap_c],
                    preferred_element_type=jnp.float32,
                )
    return summed.reshape(frames, height, across, weight.shape[-1])


def upsample(field_in):
    return jnp.repeat(jnp.repeat(field_in, 2, axis=1), 2, axis=2)


def local(features, gain_low, bias_low, w_up, b_up, gain_high, bias_high, w_res, b_res):
    first = activate(features.astype(jnp.float32), gain_low, bias_low)
    upsampled = upsample(first)
    carried = passed_along(upsampled[-2:], "tm", 1)
    stacked = jnp.concatenate([carried, upsampled], axis=0)
    padded = extended(stacked, (("row", 1), ("col", 2)), 1)
    hidden = (conv_taps(padded, w_up) + b_up).astype(jnp.bfloat16)
    hidden_f = hidden.astype(jnp.float32)
    second = activate(hidden_f, gain_high, bias_high)
    carried_high = passed_along(second[-2:], "tm", 1)
    stacked_high = jnp.concatenate([carried_high, second], axis=0)
    padded_high = extended(stacked_high, (("row", 1), ("col", 2)), 1)
    return (conv_taps(padded_high, w_res) + b_res + hidden_f).astype(jnp.bfloat16)


def solution(mesh):
    in_specs = (P("tm", "row", "col", None), P(), P(), P(), P(), P(), P(), P(), P())
    out_specs = P("tm", "row", "col", None)
    return jax.shard_map(local, mesh=mesh, in_specs=in_specs, out_specs=out_specs, check_vma=False)
```

profile of v0, /device:TPU:1, one launch (start us, length us, event | category | flops | bytes accessed | tf_op | source)
XLA Modules:
  0.0 401.8 jit_solution(6312064981148808690)
XLA Ops:
  1.4 128.0 %psum.14 = f32[2,32]{1,0:T(2,128)S(1)} all-reduce(f32[2,32]{1,0:T(2,128)S(1)} %pad_maximum_fusion.14), channel_id=1, replica_groups=mesh['tm'=4,'row'=4,'col'=16] {'row','col'}, use_global_device_ids=true, to_apply=%region_4.5 | all-reduce | flops 64 | bytes 512 | tf_op jit(solution)/shard_map/psum | solution.py:55
  129.5 7.9 %all-gather.2 = f32[4,2,32]{2,1,0:T(2,128)S(1)} all-gather(f32[1,2,32]{2,1,0:T(2,128)S(1)} %bitcast.265), channel_id=2, replica_groups=mesh['tm'=4,'row'=4,'col'=16] {'tm'}, dimensions={0}, use_global_device_ids=true | all-gather | bytes 1280 | tf_op jit(solution)/shard_map/all_gather | solution.py:11
  139.2 1.3 collective-permute-start
  143.5 1.3 collective-permute-start.2
  144.8 4.0 collective-permute-start.1
  152.0 10.8 %collective-permute-start.4 = (bf16[6,6,1,512]{3,1,2,0:T(8,128)(2,1)S(1)}, bf16[6,6,1,512]{3,1,2,0:T(8,128)(2,1)S(1)}, u32[]{:S(2)}, u32[]{:S(2)}) collective-permute-start(bf16[6,6,1,512]{3,1,2,0:T(8,128)(2,1)S(1)} %get-tuple-element.246), channel_id=1, source_target_pairs={{1,0},{2,1},{3,2},{4,3},{5,4},{6,5},{7,6},{8,7},{9,8},{10,9},{11,1... | collective-permute-start | bytes 110600 | tf_op jit(solution)/shard_map/ppermute | solution.py:37
  162.8 1.9 collective-permute-start.3
  171.7 1.7 pad_maximum_fusion
  173.4 4.1 %fusion.154 = (bf16[4,4,20,512]{3,1,2,0:T(4,128)(2,1)}, bf16[4,4,20,512]{3,1,2,0:T(4,128)(2,1)}, bf16[4,4,20,512]{3,1,2,0:T(4,128)(2,1)}, bf16[4,4,20,512]{3,1,2...) fusion(bf16[6,6,21,512]{3,1,2,0:T(8,128)(2,1)S(1)} %get-tuple-e, ...), kind=kLoop, calls=%fused_computation.253 | loop fusion | bytes 11796480 | tf_op jit(solution)/shard_map/slice | solution.py:79
  201.1 1.4 fusion.48
  202.6 1.6 convolution_add_fusion.50
  204.2 1.3 convolution_add_fusion.49
  205.5 1.3 convolution_add_fusion.48
  206.9 1.2 convolution_add_fusion.47
  208.2 1.2 convolution_add_fusion.46
  209.4 1.2 convolution_add_fusion.45
  217.3 123.9 %psum.15 = f32[2,32]{1,0:T(2,128)S(1)} all-reduce(f32[2,32]{1,0:T(2,128)S(1)} %pad_maximum_fusion.15), channel_id=1, replica_groups=mesh['tm'=4,'row'=4,'col'=16] {'row','col'}, use_global_device_ids=true, to_apply=%region_11.12 | all-reduce | flops 64 | bytes 512 | tf_op jit(solution)/shard_map/psum | solution.py:55
  341.2 7.6 %all-gather.3 = f32[4,2,32]{2,1,0:T(2,128)S(1)} all-gather(f32[1,2,32]{2,1,0:T(2,128)S(1)} %bitcast.264), channel_id=3, replica_groups=mesh['tm'=4,'row'=4,'col'=16] {'tm'}, dimensions={0}, use_global_device_ids=true | all-gather | bytes 1280 | tf_op jit(solution)/shard_map/all_gather | solution.py:11
  349.5 2.1 collective-permute-start.5
  351.6 1.6 collective-permute-done.5
  353.2 1.3 collective-permute-start.7
  354.5 4.0 collective-permute-start.6
  360.0 2.6 collective-permute-start.8
  362.6 5.5 %collective-permute-start.9 = (bf16[6,6,1,256]{3,2,1,0:T(2,128)(2,1)S(1)}, bf16[6,6,1,256]{3,2,1,0:T(2,128)(2,1)S(1)}, u32[]{:S(2)}, u32[]{:S(2)}) collective-permute-start(bf16[6,6,1,256]{3,2,1,0:T(2,128)(2,1)S(1)} %get-tuple-element.275), channel_id=1, source_target_pairs={{1,0},{2,1},{3,2},{4,3},{5,4},{6,5},{7,6},{8,7},{9,8},{10,9},{11,1... | collective-permute-start | bytes 55304 | tf_op jit(solution)/shard_map/ppermute | solution.py:37
  377.6 1.6 reshape.233
  379.9 1.6 reshape.236
  382.2 1.6 reshape.239
  384.5 1.6 reshape.242
  386.2 1.6 reshape.245
  389.4 1.2 convolution_add_fusion.24
  390.7 1.2 convolution_add_fusion.23
  391.9 1.2 convolution_add_fusion.22
  (297 shorter events, 69.3 us)
Async XLA Ops:
  139.2 3.6 collective-permute-start
  143.5 7.5 %collective-permute-start.2 = (bf16[6,1,20,512]{3,1,2,0:T(2,128)(2,1)S(1)}, bf16[6,1,20,512]{3,1,2,0:T(2,128)(2,1)S(1)}, u32[]{:S(2)}, u32[]{:S(2)}) collective-permute-start(bf16[6,1,20,512]{3,1,2,0:T(2,128)(2,1)S(1)} %get-tuple-element.253), channel_id=1, source_target_pairs={{16,0},{32,16},{48,32},{17,1},{33,17},{49,33},{18,2},{34,18},{50,3... | collective-permute-start | bytes 368648 | tf_op jit(solution)/shard_map/ppermute | solution.py:37
  144.8 7.1 %collective-permute-start.1 = (bf16[6,1,20,512]{3,1,2,0:T(2,128)(2,1)S(1)}, bf16[6,1,20,512]{3,1,2,0:T(2,128)(2,1)S(1)}, u32[]{:S(2)}, u32[]{:S(2)}) collective-permute-start(bf16[6,1,20,512]{3,1,2,0:T(2,128)(2,1)S(1)} %get-tuple-element.252), channel_id=1, source_target_pairs={{0,16},{16,32},{32,48},{1,17},{17,33},{33,49},{2,18},{18,34},{34,5... | collective-permute-start | bytes 368648 | tf_op jit(solution)/shard_map/ppermute | solution.py:35
  152.0 19.7 %collective-permute-start.4 = (bf16[6,6,1,512]{3,1,2,0:T(8,128)(2,1)S(1)}, bf16[6,6,1,512]{3,1,2,0:T(8,128)(2,1)S(1)}, u32[]{:S(2)}, u32[]{:S(2)}) collective-permute-start(bf16[6,6,1,512]{3,1,2,0:T(8,128)(2,1)S(1)} %get-tuple-element.246), channel_id=1, source_target_pairs={{1,0},{2,1},{3,2},{4,3},{5,4},{6,5},{7,6},{8,7},{9,8},{10,9},{11,1... | collective-permute-start | bytes 110600 | tf_op jit(solution)/shard_map/ppermute | solution.py:37
  162.8 8.9 %collective-permute-start.3 = (bf16[6,6,1,512]{3,1,2,0:T(8,128)(2,1)S(1)}, bf16[6,6,1,512]{3,1,2,0:T(8,128)(2,1)S(1)}, u32[]{:S(2)}, u32[]{:S(2)}) collective-permute-start(bf16[6,6,1,512]{3,1,2,0:T(8,128)(2,1)S(1)} %get-tuple-element.247), channel_id=1, source_target_pairs={{0,1},{1,2},{2,3},{3,4},{4,5},{5,6},{6,7},{7,8},{8,9},{9,10},{10,1... | collective-permute-start | bytes 110600 | tf_op jit(solution)/shard_map/ppermute | solution.py:35
  191.8 18.9 %slice-start = ((s8[7077888]{0:T(1024)(128)(4,1)}), s8[2883584]{0:T(1024)(128)(4,1)S(1)}, s32[]{:S(2)}) async-start(s8[7077888]{0:T(1024)(128)(4,1)} %bitcast.259), calls=%async_computation | async-start | bytes 5767168
  201.1 5.8 %copy-start.3 = (bf16[320,512]{1,0:T(8,128)(2,1)S(1)}, bf16[320,512]{1,0:T(8,128)(2,1)}, u32[]{:S(2)}) copy-start(bf16[320,512]{1,0:T(8,128)(2,1)} %reshape.207) | copy-start | bytes 983044
  201.1 7.0 %copy-start.21 = (bf16[320,512]{1,0:T(8,128)(2,1)S(1)}, bf16[320,512]{1,0:T(8,128)(2,1)}, u32[]{:S(2)}) copy-start(bf16[320,512]{1,0:T(8,128)(2,1)} %reshape.208) | copy-start | bytes 983044
  201.1 8.3 %copy-start.23 = (bf16[320,512]{1,0:T(8,128)(2,1)S(1)}, bf16[320,512]{1,0:T(8,128)(2,1)}, u32[]{:S(2)}) copy-start(bf16[320,512]{1,0:T(8,128)(2,1)} %reshape.209) | copy-start | bytes 983044
  201.1 9.6 %slice-start.1 = ((s8[7077888]{0:T(1024)(128)(4,1)}), s8[4194304]{0:T(1024)(128)(4,1)S(1)}, s32[]{:S(2)}) async-start(s8[7077888]{0:T(1024)(128)(4,1)} %bitcast.259), calls=%async_computation.1 | async-start | bytes 8388608
  202.6 8.1 %copy-start.8 = (bf16[320,512]{1,0:T(8,128)(2,1)S(1)}, bf16[320,512]{1,0:T(8,128)(2,1)}, u32[]{:S(2)}) copy-start(bf16[320,512]{1,0:T(8,128)(2,1)} %reshape.210) | copy-start | bytes 983044
  204.2 6.8 %copy-start.19 = (bf16[320,512]{1,0:T(8,128)(2,1)S(1)}, bf16[320,512]{1,0:T(8,128)(2,1)}, u32[]{:S(2)}) copy-start(bf16[320,512]{1,0:T(8,128)(2,1)} %reshape.211) | copy-start | bytes 983044
  205.5 5.7 %copy-start.22 = (bf16[320,512]{1,0:T(8,128)(2,1)S(1)}, bf16[320,512]{1,0:T(8,128)(2,1)}, u32[]{:S(2)}) copy-start(bf16[320,512]{1,0:T(8,128)(2,1)} %reshape.212) | copy-start | bytes 983044
  206.9 4.7 %copy-start.7 = (bf16[320,512]{1,0:T(8,128)(2,1)S(1)}, bf16[320,512]{1,0:T(8,128)(2,1)}, u32[]{:S(2)}) copy-start(bf16[320,512]{1,0:T(8,128)(2,1)} %reshape.213) | copy-start | bytes 983044
  208.2 3.7 copy-start.17
  214.8 134.5 %copy-start.46 = (f32[256]{0:T(256)S(1)}, f32[256]{0:T(256)}, u32[]{:S(2)}) copy-start(f32[256]{0:T(256)} %param.19) | copy-start | bytes 3076
  214.9 134.4 %copy-start.48 = (f32[256]{0:T(256)S(1)}, f32[256]{0:T(256)}, u32[]{:S(2)}) copy-start(f32[256]{0:T(256)} %param.18) | copy-start | bytes 3076
  349.1 19.3 %copy-start.42 = (f32[256]{0:T(256)}, f32[256]{0:T(256)S(1)}, u32[]{:S(2)}) copy-start(f32[256]{0:T(256)S(1)} %mul.89) | copy-start | bytes 3076
  349.2 19.1 %copy-start.44 = (f32[256]{0:T(256)}, f32[256]{0:T(256)S(1)}, u32[]{:S(2)}) copy-start(f32[256]{0:T(256)S(1)} %sub.35) | copy-start | bytes 3076
  349.5 3.7 collective-permute-start.5
  353.2 6.7 %collective-permute-start.7 = (bf16[6,1,20,256]{3,2,1,0:T(8,128)(2,1)S(1)}, bf16[6,1,20,256]{3,2,1,0:T(8,128)(2,1)S(1)}, u32[]{:S(2)}, u32[]{:S(2)}) collective-permute-start(bf16[6,1,20,256]{3,2,1,0:T(8,128)(2,1)S(1)} %get-tuple-element.287), channel_id=1, source_target_pairs={{16,0},{32,16},{48,32},{17,1},{33,17},{49,33},{18,2},{34,18},{50,3... | collective-permute-start | bytes 184328 | tf_op jit(solution)/shard_map/ppermute | solution.py:37
  354.5 5.4 %collective-permute-start.6 = (bf16[6,1,20,256]{3,2,1,0:T(8,128)(2,1)S(1)}, bf16[6,1,20,256]{3,2,1,0:T(8,128)(2,1)S(1)}, u32[]{:S(2)}, u32[]{:S(2)}) collective-permute-start(bf16[6,1,20,256]{3,2,1,0:T(8,128)(2,1)S(1)} %get-tuple-element.286), channel_id=1, source_target_pairs={{0,16},{16,32},{32,48},{1,17},{17,33},{33,49},{2,18},{18,34},{34,5... | collective-permute-start | bytes 184328 | tf_op jit(solution)/shard_map/ppermute | solution.py:35
  360.0 12.9 %collective-permute-start.8 = (bf16[6,6,1,256]{3,2,1,0:T(2,128)(2,1)S(1)}, bf16[6,6,1,256]{3,2,1,0:T(2,128)(2,1)S(1)}, u32[]{:S(2)}, u32[]{:S(2)}) collective-permute-start(bf16[6,6,1,256]{3,2,1,0:T(2,128)(2,1)S(1)} %get-tuple-element.274), channel_id=1, source_target_pairs={{0,1},{1,2},{2,3},{3,4},{4,5},{5,6},{6,7},{7,8},{8,9},{9,10},{10,1... | collective-permute-start | bytes 55304 | tf_op jit(solution)/shard_map/ppermute | solution.py:35
  362.6 10.3 %collective-permute-start.9 = (bf16[6,6,1,256]{3,2,1,0:T(2,128)(2,1)S(1)}, bf16[6,6,1,256]{3,2,1,0:T(2,128)(2,1)S(1)}, u32[]{:S(2)}, u32[]{:S(2)}) collective-permute-start(bf16[6,6,1,256]{3,2,1,0:T(2,128)(2,1)S(1)} %get-tuple-element.275), channel_id=1, source_target_pairs={{1,0},{2,1},{3,2},{4,3},{5,4},{6,5},{7,6},{8,7},{9,8},{10,9},{11,1... | collective-permute-start | bytes 55304 | tf_op jit(solution)/shard_map/ppermute | solution.py:37
  375.9 12.6 %copy-start.24 = (bf16[4,4,20,256]{3,2,1,0:T(8,128)(2,1)S(1)}, bf16[4,4,20,256]{3,2,1,0:T(8,128)(2,1)}, u32[]{:S(2)}) copy-start(bf16[4,4,20,256]{3,2,1,0:T(8,128)(2,1)} %get-tuple-element.265) | copy-start | bytes 491524
  381.5 11.6 %copy-start.27 = (bf16[320,256]{1,0:T(8,128)(2,1)S(1)}, bf16[320,256]{1,0:T(8,128)(2,1)}, u32[]{:S(2)}) copy-start(bf16[320,256]{1,0:T(8,128)(2,1)} %reshape.234) | copy-start | bytes 491524
  389.2 7.4 %copy-start.31 = (bf16[320,256]{1,0:T(8,128)(2,1)S(1)}, bf16[320,256]{1,0:T(8,128)(2,1)}, u32[]{:S(2)}) copy-start(bf16[320,256]{1,0:T(8,128)(2,1)} %reshape.237) | copy-start | bytes 491524
  389.4 7.5 %copy-start.38 = (bf16[320,256]{1,0:T(8,128)(2,1)S(1)}, bf16[320,256]{1,0:T(8,128)(2,1)}, u32[]{:S(2)}) copy-start(bf16[320,256]{1,0:T(8,128)(2,1)} %reshape.238) | copy-start | bytes 491524
  389.4 4.9 %copy-start = (bf16[3,3,3,256,256]{4,3,2,1,0:T(8,128)(2,1)S(1)}, bf16[3,3,3,256,256]{4,3,2,1,0:T(8,128)(2,1)}, u32[]{:S(2)}) copy-start(bf16[3,3,3,256,256]{4,3,2,1,0:T(8,128)(2,1)} %param.20) | copy-start | bytes 10616836
  390.7 6.4 %copy-start.37 = (bf16[320,256]{1,0:T(8,128)(2,1)S(1)}, bf16[320,256]{1,0:T(8,128)(2,1)}, u32[]{:S(2)}) copy-start(bf16[320,256]{1,0:T(8,128)(2,1)} %reshape.239) | copy-start | bytes 491524
  391.9 5.4 %copy-start.30 = (bf16[320,256]{1,0:T(8,128)(2,1)S(1)}, bf16[320,256]{1,0:T(8,128)(2,1)}, u32[]{:S(2)}) copy-start(bf16[320,256]{1,0:T(8,128)(2,1)} %reshape.240) | copy-start | bytes 491524
  393.2 4.4 %copy-start.36 = (bf16[320,256]{1,0:T(8,128)(2,1)S(1)}, bf16[320,256]{1,0:T(8,128)(2,1)}, u32[]{:S(2)}) copy-start(bf16[320,256]{1,0:T(8,128)(2,1)} %reshape.241) | copy-start | bytes 491524
  (31 other events, 52.4 us)
where the time goes:
time: 404 us; the launch traced here: 402 us
  blocking collectives  267 us (66%)
  local copies, waits for them, and re-layouts  58.8 us (15%)
  starting transfers between devices  34.7 us (9%)
  matrix products  28.2 us (7%)
  other arithmetic  7.31 us (2%)
    psum x2, blocking collectives, activate(): totals = lax.psum(partial_value, ('row', 'col'))  252 us
    reshape x52, local copies, waits for them, and re-layouts, conv_taps(): tapped.reshape(-1, padded.shape[-1])  39.3 us
    dot_general x54, matrix products, conv_taps(): jnp.dot(tapped.reshape(-1, padded.shape[-1]), weight[tap_t, tap_r, tap_c]...  28.2 us
    ppermute x4, starting transfers between devices, extended(): lax.ppermute(head, axis, [((i + 1) % count, i) for i in range(ends)])  18.9 us
    slice x32, local copies, waits for them, and re-layouts, conv_taps(): padded[tap_t:tap_t + frames, tap_r:tap_r + height, tap_c:tap_c + across]  16.1 us
    all_gather x2, blocking collectives, entering(): pieces = lax.all_gather(value, axis)  15.6 us
    ppermute x4, starting transfers between devices, extended(): lax.ppermute(tail, axis, [(i, (i + 1) % count) for i in range(ends)])  12.5 us
  transfers between devices with their start and end apart: 10, of which 3 were waited for; matrix products, arithmetic and copies ran while one was open for 4% of the time, Pallas kernels for 0%

commit v1 on v0

v1 whole, which is shorter than its diff:
```python
import functools

import jax
import jax.numpy as jnp
import numpy as np
from jax import lax
from jax.experimental import pallas as pl
from jax.experimental.pallas import tpu as pltpu
from jax.sharding import PartitionSpec as P

GROUPS = 32
LANES = 128
EVERY = ("tm", "row", "col")
HIGHEST = lax.Precision.HIGHEST
F32 = jnp.float32
BF16 = jnp.bfloat16
ROWS, SLOTS = 4, 16
CELLS = ROWS * SLOTS
VMEM_LIMIT = 62 * 1024 * 1024


def group_of(channel, channels):
    return lax.shift_right_logical(channel, int(np.log2(channels // GROUPS)))


def packed_sums(sums, squares):
    channels = sums.shape[-1]
    shape = (channels, LANES)
    member = group_of(lax.broadcasted_iota(jnp.int32, shape, 0), channels) == lax.broadcasted_iota(jnp.int32, shape, 1)
    both = jnp.concatenate([sums, squares, jnp.zeros((6, channels), F32)], axis=0)
    grouped = jnp.dot(both, member.astype(F32), precision=HIGHEST, preferred_element_type=F32)
    return grouped[0:1] + pltpu.roll(grouped, GROUPS, 1)[1:2]


def affine(parts, unit, gain, bias, span):
    channels = gain.shape[-1]
    spans = lax.axis_size("tm")
    each = parts.shape[0] // spans
    now = jnp.zeros((1, LANES), F32)
    before = jnp.zeros((1, LANES), F32)
    for s in range(spans):
        part = jnp.sum(parts[s * each : (s + 1) * each], axis=0, keepdims=True)
        now = now + jnp.where(s <= span, part, 0.0)
        before = before + jnp.where(s < span, part, 0.0)
    stacked = jnp.concatenate([now, before, jnp.zeros((6, LANES), F32)], axis=0)
    stacked = jnp.concatenate([stacked, pltpu.roll(stacked, LANES - GROUPS, 1)], axis=0)
    shape = (LANES, channels)
    member = group_of(lax.broadcasted_iota(jnp.int32, shape, 1), channels) == lax.broadcasted_iota(jnp.int32, shape, 0)
    spread = jnp.dot(stacked, member.astype(F32), precision=HIGHEST, preferred_element_type=F32)
    result = []
    for k in range(2):
        count = jnp.maximum(span + 1 - k, 1).astype(F32) * unit
        mean = spread[k : k + 1] / count
        var = spread[8 + k : 9 + k] / count - mean * mean
        scale = lax.rsqrt(var + 1e-06) * gain
        result.append((scale, bias - mean * scale))
    return result


def silu(x):
    return x / (1.0 + jnp.exp(-x))


def low_sums_kernel(x_ref, sums_ref, own_ref, to_right_ref, to_left_ref):
    frames, across, height, channels = x_ref.shape
    x = x_ref[...].astype(F32).reshape(frames * across * height, channels)
    row = packed_sums(jnp.sum(x, axis=0, keepdims=True), jnp.sum(x * x, axis=0, keepdims=True))
    sums_ref[...] = jnp.broadcast_to(row, sums_ref.shape)
    block = height * frames * SLOTS
    shape = (block + 32, x.shape[0])
    to = lax.broadcasted_iota(jnp.int32, shape, 0)
    edge = to - block
    k = jnp.where(to < block, to // SLOTS, edge % 16)
    column = jnp.where(to < block, to % SLOTS - 1, jnp.where(edge < 16, across - 1, 0))
    source = ((k % frames) * across + column) * height + k // frames
    hit = (lax.broadcasted_iota(jnp.int32, shape, 1) == source) & (column >= 0) & (column < across) & (k < height * frames)
    moved = jnp.dot(hit.astype(BF16), x.astype(BF16), preferred_element_type=F32).astype(BF16)
    own_ref[...] = moved[:block]
    to_right_ref[...] = moved[block : block + 16]
    to_left_ref[...] = moved[block + 16 :]


def pack_kernel(own_ref, left_ref, right_ref, out_ref):
    rows = own_ref.shape[0]
    shape = (rows, 32)
    to = lax.broadcasted_iota(jnp.int32, shape, 0)
    source = lax.broadcasted_iota(jnp.int32, shape, 1)
    slot, k = to % SLOTS, to // SLOTS
    hit = ((slot == 0) & (source == k)) | ((slot == 11) & (source == 16 + k))
    both = jnp.concatenate([left_ref[...], right_ref[...]], axis=0)
    moved = jnp.dot(hit.astype(BF16), both, preferred_element_type=F32)
    out_ref[...] = (own_ref[...].astype(F32) + moved).astype(BF16)


def position():
    tm, row, col = (lax.axis_index(a) for a in EVERY)
    return tm, row, col


def up_kernel(spans_used, unit, parts_ref, gain_ref, bias_ref, b_ref, *refs):
    n_prev, n_now = spans_used
    own = n_now > 0
    if own:
        now_ref, prev_ref, above_ref, below_ref, w_ref, hid_ref, sums_ref, x_ref, wbuf, sems = refs
    else:
        prev_ref, above_ref, below_ref, w_ref, _, hid_ref, x_ref, wbuf, sems = refs
    copies = [pltpu.make_async_copy(w_ref.at[:, k // 3, k % 3], wbuf.at[k], sems.at[k]) for k in range(9)]
    for copy in copies:
        copy.start()
    tm, row, col = position()
    last_row, last_col = lax.axis_size("row") - 1, lax.axis_size("col") - 1
    (scale, offset), (scale_prev, offset_prev) = affine(parts_ref[...], unit, gain_ref[...], bias_ref[...], tm)
    depth = scale.shape[-1]
    line = prev_ref.shape[0] // 2
    span = line // SLOTS
    slot = lax.broadcasted_iota(jnp.int32, (line, depth), 0) % SLOTS
    inside = (slot >= jnp.where(col > 0, 0, 1)) & (slot <= jnp.where(col < last_col, 11, 10))

    def place(piece, first, count, at, r, a, b, valid):
        v = silu(piece[first * SLOTS : (first + count) * SLOTS].astype(F32) * a + b)
        v = jnp.where(inside[: count * SLOTS] & valid, v, 0.0).astype(BF16)
        for f in range(count):
            x_ref[at + f, r * SLOTS : (r + 1) * SLOTS] = v[f * SLOTS : (f + 1) * SLOTS]

    past = tm > 0
    up, down = row > 0, row < last_row
    first = span - n_prev
    for r in range(2):
        place(prev_ref.at[r * line : (r + 1) * line], first, n_prev, 0, r + 1, scale_prev, offset_prev, past)
    place(above_ref.at[line:], first, n_prev, 0, 0, scale_prev, offset_prev, past & up)
    place(below_ref.at[line:], first, n_prev, 0, 3, scale_prev, offset_prev, past & down)
    if own:
        for r in range(2):
            place(now_ref.at[r * line : (r + 1) * line], 0, n_now, n_prev, r + 1, scale, offset, tm >= 0)
        place(above_ref.at[:line], 0, n_now, n_prev, 0, scale, offset, up)
        place(below_ref.at[:line], 0, n_now, n_prev, 3, scale, offset, down)

    frames = n_prev + n_now - 2
    size = frames * CELLS
    width = b_ref.shape[-1]
    x = jnp.concatenate([x_ref[a : a + frames].reshape(size, depth) for a in range(3)], axis=1)
    acc = [[None, None], [None, None]]

    def add(p, q, value):
        acc[p][q] = value if acc[p][q] is None else acc[p][q] + value

    for b in range(3):
        z = []
        for e in range(3):
            copies[3 * b + e].wait()
            z.append(jnp.dot(x, wbuf[3 * b + e].reshape(3 * depth, width), preferred_element_type=F32))
        even = pltpu.roll(z[0], 1, 0) + (z[1] + z[2])
        odd = (z[0] + z[1]) + pltpu.roll(z[2], size - 1, 0)
        for q, u in ((0, even), (1, odd)):
            add(0, q, pltpu.roll(u, SLOTS, 0) if b == 0 else u)
            add(1, q, pltpu.roll(u, size - SLOTS, 0) if b == 2 else u)
    total = jnp.zeros((1, width), F32)
    square = jnp.zeros((1, width), F32)
    if own:
        at = lax.broadcasted_iota(jnp.int32, (frames, 2, SLOTS, width), 2)
        mine = (at >= 1) & (at <= 10)
    for p in range(2):
        for q in range(2):
            hidden = (acc[p][q] + b_ref[...]).astype(BF16)
            for f in range(frames):
                hid_ref[f, (2 * p + q) * CELLS : (2 * p + q + 1) * CELLS] = hidden[f * CELLS : (f + 1) * CELLS]
            if own:
                seen = hidden.astype(F32).reshape(frames, ROWS, SLOTS, width)[:, 1:3]
                seen = jnp.where(mine, seen, 0.0).reshape(-1, width)
                total = total + jnp.sum(seen, axis=0, keepdims=True)
                square = square + jnp.sum(seen * seen, axis=0, keepdims=True)
    if own:
        sums_ref[...] = jnp.broadcast_to(packed_sums(total, square), sums_ref.shape)


def gather_matrix():
    m = np.zeros((3, 3, 20, 4, 2, 2, ROWS, SLOTS), np.float32)
    for b in range(3):
        for e in range(3):
            for y in range(4):
                for x in range(20):
                    v, u = y + b - 1, x + e - 1
                    m[b, e, x, y, v % 2, u % 2, v // 2 + 1, u // 2 + 1] = 1.0
    return m.reshape(720, 4 * CELLS)


def res_kernel(unit, parts_ref, gain_ref, bias_ref, b_ref, hid_ref, hid_prev_ref, pick_ref, w_ref, out_ref, g_ref, wbuf, sems):
    copies = [pltpu.make_async_copy(w_ref.at[k], wbuf.at[k], sems.at[k]) for k in range(3)]
    for copy in copies:
        copy.start()
    tm, row, col = position()
    last_row, last_col = lax.axis_size("row") - 1, lax.axis_size("col") - 1
    (scale, offset), (scale_prev, offset_prev) = affine(parts_ref[...], unit, gain_ref[...], bias_ref[...], tm)
    width = scale.shape[-1]
    cell = lax.broadcasted_iota(jnp.int32, (4 * CELLS, width), 0)
    parity, r, slot = cell // CELLS, (cell // SLOTS) % ROWS, cell % SLOTS
    y, x = 2 * (r - 1) + parity // 2, 2 * (slot - 1) + parity % 2
    inside = ((y >= 0) | (row > 0)) & ((y < 4) | (row < last_row)) & ((x >= 0) | (col > 0)) & ((x < 20) | (col < last_col))
    n_prev, n_now = hid_prev_ref.shape[0], hid_ref.shape[0]
    area = 80
    for f in range(n_prev + n_now):
        if f < n_prev:
            v = silu(hid_prev_ref[f].astype(F32) * scale_prev + offset_prev)
            v = jnp.where(inside & (tm > 0), v, 0.0)
        else:
            v = silu(hid_ref[f - n_prev].astype(F32) * scale + offset)
            v = jnp.where(inside, v, 0.0)
        picked = jnp.dot(pick_ref[...], v.astype(BF16), preferred_element_type=F32).astype(BF16)
        for k in range(9):
            g_ref[f * area : (f + 1) * area, k * width : (k + 1) * width] = picked[k * area : (k + 1) * area]
    total = None
    for a in range(3):
        copies[a].wait()
        part = jnp.dot(
            g_ref[a * area : (a + n_now) * area], wbuf[a].reshape(9 * width, width), preferred_element_type=F32
        )
        total = part if total is None else total + part
    for f in range(n_now):
        hidden = jnp.dot(pick_ref[4 * area : 5 * area], hid_ref[f], preferred_element_type=F32)
        decoded = total[f * area : (f + 1) * area] + b_ref[...] + hidden
        out_ref[f] = decoded.reshape(out_ref.shape[1:]).astype(BF16)


def shifted(value, axes, sizes, steps):
    place = np.arange(int(np.prod(sizes))).reshape(sizes)
    route = []
    for at in np.ndindex(*sizes):
        to = tuple(i + s for i, s in zip(at, steps))
        if all(0 <= t < n for t, n in zip(to, sizes)):
            route.append((int(place[at]), int(place[to])))
    return lax.ppermute(value, axes, route)


def params(**kw):
    return pltpu.CompilerParams(vmem_limit_bytes=VMEM_LIMIT, **kw)


VM = pl.BlockSpec(memory_space=pltpu.VMEM)
HBM = pl.BlockSpec(memory_space=pltpu.HBM)


def local(features, gain_low, bias_low, w_up, b_up, gain_high, bias_high, w_res, b_res):
    n_tm, n_row, n_col = (lax.axis_size(a) for a in EVERY)
    devices = n_tm * n_row * n_col
    frames, height, across, depth = features.shape
    width = w_up.shape[-1]
    low_unit = float(n_row * n_col * frames * height * across * (depth // GROUPS))
    high_unit = float(n_row * n_col * frames * 4 * height * across * (width // GROUPS))

    block = height * frames * SLOTS
    line = frames * SLOTS
    sums, own, to_right, to_left = pl.pallas_call(
        low_sums_kernel,
        out_shape=(
            jax.ShapeDtypeStruct((devices, LANES), F32),
            jax.ShapeDtypeStruct((block, depth), BF16),
            jax.ShapeDtypeStruct((16, depth), BF16),
            jax.ShapeDtypeStruct((16, depth), BF16),
        ),
        in_specs=[VM],
        out_specs=(VM,) * 4,
        compiler_params=params(),
        name="low_sums",
    )(features.transpose(0, 2, 1, 3))
    left = shifted(to_right, "col", (n_col,), (1,))
    right = shifted(to_left, "col", (n_col,), (-1,))
    low_parts = lax.all_to_all(sums, EVERY, 0, 0)
    now = pl.pallas_call(
        pack_kernel,
        out_shape=jax.ShapeDtypeStruct((block, depth), BF16),
        in_specs=[VM] * 3,
        out_specs=VM,
        compiler_params=params(),
        name="pack",
    )(own, left, right)
    prev = shifted(now, "tm", (n_tm,), (1,))
    above = shifted(jnp.concatenate([now[line:], prev[line:]], axis=0), "row", (n_row,), (1,))
    below = shifted(jnp.concatenate([now[:line], prev[:line]], axis=0), "row", (n_row,), (-1,))

    gl, bl, bu = gain_low.reshape(1, -1), bias_low.reshape(1, -1), b_up.reshape(1, -1)
    gh, bh, br = gain_high.reshape(1, -1), bias_high.reshape(1, -1), b_res.reshape(1, -1)

    def scratch(count):
        return [
            pltpu.VMEM((count, CELLS, depth), BF16),
            pltpu.VMEM((9, 3, depth, width), BF16),
            pltpu.SemaphoreType.DMA((9,)),
        ]

    hidden, high_sums = pl.pallas_call(
        functools.partial(up_kernel, (2, frames), low_unit),
        out_shape=(
            jax.ShapeDtypeStruct((frames, 4 * CELLS, width), BF16),
            jax.ShapeDtypeStruct((devices, LANES), F32),
        ),
        in_specs=[VM] * 8 + [HBM],
        out_specs=(VM, VM),
        scratch_shapes=scratch(2 + frames),
        compiler_params=params(),
        name="up_now",
    )(low_parts, gl, bl, bu, now, prev, above, below, w_up)
    high_parts = lax.all_to_all(high_sums, EVERY, 0, 0)
    hidden_prev = pl.pallas_call(
        functools.partial(up_kernel, (frames, 0), low_unit),
        out_shape=jax.ShapeDtypeStruct((2, 4 * CELLS, width), BF16),
        in_specs=[VM] * 7 + [HBM, HBM],
        out_specs=VM,
        scratch_shapes=scratch(frames),
        compiler_params=params(),
        cost_estimate=pl.CostEstimate(flops=27 * 2 * 128 * 512 * 256, bytes_accessed=27 * 512 * 256 * 2, transcendentals=0),
        name="up_prev",
    )(low_parts, gl, bl, bu, prev, above, below, w_up, hidden)

    area = 4 * height * across
    decoded = pl.pallas_call(
        functools.partial(res_kernel, high_unit),
        out_shape=jax.ShapeDtypeStruct((frames, 2 * across, 2 * height, width), BF16),
        in_specs=[VM] * 7 + [HBM],
        out_specs=VM,
        scratch_shapes=[
            pltpu.VMEM(((2 + frames) * area, 9 * width), BF16),
            pltpu.VMEM((3, 3, 3, width, width), BF16),
            pltpu.SemaphoreType.DMA((3,)),
        ],
        compiler_params=params(),
        name="res",
    )(high_parts, gh, bh, br, hidden, hidden_prev, jnp.asarray(gather_matrix(), BF16), w_res)
    return decoded.transpose(0, 2, 1, 3)


def solution(mesh):
    in_specs = (P("tm", "row", "col", None), P(), P(), P(), P(), P(), P(), P(), P())
    out_specs = P("tm", "row", "col", None)
    return jax.shard_map(local, mesh=mesh, in_specs=in_specs, out_specs=out_specs, check_vma=False)
```

time: 404 us -> 87.1 us (0.22)
  blocking collectives: 267 us -> 0 us
  local copies, waits for them, and re-layouts: 58.8 us -> 2.8 us
  matrix products: 28.2 us -> 0 us
  Pallas kernels: 0 us -> 24.2 us
  starting transfers between devices: 34.7 us -> 46.1 us
  waiting for transfers between devices: 3.57 us -> 13.3 us
  other arithmetic: 7.31 us -> 0.02 us
    psum x2 -> x0, blocking collectives: 252 us -> none  [activate(): totals = lax.psum(partial_value, ('row', 'col'))]
    reshape x54 -> x0, local copies, waits for them, and re-layouts: 39.4 us -> none  [the longest x52 39.3 us: conv_taps(): tapped.reshape(-1, padded.shape[-1])]
    all_to_all x0 -> x2, starting transfers between devices: none -> 31.8 us  [the longest x1 16.2 us: local(): high_parts = lax.all_to_all(high_sums, EVERY, 0, 0)]
    dot_general x54 -> x0, matrix products: 28.2 us -> none  [conv_taps(): jnp.dot(tapped.reshape(-1, padded.shape[-1]), weight[tap_t, tap_r, tap_c]...]
    pallas_call x0 -> x5, Pallas kernels: none -> 24.2 us  [the longest x1 8.49 us: local(): pl.pallas_call(functools.partial(up_kernel, (2, frames), low_unit), out_s...]
    ppermute x10 -> x5, starting transfers between devices: 34.7 us -> 14.3 us  [shifted(): return lax.ppermute(value, axes, route)]
    all_gather x2 -> x0, blocking collectives: 15.6 us -> none  [entering(): pieces = lax.all_gather(value, axis)]
    slice x35 -> x2, local copies, waits for them, and re-layouts: 16.1 us -> 0.9 us  [the longest x1 0.9 us: local(): now[:line]]
  transfers between devices with their start and end apart: 10 -> 7, of which waited for: 3 -> 4; matrix products, arithmetic and copies ran while one was open for 4% -> 1% of each run, Pallas kernels for 0% -> 9%
where the time goes in v1:
time: 87.1 us; the launch traced here: 86.7 us
  starting transfers between devices  46.1 us (53%)
  Pallas kernels  24.2 us (28%)
  waiting for transfers between devices  13.3 us (15%)
  local copies, waits for them, and re-layouts  2.8 us (3%)
    all_to_all x1, starting transfers between devices, local(): high_parts = lax.all_to_all(high_sums, EVERY, 0, 0)  16.2 us
    all_to_all x1, starting transfers between devices, local(): low_parts = lax.all_to_all(sums, EVERY, 0, 0)  15.6 us
    ppermute x5, starting transfers between devices, shifted(): return lax.ppermute(value, axes, route)  14.3 us
    pallas_call x1, Pallas kernels, local(): pl.pallas_call(functools.partial(up_kernel, (2, frames), low_unit), out_s...  8.49 us
    ppermute x5, waiting for transfers between devices, shifted(): return lax.ppermute(value, axes, route)  6.67 us
    all_to_all x1, waiting for transfers between devices, local(): high_parts = lax.all_to_all(high_sums, EVERY, 0, 0)  6.65 us
    pallas_call x1, Pallas kernels, local(): pl.pallas_call(functools.partial(up_kernel, (frames, 0), low_unit), out_s...  6.23 us
    pallas_call x1, Pallas kernels, local(): pl.pallas_call(functools.partial(res_kernel, high_unit), out_shape=jax.Sh...  5.79 us
  transfers between devices with their start and end apart: 7, of which 4 were waited for; matrix products, arithmetic and copies ran while one was open for 1% of the time, Pallas kernels for 9%

profile of v1, /device:TPU:1, one launch (start us, length us, event | category | flops | bytes accessed | tf_op | source)
XLA Modules:
  0.0 86.7 jit_solution(13608896937981361953)
XLA Ops:
  0.0 2.0 %low_sums.1 = (f32[256,128]{1,0:T(8,128)}, bf16[128,512]{1,0:T(8,128)(2,1)}, bf16[16,512]{1,0:T(8,128)(2,1)}, bf16[16,512]{1,0:T(8,128)(2,1)}) custom-call(bf16[4,10,2,512]{3,2,1,0:T(2,128)(2,1)} %bitcast.21), custom_call_target="tpu_custom_call" | custom-call | tf_op jit(solution)/shard_map/low_sums/pallas_call | solution.py:252
  2.0 4.9 %collective-permute-start = (bf16[16,512]{1,0:T(8,128)(2,1)}, bf16[16,512]{1,0:T(8,128)(2,1)S(1)}, u32[]{:S(2)}, u32[]{:S(2)}) collective-permute-start(bf16[16,512]{1,0:T(8,128)(2,1)} %get-tuple-element.13), channel_id=1, source_target_pairs={{0,1},{1,2},{2,3},{3,4},{4,5},{5,6},{6,7},{7,8},{8,9},{9,10},{10,1... | collective-permute-start | bytes 49160 | tf_op jit(solution)/shard_map/ppermute | solution.py:231
  6.9 1.9 %collective-permute-start.1 = (bf16[16,512]{1,0:T(8,128)(2,1)}, bf16[16,512]{1,0:T(8,128)(2,1)S(1)}, u32[]{:S(2)}, u32[]{:S(2)}) collective-permute-start(bf16[16,512]{1,0:T(8,128)(2,1)} %get-tuple-element.14), channel_id=1, source_target_pairs={{1,0},{2,1},{3,2},{4,3},{5,4},{6,5},{7,6},{8,7},{9,8},{10,9},{11,1... | collective-permute-start | bytes 49160 | tf_op jit(solution)/shard_map/ppermute | solution.py:231
  8.8 15.6 %all-to-all-start = ((f32[256,1,128]{2,1,0:T(1,128)}), f32[256,1,128]{2,1,0:T(1,128)S(1)}, u32[]{:S(2)}, u32[]{:S(2)}) async-start(f32[256,1,128]{2,1,0:T(1,128)} %bitcast.19), calls=%async_computation | async-start | bytes 262144 | tf_op jit(solution)/shard_map/all_to_all | solution.py:267
  24.4 0.0 collective-permute-done.left_ref
  24.4 0.0 copy-start.5
  24.4 0.0 collective-permute-done.1.right_ref
  24.5 0.0 copy-start.6
  24.5 0.6 copy-done.5
  25.0 0.0 copy-done.6
  25.1 1.7 %pack.1.refs_0_ = bf16[128,512]{1,0:T(8,128)(2,1)} custom-call(bf16[128,512]{1,0:T(8,128)(2,1)} %get-tuple-element.12.own_ref, bf16[16,512]{1,0:T(8,128)(2,1)} %copy-done.5, bf16[16,512]{1,0:T(8,128)(2,1)} %copy-done.6), custom_call_target="tpu_custom_call" | custom-call | tf_op jit(solution)/shard_map/pack/pallas_call | solution.py:268
  26.8 3.3 %collective-permute-start.2 = (bf16[128,512]{1,0:T(8,128)(2,1)}, bf16[128,512]{1,0:T(8,128)(2,1)S(1)}, u32[]{:S(2)}, u32[]{:S(2)}) collective-permute-start(bf16[128,512]{1,0:T(8,128)(2,1)} %pack.1.refs_0_), channel_id=1, source_target_pairs={{0,64},{64,128},{128,192},{1,65},{65,129},{129,193},{2,66},{66,130... | collective-permute-start | bytes 393224 | tf_op jit(solution)/shard_map/ppermute | solution.py:231
  30.1 0.9 %fusion = (bf16[64,512]{1,0:T(8,128)(2,1)S(1)}, bf16[64,512]{1,0:T(8,128)(2,1)S(1)}) fusion(bf16[128,512]{1,0:T(8,128)(2,1)} %pack.1.refs_0_), kind=kLoop, calls=%fused_computation.2 | loop fusion | bytes 262144 | tf_op jit(solution)/shard_map/slice | solution.py:278
  31.0 2.3 %collective-permute-done.2.refs_1_.refs_0_ = bf16[128,512]{1,0:T(8,128)(2,1)S(1)} collective-permute-done((bf16[128,512]{1,0:T(8,128)(2,1)}, bf16[128,512]{1,0:T(8,128)(2,1)S(1)}, u32[]{:S(2)}, u32[]{:S(2)}) %collective-permute-start.2) | collective-permute-done | bytes 131104 | tf_op jit(solution)/shard_map/ppermute | solution.py:231
  33.3 0.0 copy-start.1
  33.3 2.9 %collective-permute-start.3 = (bf16[128,512]{1,0:T(8,128)(2,1)S(1)}, bf16[128,512]{1,0:T(8,128)(2,1)S(1)}, u32[]{:S(2)}, u32[]{:S(2)}) collective-permute-start(bf16[128,512]{1,0:T(8,128)(2,1)S(1)} %pad_maximum_fusion), channel_id=1, source_target_pairs={{0,16},{16,32},{32,48},{1,17},{17,33},{33,49},{2,18},{18,34},{34,5... | collective-permute-start | bytes 393224 | tf_op jit(solution)/shard_map/ppermute | solution.py:231
  36.2 1.3 %collective-permute-start.4 = (bf16[128,512]{1,0:T(8,128)(2,1)S(1)}, bf16[128,512]{1,0:T(8,128)(2,1)S(1)}, u32[]{:S(2)}, u32[]{:S(2)}) collective-permute-start(bf16[128,512]{1,0:T(8,128)(2,1)S(1)} %pad_maximum_fusion.1), channel_id=1, source_target_pairs={{16,0},{32,16},{48,32},{17,1},{33,17},{49,33},{18,2},{34,18},{50,3... | collective-permute-start | bytes 393224 | tf_op jit(solution)/shard_map/ppermute | solution.py:231
  37.5 0.0 all-to-all-done
  37.6 0.0 copy-start
  37.6 0.6 collective-permute-done.3.refs_2_.refs_1_
  38.2 0.0 copy-start.2
  38.2 3.8 %collective-permute-done.4.refs_3_.refs_2_ = bf16[128,512]{1,0:T(8,128)(2,1)S(1)} collective-permute-done((bf16[128,512]{1,0:T(8,128)(2,1)S(1)}, bf16[128,512]{1,0:T(8,128)(2,1)S(1)}, u32[]{:S(2)}, u32[]{:S(2)}) %collective-permute-start.4) | collective-permute-done | bytes 131104 | tf_op jit(solution)/shard_map/ppermute | solution.py:231
  42.0 0.0 copy-done.1
  42.0 0.0 copy-done
  42.0 0.0 copy-done.2
  42.0 0.6 copy-done.3
  42.6 8.5 %up_now.1 = (bf16[4,256,256]{2,1,0:T(8,128)(2,1)}, f32[256,128]{1,0:T(8,128)}) custom-call(f32[256,128]{1,0:T(8,128)} %bitcast.16, f32[1,512]{1,0:T(1,128)} %bitcast.22, f32[1,512]{1,0:T(1,128)} %bitcast.24, f32[1,256]{1,0:T(1,128)} %bitcast.26, bf16[128,512]{1,0:T(8,128)(2,1)} %pack.1.refs_0_, bf16[128,512]{1,0:T(8,128)(2,1)} %copy-done.1, ...), custom_call_target="tpu_custom_call" | custom-call | tf_op jit(solution)/shard_map/up_now/pallas_call | solution.py:290
  51.1 16.2 %all-to-all-start.1 = ((f32[256,1,128]{2,1,0:T(1,128)}), f32[256,1,128]{2,1,0:T(1,128)S(1)}, u32[]{:S(2)}, u32[]{:S(2)}) async-start(f32[256,1,128]{2,1,0:T(1,128)} %bitcast.20), calls=%async_computation.1 | async-start | bytes 262144 | tf_op jit(solution)/shard_map/all_to_all | solution.py:302
  67.3 6.2 %up_prev.1.hid_prev_ref = bf16[2,256,256]{2,1,0:T(8,128)(2,1)} custom-call(f32[256,128]{1,0:T(8,128)} %bitcast.17, f32[1,512]{1,0:T(1,128)} %bitcast.23, f32[1,512]{1,0:T(1,128)} %bitcast.25, f32[1,256]{1,0:T(1,128)} %bitcast.27, bf16[128,512]{1,0:T(8,128)(2,1)} %copy-done.1, bf16[128,512]{1,0:T(8,128)(2,1)} %copy-done.2, bf16[128,512]{1,0:T(8,128)(2,1)} %copy-done.3, ...), custom_call_target="tpu_custom_call" | custom-call | flops 905969664 | bytes 7077888 | tf_op jit(solution)/shard_map/up_prev/pallas_call | solution.py:303
  73.6 6.7 %all-to-all-done.1 = f32[256,1,128]{2,1,0:T(1,128)S(1)} async-done(((f32[256,1,128]{2,1,0:T(1,128)}), f32[256,1,128]{2,1,0:T(1,128)S(1)}, u32[]{:S(2)}, u32[]{:S(2)}) %all-to-all-start.1) | async-done | bytes 131104 | tf_op jit(solution)/shard_map/all_to_all | solution.py:302
  80.2 0.6 copy-done.4
  80.9 5.8 %res.1 = bf16[4,20,4,256]{3,2,1,0:T(4,128)(2,1)} custom-call(f32[256,128]{1,0:T(8,128)} %bitcast.18, f32[1,256]{1,0:T(1,128)} %bitcast.28, f32[1,256]{1,0:T(1,128)} %bitcast.29, f32[1,256]{1,0:T(1,128)} %bitcast.30, bf16[4,256,256]{2,1,0:T(8,128)(2,1)} %get-tuple-element.16.refs_4_.hid_ref, bf16[2,256,256]{2,1,0:T(8,128)(2,1)} %up_prev.1.hid_prev_ref, ...), custom_call_target="tpu_custom_call" | custom-call | tf_op jit(solution)/shard_map/res/pallas_call | solution.py:315
  (5 shorter events, 0.0 us)
Async XLA Ops:
  2.0 22.5 %collective-permute-start = (bf16[16,512]{1,0:T(8,128)(2,1)}, bf16[16,512]{1,0:T(8,128)(2,1)S(1)}, u32[]{:S(2)}, u32[]{:S(2)}) collective-permute-start(bf16[16,512]{1,0:T(8,128)(2,1)} %get-tuple-element.13), channel_id=1, source_target_pairs={{0,1},{1,2},{2,3},{3,4},{4,5},{5,6},{6,7},{7,8},{8,9},{9,10},{10,1... | collective-permute-start | bytes 49160 | tf_op jit(solution)/shard_map/ppermute | solution.py:231
  6.9 17.5 %collective-permute-start.1 = (bf16[16,512]{1,0:T(8,128)(2,1)}, bf16[16,512]{1,0:T(8,128)(2,1)S(1)}, u32[]{:S(2)}, u32[]{:S(2)}) collective-permute-start(bf16[16,512]{1,0:T(8,128)(2,1)} %get-tuple-element.14), channel_id=1, source_target_pairs={{1,0},{2,1},{3,2},{4,3},{5,4},{6,5},{7,6},{8,7},{9,8},{10,9},{11,1... | collective-permute-start | bytes 49160 | tf_op jit(solution)/shard_map/ppermute | solution.py:231
  8.8 28.7 %all-to-all-start = ((f32[256,1,128]{2,1,0:T(1,128)}), f32[256,1,128]{2,1,0:T(1,128)S(1)}, u32[]{:S(2)}, u32[]{:S(2)}) async-start(f32[256,1,128]{2,1,0:T(1,128)} %bitcast.19), calls=%async_computation | async-start | bytes 262144 | tf_op jit(solution)/shard_map/all_to_all | solution.py:267
  24.4 0.6 copy-start.5
  24.5 0.6 copy-start.6
  26.8 6.5 %collective-permute-start.2 = (bf16[128,512]{1,0:T(8,128)(2,1)}, bf16[128,512]{1,0:T(8,128)(2,1)S(1)}, u32[]{:S(2)}, u32[]{:S(2)}) collective-permute-start(bf16[128,512]{1,0:T(8,128)(2,1)} %pack.1.refs_0_), channel_id=1, source_target_pairs={{0,64},{64,128},{128,192},{1,65},{65,129},{129,193},{2,66},{66,130... | collective-permute-start | bytes 393224 | tf_op jit(solution)/shard_map/ppermute | solution.py:231
  33.3 8.7 %copy-start.1 = (bf16[128,512]{1,0:T(8,128)(2,1)}, bf16[128,512]{1,0:T(8,128)(2,1)S(1)}, u32[]{:S(2)}) copy-start(bf16[128,512]{1,0:T(8,128)(2,1)S(1)} %collective-permute-done.2.refs_1_.refs_0_) | copy-start | bytes 393220
  33.3 4.9 %collective-permute-start.3 = (bf16[128,512]{1,0:T(8,128)(2,1)S(1)}, bf16[128,512]{1,0:T(8,128)(2,1)S(1)}, u32[]{:S(2)}, u32[]{:S(2)}) collective-permute-start(bf16[128,512]{1,0:T(8,128)(2,1)S(1)} %pad_maximum_fusion), channel_id=1, source_target_pairs={{0,16},{16,32},{32,48},{1,17},{17,33},{33,49},{2,18},{18,34},{34,5... | collective-permute-start | bytes 393224 | tf_op jit(solution)/shard_map/ppermute | solution.py:231
  36.2 5.7 %collective-permute-start.4 = (bf16[128,512]{1,0:T(8,128)(2,1)S(1)}, bf16[128,512]{1,0:T(8,128)(2,1)S(1)}, u32[]{:S(2)}, u32[]{:S(2)}) collective-permute-start(bf16[128,512]{1,0:T(8,128)(2,1)S(1)} %pad_maximum_fusion.1), channel_id=1, source_target_pairs={{16,0},{32,16},{48,32},{17,1},{33,17},{49,33},{18,2},{34,18},{50,3... | collective-permute-start | bytes 393224 | tf_op jit(solution)/shard_map/ppermute | solution.py:231
  37.6 4.4 %copy-start = (f32[256,1,128]{2,1,0:T(1,128)}, f32[256,1,128]{2,1,0:T(1,128)S(1)}, u32[]{:S(2)}) copy-start(f32[256,1,128]{2,1,0:T(1,128)S(1)} %all-to-all-done) | copy-start | bytes 393220
  38.2 3.8 %copy-start.2 = (bf16[128,512]{1,0:T(8,128)(2,1)}, bf16[128,512]{1,0:T(8,128)(2,1)S(1)}, u32[]{:S(2)}) copy-start(bf16[128,512]{1,0:T(8,128)(2,1)S(1)} %collective-permute-done.3.refs_2_.refs_1_) | copy-start | bytes 393220
  42.0 0.7 copy-start.3
  51.1 29.1 %all-to-all-start.1 = ((f32[256,1,128]{2,1,0:T(1,128)}), f32[256,1,128]{2,1,0:T(1,128)S(1)}, u32[]{:S(2)}, u32[]{:S(2)}) async-start(f32[256,1,128]{2,1,0:T(1,128)} %bitcast.20), calls=%async_computation.1 | async-start | bytes 262144 | tf_op jit(solution)/shard_map/all_to_all | solution.py:302
  80.2 0.6 copy-start.4

commit v2 on v1

v2 whole, which is shorter than its diff:
```python
import functools

import jax
import jax.numpy as jnp
import numpy as np
from jax import lax
from jax.experimental import pallas as pl
from jax.experimental.pallas import tpu as pltpu
from jax.sharding import PartitionSpec as P

GROUPS = 32
LANES = 128
EVERY = ("tm", "row", "col")
HIGHEST = lax.Precision.HIGHEST
F32 = jnp.float32
BF16 = jnp.bfloat16
ROWS, SLOTS = 4, 16
CELLS = ROWS * SLOTS
MIB = 1024 * 1024


def group_of(channel, channels):
    return lax.shift_right_logical(channel, int(np.log2(channels // GROUPS)))


def packed_sums(sums, squares):
    channels = sums.shape[-1]
    shape = (channels, LANES)
    member = group_of(lax.broadcasted_iota(jnp.int32, shape, 0), channels) == lax.broadcasted_iota(jnp.int32, shape, 1)
    both = jnp.concatenate([sums, squares, jnp.zeros((6, channels), F32)], axis=0)
    grouped = jnp.dot(both, member.astype(F32), precision=HIGHEST, preferred_element_type=F32)
    return grouped[0:1] + pltpu.roll(grouped, GROUPS, 1)[1:2]


def affine(parts, unit, gain, bias, span):
    channels = gain.shape[-1]
    spans = lax.axis_size("tm")
    each = parts.shape[0] // spans
    now = jnp.zeros((1, LANES), F32)
    before = jnp.zeros((1, LANES), F32)
    for s in range(spans):
        part = jnp.sum(parts[s * each : (s + 1) * each], axis=0, keepdims=True)
        now = now + jnp.where(s <= span, part, 0.0)
        before = before + jnp.where(s < span, part, 0.0)
    stacked = jnp.concatenate([now, before, jnp.zeros((6, LANES), F32)], axis=0)
    stacked = jnp.concatenate([stacked, pltpu.roll(stacked, LANES - GROUPS, 1)], axis=0)
    shape = (LANES, channels)
    member = group_of(lax.broadcasted_iota(jnp.int32, shape, 1), channels) == lax.broadcasted_iota(jnp.int32, shape, 0)
    spread = jnp.dot(stacked, member.astype(F32), precision=HIGHEST, preferred_element_type=F32)
    result = []
    for k in range(2):
        count = jnp.maximum(span + 1 - k, 1).astype(F32) * unit
        mean = spread[k : k + 1] / count
        var = spread[8 + k : 9 + k] / count - mean * mean
        scale = lax.rsqrt(var + 1e-06) * gain
        result.append((scale, bias - mean * scale))
    return result


def silu(x):
    return x / (1.0 + jnp.exp(-x))


def low_sums_kernel(x_ref, sums_ref, own_ref, to_right_ref, to_left_ref):
    frames, across, height, channels = x_ref.shape
    x = x_ref[...].astype(F32).reshape(frames * across * height, channels)
    row = packed_sums(jnp.sum(x, axis=0, keepdims=True), jnp.sum(x * x, axis=0, keepdims=True))
    sums_ref[...] = jnp.broadcast_to(row, sums_ref.shape)
    block = height * frames * SLOTS
    shape = (block + 32, x.shape[0])
    to = lax.broadcasted_iota(jnp.int32, shape, 0)
    edge = to - block
    k = jnp.where(to < block, to // SLOTS, edge % 16)
    column = jnp.where(to < block, to % SLOTS - 1, jnp.where(edge < 16, across - 1, 0))
    source = ((k % frames) * across + column) * height + k // frames
    hit = (lax.broadcasted_iota(jnp.int32, shape, 1) == source) & (column >= 0) & (column < across) & (k < height * frames)
    moved = jnp.dot(hit.astype(BF16), x.astype(BF16), preferred_element_type=F32).astype(BF16)
    own_ref[...] = moved[:block]
    to_right_ref[...] = moved[block : block + 16]
    to_left_ref[...] = moved[block + 16 :]


def pack_kernel(own_ref, left_ref, right_ref, prev_own_ref, prev_left_ref, prev_right_ref, gain_ref, bias_ref, b_ref, now_ref, prev_ref, up_ref, down_ref, par_ref):
    rows = own_ref.shape[0]
    line = rows // 2
    shape = (rows, 32)
    to = lax.broadcasted_iota(jnp.int32, shape, 0)
    source = lax.broadcasted_iota(jnp.int32, shape, 1)
    slot, k = to % SLOTS, to // SLOTS
    hit = (((slot == 0) & (source == k)) | ((slot == 11) & (source == 16 + k))).astype(BF16)
    for j, (own, left, right, out) in enumerate(
        ((own_ref, left_ref, right_ref, now_ref), (prev_own_ref, prev_left_ref, prev_right_ref, prev_ref))
    ):
        both = jnp.concatenate([left[...], right[...]], axis=0)
        moved = jnp.dot(hit, both, preferred_element_type=F32)
        block = (own[...].astype(F32) + moved).astype(BF16)
        out[...] = block
        up_ref[j * line : (j + 1) * line] = block[:line]
        down_ref[j * line : (j + 1) * line] = block[line:]
    par_ref[0:1] = gain_ref[...]
    par_ref[1:2] = bias_ref[...]
    par_ref[2:3, : b_ref.shape[1]] = b_ref[...]


def position():
    tm, row, col = (lax.axis_index(a) for a in EVERY)
    return tm, row, col


def up_kernel(
    unit,
    parts_ref,
    par_ref,
    now_ref,
    prev_ref,
    above_ref,
    below_ref,
    w_ref,
    hid_ref,
    sums_ref,
    x_ref,
    wbuf,
    sems,
):
    copies = [pltpu.make_async_copy(w_ref.at[:, k // 3, k % 3], wbuf.at[k], sems.at[k]) for k in range(9)]
    for copy in copies:
        copy.start()
    tm, row, col = position()
    last_row, last_col = lax.axis_size("row") - 1, lax.axis_size("col") - 1
    (scale, offset), (scale_prev, offset_prev) = affine(parts_ref[...], unit, par_ref[0:1], par_ref[1:2], tm)
    depth = scale.shape[-1]
    line = prev_ref.shape[0] // 2
    span = line // SLOTS
    slot = lax.broadcasted_iota(jnp.int32, (line, depth), 0) % SLOTS
    inside = (slot >= jnp.where(col > 0, 0, 1)) & (slot <= jnp.where(col < last_col, 11, 10))

    def place(piece, at, r, a, b, valid):
        v = silu(piece[...].astype(F32) * a + b)
        v = jnp.where(inside & valid, v, 0.0).astype(BF16)
        for f in range(span):
            x_ref[at + f, r * SLOTS : (r + 1) * SLOTS] = v[f * SLOTS : (f + 1) * SLOTS]

    past = tm > 0
    up, down = row > 0, row < last_row
    for r in range(2):
        half = slice(r * line, (r + 1) * line)
        place(prev_ref.at[half], 0, r + 1, scale_prev, offset_prev, past)
        place(now_ref.at[half], span, r + 1, scale, offset, tm >= 0)
    for r, ref, valid in ((0, above_ref, up), (3, below_ref, down)):
        place(ref.at[line:], 0, r, scale_prev, offset_prev, past & valid)
        place(ref.at[:line], span, r, scale, offset, valid)

    frames = 2 * span - 2
    size = frames * CELLS
    width = wbuf.shape[-1]
    up_bias = par_ref[2:3, :width]
    x = jnp.concatenate([x_ref[a : a + frames].reshape(size, depth) for a in range(3)], axis=1)
    acc = [[None, None], [None, None]]

    def add(p, q, value):
        acc[p][q] = value if acc[p][q] is None else acc[p][q] + value

    for b in range(3):
        z = []
        for e in range(3):
            copies[3 * b + e].wait()
            z.append(jnp.dot(x, wbuf[3 * b + e].reshape(3 * depth, width), preferred_element_type=F32))
        even = pltpu.roll(z[0], 1, 0) + (z[1] + z[2])
        odd = (z[0] + z[1]) + pltpu.roll(z[2], size - 1, 0)
        for q, u in ((0, even), (1, odd)):
            add(0, q, pltpu.roll(u, SLOTS, 0) if b == 0 else u)
            add(1, q, pltpu.roll(u, size - SLOTS, 0) if b == 2 else u)
    total = jnp.zeros((1, width), F32)
    square = jnp.zeros((1, width), F32)
    at = lax.broadcasted_iota(jnp.int32, (span, 2, SLOTS, width), 2)
    mine = (at >= 1) & (at <= 10)
    for p in range(2):
        for q in range(2):
            hidden = (acc[p][q] + up_bias).astype(BF16)
            for f in range(frames):
                hid_ref[f, (2 * p + q) * CELLS : (2 * p + q + 1) * CELLS] = hidden[f * CELLS : (f + 1) * CELLS]
            seen = hidden[frames * CELLS - span * CELLS :].astype(F32).reshape(span, ROWS, SLOTS, width)[:, 1:3]
            seen = jnp.where(mine, seen, 0.0).reshape(-1, width)
            total = total + jnp.sum(seen, axis=0, keepdims=True)
            square = square + jnp.sum(seen * seen, axis=0, keepdims=True)
    sums_ref[...] = jnp.broadcast_to(packed_sums(total, square), sums_ref.shape)


def gather_matrix():
    m = np.zeros((3, 3, 20, 4, 2, 2, ROWS, SLOTS), np.float32)
    for b in range(3):
        for e in range(3):
            for y in range(4):
                for x in range(20):
                    v, u = y + b - 1, x + e - 1
                    m[b, e, x, y, v % 2, u % 2, v // 2 + 1, u // 2 + 1] = 1.0
    return m.reshape(720, 4 * CELLS)


def res_kernel(unit, parts_ref, gain_ref, bias_ref, b_ref, hid_ref, pick_ref, w_ref, out_ref, g_ref, wbuf, sems):
    copies = [pltpu.make_async_copy(w_ref.at[k], wbuf.at[k], sems.at[k]) for k in range(3)]
    for copy in copies:
        copy.start()
    tm, row, col = position()
    last_row, last_col = lax.axis_size("row") - 1, lax.axis_size("col") - 1
    (scale, offset), (scale_prev, offset_prev) = affine(parts_ref[...], unit, gain_ref[...], bias_ref[...], tm)
    width = scale.shape[-1]
    cell = lax.broadcasted_iota(jnp.int32, (4 * CELLS, width), 0)
    parity, r, slot = cell // CELLS, (cell // SLOTS) % ROWS, cell % SLOTS
    y, x = 2 * (r - 1) + parity // 2, 2 * (slot - 1) + parity % 2
    inside = ((y >= 0) | (row > 0)) & ((y < 4) | (row < last_row)) & ((x >= 0) | (col > 0)) & ((x < 20) | (col < last_col))
    n_now = out_ref.shape[0]
    n_prev = hid_ref.shape[0] - n_now
    area = 80
    for f in range(n_prev + n_now):
        a, b = (scale_prev, offset_prev) if f < n_prev else (scale, offset)
        valid = inside & (tm > 0) if f < n_prev else inside
        v = jnp.where(valid, silu(hid_ref[f].astype(F32) * a + b), 0.0)
        picked = jnp.dot(pick_ref[...], v.astype(BF16), preferred_element_type=F32).astype(BF16)
        for k in range(9):
            g_ref[f * area : (f + 1) * area, k * width : (k + 1) * width] = picked[k * area : (k + 1) * area]
    total = None
    for a in range(3):
        copies[a].wait()
        part = jnp.dot(
            g_ref[a * area : (a + n_now) * area], wbuf[a].reshape(9 * width, width), preferred_element_type=F32
        )
        total = part if total is None else total + part
    for f in range(n_now):
        hidden = jnp.dot(pick_ref[4 * area : 5 * area], hid_ref[n_prev + f], preferred_element_type=F32)
        decoded = total[f * area : (f + 1) * area] + b_ref[...] + hidden
        out_ref[f] = decoded.reshape(out_ref.shape[1:]).astype(BF16)


def shifted(value, axes, steps):
    sizes = tuple(lax.axis_size(a) for a in axes)
    place = np.arange(int(np.prod(sizes))).reshape(sizes)
    route = [(int(place[at]), int(place[tuple((i + s) % n for i, s, n in zip(at, steps, sizes))])) for at in np.ndindex(*sizes)]
    return lax.ppermute(value, axes, route)


def params(mib):
    return pltpu.CompilerParams(vmem_limit_bytes=mib * MIB)


def in_hbm(array):
    return pltpu.with_memory_space_constraint(array, pltpu.HBM)


VM = pl.BlockSpec(memory_space=pltpu.VMEM)
HBM = pl.BlockSpec(memory_space=pltpu.HBM)


def local(features, gain_low, bias_low, w_up, b_up, gain_high, bias_high, w_res, b_res):
    n_tm, n_row, n_col = (lax.axis_size(a) for a in EVERY)
    devices = n_tm * n_row * n_col
    frames, height, across, depth = features.shape
    width = w_up.shape[-1]
    low_unit = float(n_row * n_col * frames * height * across * (depth // GROUPS))
    high_unit = float(n_row * n_col * frames * 4 * height * across * (width // GROUPS))

    block = height * frames * SLOTS
    line = frames * SLOTS
    sums, own, to_right, to_left = pl.pallas_call(
        low_sums_kernel,
        out_shape=(
            jax.ShapeDtypeStruct((devices, LANES), F32),
            jax.ShapeDtypeStruct((block, depth), BF16),
            jax.ShapeDtypeStruct((16, depth), BF16),
            jax.ShapeDtypeStruct((16, depth), BF16),
        ),
        in_specs=[VM],
        out_specs=(VM,) * 4,
        compiler_params=params(16),
        name="low_sums",
    )(features.transpose(0, 2, 1, 3))
    prev_own = shifted(own, ("tm",), (1,))
    prev_left = shifted(to_right, ("tm", "col"), (1, 1))
    prev_right = shifted(to_left, ("tm", "col"), (1, -1))
    left = shifted(to_right, ("col",), (1,))
    right = shifted(to_left, ("col",), (-1,))
    low_parts = lax.all_to_all(sums, EVERY, 0, 0)
    gl, bl, bu = gain_low.reshape(1, -1), bias_low.reshape(1, -1), b_up.reshape(1, -1)
    gh, bh, br = gain_high.reshape(1, -1), bias_high.reshape(1, -1), b_res.reshape(1, -1)
    now, prev, up, down, par = pl.pallas_call(
        pack_kernel,
        out_shape=(jax.ShapeDtypeStruct((block, depth), BF16),) * 4 + (jax.ShapeDtypeStruct((8, depth), F32),),
        in_specs=[VM] * 9,
        out_specs=(VM,) * 5,
        compiler_params=params(16),
        name="pack",
    )(own, left, right, prev_own, prev_left, prev_right, in_hbm(gl), in_hbm(bl), in_hbm(bu))
    above = shifted(down, ("row",), (1,))
    below = shifted(up, ("row",), (-1,))

    hidden, high_sums = pl.pallas_call(
        functools.partial(up_kernel, low_unit),
        out_shape=(
            jax.ShapeDtypeStruct((2 + frames, 4 * CELLS, width), BF16),
            jax.ShapeDtypeStruct((devices, LANES), F32),
        ),
        in_specs=[VM] * 6 + [HBM],
        out_specs=(VM, VM),
        scratch_shapes=[
            pltpu.VMEM((2 * frames, CELLS, depth), BF16),
            pltpu.VMEM((9, 3, depth, width), BF16),
            pltpu.SemaphoreType.DMA((9,)),
        ],
        compiler_params=params(28),
        name="up",
    )(low_parts, par, now, prev, above, below, in_hbm(w_up))
    high_parts = lax.all_to_all(high_sums, EVERY, 0, 0)

    area = 4 * height * across
    decoded = pl.pallas_call(
        functools.partial(res_kernel, high_unit),
        out_shape=jax.ShapeDtypeStruct((frames, 2 * across, 2 * height, width), BF16),
        in_specs=[VM] * 6 + [HBM],
        out_specs=VM,
        scratch_shapes=[
            pltpu.VMEM(((2 + frames) * area, 9 * width), BF16),
            pltpu.VMEM((3, 3, 3, width, width), BF16),
            pltpu.SemaphoreType.DMA((3,)),
        ],
        compiler_params=params(24),
        name="res",
    )(high_parts, gh, bh, br, hidden, jnp.asarray(gather_matrix(), BF16), in_hbm(w_res))
    return decoded.transpose(0, 2, 1, 3)


def solution(mesh):
    in_specs = (P("tm", "row", "col", None), P(), P(), P(), P(), P(), P(), P(), P())
    out_specs = P("tm", "row", "col", None)
    return jax.shard_map(local, mesh=mesh, in_specs=in_specs, out_specs=out_specs, check_vma=False)
```

time: 87.1 us -> 72.8 us (0.84)
  blocking collectives: 0 us -> 25.3 us
  starting transfers between devices: 46.1 us -> 25.6 us
  Pallas kernels: 24.2 us -> 15.4 us
  waiting for transfers between devices: 13.3 us -> 5.15 us
  local copies, waits for them, and re-layouts: 2.8 us -> 0.95 us
    all_to_all x0 -> x1, blocking collectives: none -> 25.3 us  [local(): high_parts = lax.all_to_all(high_sums, EVERY, 0, 0)]
    all_to_all x1 -> x0, starting transfers between devices: 16.2 us -> none  [local(): high_parts = lax.all_to_all(high_sums, EVERY, 0, 0)]
    all_to_all x1 -> x0, waiting for transfers between devices: 6.65 us -> none  [local(): high_parts = lax.all_to_all(high_sums, EVERY, 0, 0)]
    pallas_call x3 -> x2, Pallas kernels: 16.5 us -> 9.86 us  [the longest x1 8.95 us: local(): pl.pallas_call(functools.partial(up_kernel, low_unit), out_shape=(jax.Sha...]
    ppermute x5 -> x7, starting transfers between devices: 14.3 us -> 10.8 us  [shifted(): return lax.ppermute(value, axes, route)]
    ppermute x5 -> x7, waiting for transfers between devices: 6.67 us -> 4.7 us  [shifted(): return lax.ppermute(value, axes, route)]
    pallas_call x1, Pallas kernels: 5.79 us -> 4.46 us  [local(): pl.pallas_call(functools.partial(res_kernel, high_unit), out_shape=jax.Sh...]
    unnamed x14 -> x10, local copies, waits for them, and re-layouts: 1.89 us -> 0.95 us
  transfers between devices with their start and end apart: 7 -> 8, of which waited for: 4 -> 3; matrix products, arithmetic and copies ran while one was open for 1% -> 0% of each run, Pallas kernels for 9% -> 1%
where the time goes in v2:
time: 72.8 us; the launch traced here: 72.6 us
  starting transfers between devices  25.6 us (35%)
  blocking collectives  25.3 us (35%)
  Pallas kernels  15.4 us (21%)
  waiting for transfers between devices  5.15 us (7%)
  local copies, waits for them, and re-layouts  0.95 us (1%)
    all_to_all x1, blocking collectives, local(): high_parts = lax.all_to_all(high_sums, EVERY, 0, 0)  25.3 us
    all_to_all x1, starting transfers between devices, local(): low_parts = lax.all_to_all(sums, EVERY, 0, 0)  14.8 us
    ppermute x7, starting transfers between devices, shifted(): return lax.ppermute(value, axes, route)  10.8 us
    pallas_call x1, Pallas kernels, local(): pl.pallas_call(functools.partial(up_kernel, low_unit), out_shape=(jax.Sha...  8.95 us
    ppermute x7, waiting for transfers between devices, shifted(): return lax.ppermute(value, axes, route)  4.7 us
    pallas_call x1, Pallas kernels, local(): pl.pallas_call(functools.partial(res_kernel, high_unit), out_shape=jax.Sh...  4.46 us
  transfers between devices with their start and end apart: 8, of which 3 were waited for; matrix products, arithmetic and copies ran while one was open for 0% of the time, Pallas kernels for 1%

profile of v2, /device:TPU:1, one launch (start us, length us, event | category | flops | bytes accessed | tf_op | source)
XLA Modules:
  0.0 72.6 jit_solution(2615552489697398340)
XLA Ops:
  0.0 0.0 copy-start
  0.0 0.0 copy-start.1
  0.0 0.9 %copy-done.1 = bf16[4,2,10,512]{3,1,2,0:T(2,128)(2,1)S(1)} copy-done((bf16[4,2,10,512]{3,1,2,0:T(2,128)(2,1)S(1)}, bf16[4,2,10,512]{3,1,2,0:T(2,128)(2,1)}, u32[]{:S(2)}) %copy-start.1) | copy-done | bytes 81944
  0.9 0.0 copy-start.2
  0.9 0.0 copy-start.3
  0.9 0.0 copy-start.4
  0.9 1.1 %low_sums.1 = (f32[256,128]{1,0:T(8,128)}, bf16[128,512]{1,0:T(8,128)(2,1)S(1)}, bf16[16,512]{1,0:T(8,128)(2,1)S(1)}, bf16[16,512]{1,0:T(8,128)(2,1)S(1)}) custom-call(bf16[4,10,2,512]{3,2,1,0:T(2,128)(2,1)S(1)} %bitcast.19), custom_call_target="tpu_custom_call" | custom-call | tf_op jit(solution)/shard_map/low_sums/pallas_call | solution.py:264
  2.0 2.1 %collective-permute-start.2 = (bf16[128,512]{1,0:T(8,128)(2,1)S(1)}, bf16[128,512]{1,0:T(8,128)(2,1)S(1)}, u32[]{:S(2)}, u32[]{:S(2)}) collective-permute-start(bf16[128,512]{1,0:T(8,128)(2,1)S(1)} %get-tuple-element.17.own_ref), channel_id=1, source_target_pairs={{0,64},{64,128},{128,192},{192,0},{1,65},{65,129},{129,193},{193,1... | collective-permute-start | bytes 393224 | tf_op jit(solution)/shard_map/ppermute | solution.py:239
  4.1 14.8 %all-to-all-start = ((f32[256,1,128]{2,1,0:T(1,128)}), f32[256,1,128]{2,1,0:T(1,128)S(1)}, u32[]{:S(2)}, u32[]{:S(2)}) async-start(f32[256,1,128]{2,1,0:T(1,128)} %bitcast.2), calls=%async_computation | async-start | bytes 262144 | tf_op jit(solution)/shard_map/all_to_all | solution.py:282
  19.0 2.8 %collective-permute-start.3 = (bf16[16,512]{1,0:T(8,128)(2,1)S(1)}, bf16[16,512]{1,0:T(8,128)(2,1)S(1)}, u32[]{:S(2)}, u32[]{:S(2)}) collective-permute-start(bf16[16,512]{1,0:T(8,128)(2,1)S(1)} %get-tuple-element.18), channel_id=1, source_target_pairs={{0,65},{1,66},{2,67},{3,68},{4,69},{5,70},{6,71},{7,72},{8,73},{9,... | collective-permute-start | bytes 49160 | tf_op jit(solution)/shard_map/ppermute | solution.py:239
  21.8 0.3 collective-permute-start
  22.1 1.3 %collective-permute-start.4 = (bf16[16,512]{1,0:T(8,128)(2,1)S(1)}, bf16[16,512]{1,0:T(8,128)(2,1)S(1)}, u32[]{:S(2)}, u32[]{:S(2)}) collective-permute-start(bf16[16,512]{1,0:T(8,128)(2,1)S(1)} %get-tuple-element.19), channel_id=1, source_target_pairs={{0,79},{1,64},{2,65},{3,66},{4,67},{5,68},{6,69},{7,70},{8,71},{9,... | collective-permute-start | bytes 49160 | tf_op jit(solution)/shard_map/ppermute | solution.py:239
  23.4 1.4 %collective-permute-start.1 = (bf16[16,512]{1,0:T(8,128)(2,1)S(1)}, bf16[16,512]{1,0:T(8,128)(2,1)S(1)}, u32[]{:S(2)}, u32[]{:S(2)}) collective-permute-start(bf16[16,512]{1,0:T(8,128)(2,1)S(1)} %get-tuple-element.19), channel_id=1, source_target_pairs={{0,15},{1,0},{2,1},{3,2},{4,3},{5,4},{6,5},{7,6},{8,7},{9,8},{10,9... | collective-permute-start | bytes 49160 | tf_op jit(solution)/shard_map/ppermute | solution.py:239
  24.8 0.0 collective-permute-done.3.prev_left_ref
  24.8 0.0 collective-permute-done.left_ref
  24.9 2.8 %collective-permute-done.4.prev_right_ref = bf16[16,512]{1,0:T(8,128)(2,1)S(1)} collective-permute-done((bf16[16,512]{1,0:T(8,128)(2,1)S(1)}, bf16[16,512]{1,0:T(8,128)(2,1)S(1)}, u32[]{:S(2)}, u32[]{:S(2)}) %collective-permute-start.4) | collective-permute-done | bytes 16416 | tf_op jit(solution)/shard_map/ppermute | solution.py:239
  27.6 0.0 collective-permute-done.1.right_ref
  27.6 0.0 collective-permute-done.2.prev_own_ref
  27.6 0.9 %pack.1 = (bf16[128,512]{1,0:T(8,128)(2,1)S(1)}, bf16[128,512]{1,0:T(8,128)(2,1)S(1)}, bf16[128,512]{1,0:T(8,128)(2,1)S(1)}, bf16[128,512]{1,0:T(8,128)(2,1)S(1)}, f32[8,512]{1,0:T(8,128)S(1)}) custom-call(bf16[128,512]{1,0:T(8,128)(2,1)S(1)} %get-tuple-element.17.own_ref, bf16[16,512]{1,0:T(8,128)(2,1)S(1)} %collective-permute-done.left_ref, ...), custom_call_target="tpu_custom_call" | custom-call | tf_op jit(solution)/shard_map/pack/pallas_call | solution.py:285
  28.6 1.3 %collective-permute-start.5 = (bf16[128,512]{1,0:T(8,128)(2,1)S(1)}, bf16[128,512]{1,0:T(8,128)(2,1)S(1)}, u32[]{:S(2)}, u32[]{:S(2)}) collective-permute-start(bf16[128,512]{1,0:T(8,128)(2,1)S(1)} %get-tuple-element.23), channel_id=1, source_target_pairs={{0,16},{16,32},{32,48},{48,0},{1,17},{17,33},{33,49},{49,1},{2,18}... | collective-permute-start | bytes 393224 | tf_op jit(solution)/shard_map/ppermute | solution.py:239
  29.8 1.5 %collective-permute-start.6 = (bf16[128,512]{1,0:T(8,128)(2,1)S(1)}, bf16[128,512]{1,0:T(8,128)(2,1)S(1)}, u32[]{:S(2)}, u32[]{:S(2)}) collective-permute-start(bf16[128,512]{1,0:T(8,128)(2,1)S(1)} %get-tuple-element.24), channel_id=1, source_target_pairs={{0,48},{16,0},{32,16},{48,32},{1,49},{17,1},{33,17},{49,33},{2,50}... | collective-permute-start | bytes 393224 | tf_op jit(solution)/shard_map/ppermute | solution.py:239
  31.3 0.4 all-to-all-done
  31.8 1.9 %collective-permute-done.5.above_ref = bf16[128,512]{1,0:T(8,128)(2,1)S(1)} collective-permute-done((bf16[128,512]{1,0:T(8,128)(2,1)S(1)}, bf16[128,512]{1,0:T(8,128)(2,1)S(1)}, u32[]{:S(2)}, u32[]{:S(2)}) %collective-permute-start.5) | collective-permute-done | bytes 131104 | tf_op jit(solution)/shard_map/ppermute | solution.py:239
  33.7 0.0 collective-permute-done.6.below_ref
  33.7 8.9 %up.1 = (bf16[6,256,256]{2,1,0:T(8,128)(2,1)S(1)}, f32[256,128]{1,0:T(8,128)S(1)}) custom-call(f32[256,128]{1,0:T(8,128)S(1)} %bitcast.16, f32[8,512]{1,0:T(8,128)S(1)} %get-tuple-element.20.par_ref, bf16[128,512]{1,0:T(8,128)(2,1)S(1)} %get-tuple-element.21.now_ref, bf16[128,512]{1,0:T(8,128)(2,1)S(1)} %get-tuple-element.22.prev_ref, ...), custom_call_target="tpu_custom_call" | custom-call | tf_op jit(solution)/shard_map/up/pallas_call | solution.py:296
  42.6 25.3 %all_to_all.22 = f32[256,1,128]{2,1,0:T(1,128)S(1)} all-to-all(f32[256,1,128]{2,1,0:T(1,128)S(1)} %bitcast.18), channel_id=1, replica_groups=mesh['tm'=4,'row'=4,'col'=16] {'tm','row','col'}, dimensions={0} | all-to-all | bytes 262144 | tf_op jit(solution)/shard_map/all_to_all | solution.py:312
  68.0 0.0 copy-done
  68.0 0.0 copy-done.2
  68.0 0.0 copy-done.3
  68.0 0.0 copy-done.4
  68.0 4.5 %res.1 = bf16[4,20,4,256]{3,2,1,0:T(4,128)(2,1)} custom-call(f32[256,128]{1,0:T(8,128)S(1)} %bitcast.17, f32[1,256]{1,0:T(1,128)S(1)} %bitcast.20, f32[1,256]{1,0:T(1,128)S(1)} %bitcast.21, f32[1,256]{1,0:T(1,128)S(1)} %bitcast.22, bf16[6,256,256]{2,1,0:T(8,128)(2,1)S(1)} %get-tuple-element.26.hid_ref, bf16[720,256]{1,0:T(8,128)(2,1)S(1)} %copy-done, ...), custom_call_target="tpu_custom_call" | custom-call | tf_op jit(solution)/shard_map/res/pallas_call | solution.py:315
Async XLA Ops:
  0.0 68.0 %copy-start = (bf16[720,256]{1,0:T(8,128)(2,1)S(1)}, bf16[720,256]{1,0:T(8,128)(2,1)}, u32[]{:S(2)}) copy-start(bf16[720,256]{1,0:T(8,128)(2,1)} %constant.2.clone.pick_ref) | copy-start | bytes 1105924
  0.0 0.9 %copy-start.1 = (bf16[4,2,10,512]{3,1,2,0:T(2,128)(2,1)S(1)}, bf16[4,2,10,512]{3,1,2,0:T(2,128)(2,1)}, u32[]{:S(2)}) copy-start(bf16[4,2,10,512]{3,1,2,0:T(2,128)(2,1)} %param.10) | copy-start | bytes 245764
  0.9 67.0 %copy-start.2 = (f32[256]{0:T(256)S(1)}, f32[256]{0:T(256)}, u32[]{:S(2)}) copy-start(f32[256]{0:T(256)} %param.15) | copy-start | bytes 3076
  0.9 67.0 %copy-start.3 = (f32[256]{0:T(256)S(1)}, f32[256]{0:T(256)}, u32[]{:S(2)}) copy-start(f32[256]{0:T(256)} %param.16) | copy-start | bytes 3076
  0.9 67.0 %copy-start.4 = (f32[256]{0:T(256)S(1)}, f32[256]{0:T(256)}, u32[]{:S(2)}) copy-start(f32[256]{0:T(256)} %param.18) | copy-start | bytes 3076
  2.0 25.6 %collective-permute-start.2 = (bf16[128,512]{1,0:T(8,128)(2,1)S(1)}, bf16[128,512]{1,0:T(8,128)(2,1)S(1)}, u32[]{:S(2)}, u32[]{:S(2)}) collective-permute-start(bf16[128,512]{1,0:T(8,128)(2,1)S(1)} %get-tuple-element.17.own_ref), channel_id=1, source_target_pairs={{0,64},{64,128},{128,192},{192,0},{1,65},{65,129},{129,193},{193,1... | collective-permute-start | bytes 393224 | tf_op jit(solution)/shard_map/ppermute | solution.py:239
  4.1 27.6 %all-to-all-start = ((f32[256,1,128]{2,1,0:T(1,128)}), f32[256,1,128]{2,1,0:T(1,128)S(1)}, u32[]{:S(2)}, u32[]{:S(2)}) async-start(f32[256,1,128]{2,1,0:T(1,128)} %bitcast.2), calls=%async_computation | async-start | bytes 262144 | tf_op jit(solution)/shard_map/all_to_all | solution.py:282
  19.0 5.9 %collective-permute-start.3 = (bf16[16,512]{1,0:T(8,128)(2,1)S(1)}, bf16[16,512]{1,0:T(8,128)(2,1)S(1)}, u32[]{:S(2)}, u32[]{:S(2)}) collective-permute-start(bf16[16,512]{1,0:T(8,128)(2,1)S(1)} %get-tuple-element.18), channel_id=1, source_target_pairs={{0,65},{1,66},{2,67},{3,68},{4,69},{5,70},{6,71},{7,72},{8,73},{9,... | collective-permute-start | bytes 49160 | tf_op jit(solution)/shard_map/ppermute | solution.py:239
  21.8 3.1 %collective-permute-start = (bf16[16,512]{1,0:T(8,128)(2,1)S(1)}, bf16[16,512]{1,0:T(8,128)(2,1)S(1)}, u32[]{:S(2)}, u32[]{:S(2)}) collective-permute-start(bf16[16,512]{1,0:T(8,128)(2,1)S(1)} %get-tuple-element.18), channel_id=1, source_target_pairs={{0,1},{1,2},{2,3},{3,4},{4,5},{5,6},{6,7},{7,8},{8,9},{9,10},{10,1... | collective-permute-start | bytes 49160 | tf_op jit(solution)/shard_map/ppermute | solution.py:239
  22.1 5.6 %collective-permute-start.4 = (bf16[16,512]{1,0:T(8,128)(2,1)S(1)}, bf16[16,512]{1,0:T(8,128)(2,1)S(1)}, u32[]{:S(2)}, u32[]{:S(2)}) collective-permute-start(bf16[16,512]{1,0:T(8,128)(2,1)S(1)} %get-tuple-element.19), channel_id=1, source_target_pairs={{0,79},{1,64},{2,65},{3,66},{4,67},{5,68},{6,69},{7,70},{8,71},{9,... | collective-permute-start | bytes 49160 | tf_op jit(solution)/shard_map/ppermute | solution.py:239
  23.4 4.2 %collective-permute-start.1 = (bf16[16,512]{1,0:T(8,128)(2,1)S(1)}, bf16[16,512]{1,0:T(8,128)(2,1)S(1)}, u32[]{:S(2)}, u32[]{:S(2)}) collective-permute-start(bf16[16,512]{1,0:T(8,128)(2,1)S(1)} %get-tuple-element.19), channel_id=1, source_target_pairs={{0,15},{1,0},{2,1},{3,2},{4,3},{5,4},{6,5},{7,6},{8,7},{9,8},{10,9... | collective-permute-start | bytes 49160 | tf_op jit(solution)/shard_map/ppermute | solution.py:239
  28.6 5.1 %collective-permute-start.5 = (bf16[128,512]{1,0:T(8,128)(2,1)S(1)}, bf16[128,512]{1,0:T(8,128)(2,1)S(1)}, u32[]{:S(2)}, u32[]{:S(2)}) collective-permute-start(bf16[128,512]{1,0:T(8,128)(2,1)S(1)} %get-tuple-element.23), channel_id=1, source_target_pairs={{0,16},{16,32},{32,48},{48,0},{1,17},{17,33},{33,49},{49,1},{2,18}... | collective-permute-start | bytes 393224 | tf_op jit(solution)/shard_map/ppermute | solution.py:239
  29.8 3.8 %collective-permute-start.6 = (bf16[128,512]{1,0:T(8,128)(2,1)S(1)}, bf16[128,512]{1,0:T(8,128)(2,1)S(1)}, u32[]{:S(2)}, u32[]{:S(2)}) collective-permute-start(bf16[128,512]{1,0:T(8,128)(2,1)S(1)} %get-tuple-element.24), channel_id=1, source_target_pairs={{0,48},{16,0},{32,16},{48,32},{1,49},{17,1},{33,17},{49,33},{2,50}... | collective-permute-start | bytes 393224 | tf_op jit(solution)/shard_map/ppermute | solution.py:239

commit v3 on v2

v3 whole, which is shorter than its diff:
```python
import functools

import jax
import jax.numpy as jnp
import numpy as np
from jax import lax
from jax.experimental import pallas as pl
from jax.experimental.pallas import tpu as pltpu
from jax.sharding import PartitionSpec as P

GROUPS = 32
LANES = 128
EVERY = ("tm", "row", "col")
HIGHEST = lax.Precision.HIGHEST
F32 = jnp.float32
BF16 = jnp.bfloat16
ROWS, ACROSS, SLOTS = 4, 12, 16
CELLS = ROWS * ACROSS
MIB = 1024 * 1024


def group_of(channel, channels):
    return lax.shift_right_logical(channel, int(np.log2(channels // GROUPS)))


def packed_sums(sums, squares):
    channels = sums.shape[-1]
    shape = (channels, LANES)
    member = group_of(lax.broadcasted_iota(jnp.int32, shape, 0), channels) == lax.broadcasted_iota(jnp.int32, shape, 1)
    both = jnp.concatenate([sums, squares, jnp.zeros((6, channels), F32)], axis=0)
    grouped = jnp.dot(both, member.astype(F32), precision=HIGHEST, preferred_element_type=F32)
    return grouped[0:1] + pltpu.roll(grouped, GROUPS, 1)[1:2]


def affine(parts, unit, gain, bias, span):
    channels = gain.shape[-1]
    spans = lax.axis_size("tm")
    each = parts.shape[0] // spans
    now = jnp.zeros((1, LANES), F32)
    before = jnp.zeros((1, LANES), F32)
    for s in range(spans):
        part = jnp.sum(parts[s * each : (s + 1) * each], axis=0, keepdims=True)
        now = now + jnp.where(s <= span, part, 0.0)
        before = before + jnp.where(s < span, part, 0.0)
    stacked = jnp.concatenate([now, before, jnp.zeros((6, LANES), F32)], axis=0)
    stacked = jnp.concatenate([stacked, pltpu.roll(stacked, LANES - GROUPS, 1)], axis=0)
    shape = (LANES, channels)
    member = group_of(lax.broadcasted_iota(jnp.int32, shape, 1), channels) == lax.broadcasted_iota(jnp.int32, shape, 0)
    spread = jnp.dot(stacked, member.astype(F32), precision=HIGHEST, preferred_element_type=F32)
    result = []
    for k in range(2):
        count = jnp.maximum(span + 1 - k, 1).astype(F32) * unit
        mean = spread[k : k + 1] / count
        var = spread[8 + k : 9 + k] / count - mean * mean
        scale = lax.rsqrt(var + 1e-06) * gain
        result.append((scale, bias - mean * scale))
    return result


def silu(x):
    return x / (1.0 + jnp.exp(-x))


def low_sums_kernel(x_ref, sums_ref):
    x = x_ref[...].astype(F32)
    row = packed_sums(jnp.sum(x, axis=0, keepdims=True), jnp.sum(x * x, axis=0, keepdims=True))
    sums_ref[...] = jnp.broadcast_to(row, sums_ref.shape)


def lay_out_kernel(x_ref, own_ref, to_core_ref, to_chip_ref):
    frames, across, height, channels = x_ref.shape
    x = x_ref[...].astype(F32).reshape(frames * across * height, channels)
    block = height * frames * SLOTS
    shape = (block + 32, x.shape[0])
    to = lax.broadcasted_iota(jnp.int32, shape, 0)
    edge = to - block
    odd = lax.axis_index("col") % 2
    last = (edge < 16).astype(jnp.int32) != odd
    k = jnp.where(to < block, to // SLOTS, edge % 16)
    column = jnp.where(to < block, to % SLOTS - 1, jnp.where(last, across - 1, 0))
    source = ((k % frames) * across + column) * height + k // frames
    hit = (lax.broadcasted_iota(jnp.int32, shape, 1) == source) & (column >= 0) & (column < across) & (k < height * frames)
    moved = jnp.dot(hit.astype(BF16), x.astype(BF16), preferred_element_type=F32).astype(BF16)
    own_ref[...] = moved[:block]
    to_core_ref[...] = moved[block : block + 16]
    to_chip_ref[...] = moved[block + 16 :]


def narrow(rows):
    shape = (rows // 16 * 12, rows)
    to, source = (lax.broadcasted_iota(jnp.int32, shape, d) for d in range(2))
    return (source == to // 12 * SLOTS + to % 12).astype(BF16)


def widen(rows):
    shape = (rows // 12 * 16, rows)
    to, source = (lax.broadcasted_iota(jnp.int32, shape, d) for d in range(2))
    return ((to % SLOTS < 12) & (source == to // SLOTS * 12 + to % SLOTS)).astype(BF16)


def pack_kernel(own_ref, core_ref, chip_ref, prev_own_ref, prev_core_ref, prev_chip_ref, now_ref, prev_ref, up_ref, down_ref):
    rows = own_ref.shape[0]
    line = rows // 2
    shape = (rows, 32)
    to = lax.broadcasted_iota(jnp.int32, shape, 0)
    source = lax.broadcasted_iota(jnp.int32, shape, 1)
    core_slot = jnp.where(lax.axis_index("col") % 2 == 0, 11, 0)
    slot, k = to % SLOTS, to // SLOTS
    hit = (((slot == core_slot) & (source == k)) | ((slot == 11 - core_slot) & (source == 16 + k))).astype(BF16)
    take = narrow(line)
    for j, (own, core, chip, out) in enumerate(
        ((own_ref, core_ref, chip_ref, now_ref), (prev_own_ref, prev_core_ref, prev_chip_ref, prev_ref))
    ):
        both = jnp.concatenate([core[...], chip[...]], axis=0)
        moved = jnp.dot(hit, both, preferred_element_type=F32)
        block = (own[...].astype(F32) + moved).astype(BF16)
        out[...] = block
        for ref, half in ((up_ref, block[:line]), (down_ref, block[line:])):
            sent = jnp.dot(take, half, preferred_element_type=F32).astype(BF16)
            ref[j * sent.shape[0] : (j + 1) * sent.shape[0]] = sent


def fetch_kernel(
    unit,
    parts_ref,
    gain_ref,
    bias_ref,
    b_ref,
    w_ref,
    coef_ref,
    w_out_ref,
    gain_buf,
    bias_buf,
    b_buf,
    small,
    sems,
):
    pairs = ((gain_ref, gain_buf), (bias_ref, bias_buf), (b_ref, b_buf))
    few = [pltpu.make_async_copy(ref, buf, small.at[k]) for k, (ref, buf) in enumerate(pairs)]
    weights = [pltpu.make_async_copy(w_ref.at[a], w_out_ref.at[a], sems.at[a]) for a in range(3)]
    for copy in few + weights:
        copy.start()
    for copy in few:
        copy.wait()
    now, before = affine(parts_ref[...], unit, gain_buf[...], bias_buf[...], lax.axis_index("tm"))
    for k, row in enumerate(now + before):
        coef_ref[k : k + 1] = row
    coef_ref[4:5, : b_buf.shape[1]] = b_buf[...]
    for copy in weights:
        copy.wait()


def position():
    tm, row, col = (lax.axis_index(a) for a in EVERY)
    return tm, row, col


def up_kernel(
    coef_ref, now_ref, prev_ref, above_ref, below_ref, w_ref, w_res_ref, hid_ref, sums_ref, w_res_out_ref, x_ref, acc_ref, sem
):
    ahead = pltpu.make_async_copy(w_res_ref.at[0], w_res_out_ref, sem)
    ahead.start()
    tm, row, col = position()
    last_row, last_col = lax.axis_size("row") - 1, lax.axis_size("col") - 1
    scale, offset, scale_prev, offset_prev = (coef_ref[k : k + 1] for k in range(4))
    depth = scale.shape[-1]
    line = prev_ref.shape[0] // 2
    span = line // SLOTS
    sent = above_ref.shape[0] // 2
    slot = lax.broadcasted_iota(jnp.int32, (line, depth), 0) % SLOTS
    inside = (slot >= jnp.where(col > 0, 0, 1)) & (slot <= jnp.where(col < last_col, 11, 10))
    up, down = row > 0, row < last_row

    def active(piece, a, b, valid):
        v = piece[...]
        if v.shape[0] < line:
            v = jnp.dot(widen(v.shape[0]), v, preferred_element_type=F32)
        v = silu(v.astype(F32) * a + b)
        return jnp.where(inside & valid, v, 0.0).astype(BF16)

    take = narrow(ROWS * SLOTS)

    def place_span(block, part, at, a, b, valid):
        rows = [
            active(above_ref.at[part], a, b, valid & up),
            active(block.at[:line], a, b, valid),
            active(block.at[line:], a, b, valid),
            active(below_ref.at[part], a, b, valid & down),
        ]
        for f in range(span):
            frame = jnp.concatenate([r[f * SLOTS : (f + 1) * SLOTS] for r in rows], axis=0)
            x_ref[at + f] = jnp.dot(take, frame, preferred_element_type=F32).astype(BF16)

    place_span(prev_ref, slice(sent, 2 * sent), 0, scale_prev, offset_prev, tm > 0)
    place_span(now_ref, slice(0, sent), span, scale, offset, tm >= 0)
    acc_ref[...] = jnp.zeros_like(acc_ref)

    frames = 2 * span - 2
    size = frames * CELLS
    width = w_ref.shape[-1]
    up_bias = coef_ref[4:5, :width]
    for b in range(3):

        @pl.when(tm >= 0)
        def _():
            x = jnp.concatenate([x_ref[a : a + frames].reshape(size, depth) for a in range(3)], axis=1)
            z = [
                jnp.dot(x, w_ref[:, b, e].reshape(3 * depth, width), preferred_element_type=F32) for e in range(3)
            ]
            even = pltpu.roll(z[0], 1, 0) + (z[1] + z[2])
            odd = (z[0] + z[1]) + pltpu.roll(z[2], size - 1, 0)
            for p in range(2):
                at = SLOTS + ACROSS * ((b == 0 and p == 0) - (b == 2 and p == 1))
                for q, u in ((0, even), (1, odd)):
                    acc_ref[2 * p + q, at : at + size] += u

    total = jnp.zeros((1, width), F32)
    square = jnp.zeros((1, width), F32)
    cell = lax.broadcasted_iota(jnp.int32, (span * CELLS, width), 0) % CELLS
    r, c = cell // ACROSS, cell % ACROSS
    mine = (r >= 1) & (r <= 2) & (c >= 1) & (c <= 10)
    for k in range(4):
        hidden = (acc_ref[k, SLOTS : SLOTS + size] + up_bias).astype(BF16)
        for f in range(frames):
            hid_ref[f, k * CELLS : (k + 1) * CELLS] = hidden[f * CELLS : (f + 1) * CELLS]
        seen = jnp.where(mine, hidden[size - span * CELLS :].astype(F32), 0.0)
        total = total + jnp.sum(seen, axis=0, keepdims=True)
        square = square + jnp.sum(seen * seen, axis=0, keepdims=True)
    sums_ref[...] = jnp.broadcast_to(packed_sums(total, square), sums_ref.shape)
    ahead.wait()


def gather_matrix():
    m = np.zeros((3, 3, 20, 4, 2, 2, ROWS, ACROSS), np.float32)
    for b in range(3):
        for e in range(3):
            for y in range(4):
                for x in range(20):
                    v, u = y + b - 1, x + e - 1
                    m[b, e, x, y, v % 2, u % 2, v // 2 + 1, u // 2 + 1] = 1.0
    return m.reshape(720, 4 * CELLS)


def res_kernel(unit, parts_ref, gain_ref, bias_ref, b_ref, hid_ref, pick_ref, w_first_ref, w_ref, out_ref, g_ref, t_ref, wbuf, sems):
    copies = [pltpu.make_async_copy(w_ref.at[k + 1], wbuf.at[k], sems.at[k]) for k in range(2)]
    for copy in copies:
        copy.start()
    tm, row, col = position()
    last_row, last_col = lax.axis_size("row") - 1, lax.axis_size("col") - 1
    (scale, offset), (scale_prev, offset_prev) = affine(parts_ref[...], unit, gain_ref[...], bias_ref[...], tm)
    width = scale.shape[-1]
    cell = lax.broadcasted_iota(jnp.int32, (4 * CELLS, width), 0)
    parity, r, slot = cell // CELLS, (cell // ACROSS) % ROWS, cell % ACROSS
    y, x = 2 * (r - 1) + parity // 2, 2 * (slot - 1) + parity % 2
    inside = ((y >= 0) | (row > 0)) & ((y < 4) | (row < last_row)) & ((x >= 0) | (col > 0)) & ((x < 20) | (col < last_col))
    n_now = out_ref.shape[0]
    n_prev = hid_ref.shape[0] - n_now
    area = 80
    for f in range(n_prev + n_now):
        a, b = (scale_prev, offset_prev) if f < n_prev else (scale, offset)
        valid = inside & (tm > 0) if f < n_prev else inside
        v = jnp.where(valid, silu(hid_ref[f].astype(F32) * a + b), 0.0)
        picked = jnp.dot(pick_ref[...], v.astype(BF16), preferred_element_type=F32).astype(BF16)
        for k in range(9):
            g_ref[f * area : (f + 1) * area, k * width : (k + 1) * width] = picked[k * area : (k + 1) * area]

    def part(a, w):
        slab = g_ref[a * area : (a + n_now) * area]
        return jnp.dot(slab, w.reshape(9 * width, width), preferred_element_type=F32)

    t_ref[...] = part(0, w_first_ref[...])

    @pl.when(tm >= 0)
    def _():
        for copy in copies:
            copy.wait()
        total = t_ref[...] + (part(1, wbuf[0]) + part(2, wbuf[1]))
        for f in range(n_now):
            hidden = jnp.dot(pick_ref[4 * area : 5 * area], hid_ref[n_prev + f], preferred_element_type=F32)
            decoded = total[f * area : (f + 1) * area] + b_ref[...] + hidden
            out_ref[f] = decoded.reshape(out_ref.shape[1:]).astype(BF16)


def shifted(value, spans, column):
    n_tm, n_col = lax.axis_size("tm"), lax.axis_size("col")
    route = [(t * n_col + c, (t + spans) % n_tm * n_col + column(c)) for t in range(n_tm) for c in range(n_col)]
    return lax.ppermute(value, ("tm", "col"), route)


def params(mib):
    return pltpu.CompilerParams(vmem_limit_bytes=mib * MIB)


def in_hbm(array):
    return pltpu.with_memory_space_constraint(array, pltpu.HBM)


VM = pl.BlockSpec(memory_space=pltpu.VMEM)
HBM = pl.BlockSpec(memory_space=pltpu.HBM)


def local(features, gain_low, bias_low, w_up, b_up, gain_high, bias_high, w_res, b_res):
    n_tm, n_row, n_col = (lax.axis_size(a) for a in EVERY)
    devices = n_tm * n_row * n_col
    frames, height, across, depth = features.shape
    width = w_up.shape[-1]
    low_unit = float(n_row * n_col * frames * height * across * (depth // GROUPS))
    high_unit = float(n_row * n_col * frames * 4 * height * across * (width // GROUPS))

    block = height * frames * SLOTS
    line = frames * SLOTS
    own, to_core, to_chip = pl.pallas_call(
        lay_out_kernel,
        out_shape=(
            jax.ShapeDtypeStruct((block, depth), BF16),
            jax.ShapeDtypeStruct((16, depth), BF16),
            jax.ShapeDtypeStruct((16, depth), BF16),
        ),
        in_specs=[VM],
        out_specs=(VM,) * 3,
        compiler_params=params(16),
        name="lay_out",
    )(features.transpose(0, 2, 1, 3))
    sums = pl.pallas_call(
        low_sums_kernel,
        out_shape=jax.ShapeDtypeStruct((devices, LANES), F32),
        in_specs=[VM],
        out_specs=VM,
        compiler_params=params(16),
        name="low_sums",
    )(own)
    prev_own = shifted(own, 1, lambda c: c)
    prev_chip = shifted(to_chip, 1, lambda c: (c - 1 + 2 * (c % 2)) % n_col)
    chip = shifted(to_chip, 0, lambda c: (c - 1 + 2 * (c % 2)) % n_col)
    prev_core = shifted(to_core, 1, lambda c: c ^ 1)
    core = shifted(to_core, 0, lambda c: c ^ 1)
    first = (core, chip, prev_core, prev_chip, prev_own)
    sums, first = lax.optimization_barrier((sums, first))
    core, chip, prev_core, prev_chip, prev_own = first
    low_parts = lax.all_to_all(sums, EVERY, 0, 0)
    gl, bl, bu = gain_low.reshape(1, -1), bias_low.reshape(1, -1), b_up.reshape(1, -1)
    gh, bh, br = gain_high.reshape(1, -1), bias_high.reshape(1, -1), b_res.reshape(1, -1)
    now, prev, up, down = pl.pallas_call(
        pack_kernel,
        out_shape=(jax.ShapeDtypeStruct((block, depth), BF16),) * 2
        + (jax.ShapeDtypeStruct((block // 16 * 12, depth), BF16),) * 2,
        in_specs=[VM] * 6,
        out_specs=(VM,) * 4,
        compiler_params=params(16),
        name="pack",
    )(own, core, chip, prev_own, prev_core, prev_chip)
    above = lax.ppermute(down, "row", [(i, (i + 1) % n_row) for i in range(n_row)])
    below = lax.ppermute(up, "row", [(i, (i - 1) % n_row) for i in range(n_row)])
    coef, w_near = pl.pallas_call(
        functools.partial(fetch_kernel, low_unit),
        out_shape=(
            jax.ShapeDtypeStruct((8, depth), F32),
            jax.ShapeDtypeStruct((3, 3, 3, depth, width), BF16),
        ),
        in_specs=[VM] + [HBM] * 4,
        out_specs=(VM,) * 2,
        scratch_shapes=[
            pltpu.VMEM((1, depth), F32),
            pltpu.VMEM((1, depth), F32),
            pltpu.VMEM((1, width), F32),
            pltpu.SemaphoreType.DMA((3,)),
            pltpu.SemaphoreType.DMA((3,)),
        ],
        compiler_params=params(16),
        name="fetch",
    )(low_parts, in_hbm(gl), in_hbm(bl), in_hbm(bu), in_hbm(w_up))
    hidden, high_sums, w_res_near = pl.pallas_call(
        up_kernel,
        out_shape=(
            jax.ShapeDtypeStruct((2 + frames, 4 * CELLS, width), BF16),
            jax.ShapeDtypeStruct((devices, LANES), F32),
            jax.ShapeDtypeStruct((3, 3, width, width), BF16),
        ),
        in_specs=[VM] * 6 + [HBM],
        out_specs=(VM,) * 3,
        scratch_shapes=[
            pltpu.VMEM((2 * frames, CELLS, depth), BF16),
            pltpu.VMEM((4, (2 + frames) * CELLS + 2 * SLOTS, width), F32),
            pltpu.SemaphoreType.DMA,
        ],
        compiler_params=params(20),
        name="up",
    )(coef, now, prev, above, below, w_near, in_hbm(w_res))
    high_parts = lax.all_to_all(high_sums, EVERY, 0, 0)

    area = 4 * height * across
    decoded = pl.pallas_call(
        functools.partial(res_kernel, high_unit),
        out_shape=jax.ShapeDtypeStruct((frames, 2 * across, 2 * height, width), BF16),
        in_specs=[VM] * 7 + [HBM],
        out_specs=VM,
        scratch_shapes=[
            pltpu.VMEM(((2 + frames) * area, 9 * width), BF16),
            pltpu.VMEM((frames * area, width), F32),
            pltpu.VMEM((2, 3, 3, width, width), BF16),
            pltpu.SemaphoreType.DMA((2,)),
        ],
        compiler_params=params(24),
        name="res",
    )(high_parts, gh, bh, br, hidden, jnp.asarray(gather_matrix(), BF16), w_res_near, in_hbm(w_res))
    return decoded.transpose(0, 2, 1, 3)


def solution(mesh):
    in_specs = (P("tm", "row", "col", None), P(), P(), P(), P(), P(), P(), P(), P())
    out_specs = P("tm", "row", "col", None)
    return jax.shard_map(local, mesh=mesh, in_specs=in_specs, out_specs=out_specs, check_vma=False)
```

time: 72.8 us -> 66.9 us (0.919)
  blocking collectives: 25.3 us -> 18.6 us
  waiting for transfers between devices: 5.15 us -> 11.7 us
  starting transfers between devices: 25.6 us -> 22.7 us
  Pallas kernels: 15.4 us -> 12.5 us
    all_to_all x1, waiting for transfers between devices: 0.45 us -> 9.55 us  [local(): low_parts = lax.all_to_all(sums, EVERY, 0, 0)]
    all_to_all x1, blocking collectives: 25.3 us -> 18.6 us  [local(): high_parts = lax.all_to_all(high_sums, EVERY, 0, 0)]
    ppermute x7, waiting for transfers between devices: 4.7 us -> 2.16 us  [the longest x5 2.16 us: shifted(): return lax.ppermute(value, ('tm', 'col'), route)]
    all_to_all x1, starting transfers between devices: 14.8 us -> 12.9 us  [local(): low_parts = lax.all_to_all(sums, EVERY, 0, 0)]
    pallas_call x2 -> x4, Pallas kernels: 10 us -> 8.27 us  [the longest x1 3.87 us: local(): pl.pallas_call(up_kernel, out_shape=(jax.ShapeDtypeStruct((2 + frames, 4...]
    ppermute x7, starting transfers between devices: 10.8 us -> 9.86 us  [the longest x5 7.09 us: shifted(): return lax.ppermute(value, ('tm', 'col'), route)]
  transfers between devices with their start and end apart: 8 -> 8, of which waited for: 3 -> 4; matrix products, arithmetic and copies ran while one was open for 0% -> 0% of each run, Pallas kernels for 1% -> 7%
where the time goes in v3:
time: 66.9 us; the launch traced here: 66.7 us
  starting transfers between devices  22.7 us (34%)
  blocking collectives  18.6 us (28%)
  Pallas kernels  12.5 us (19%)
  waiting for transfers between devices  11.7 us (17%)
  local copies, waits for them, and re-layouts  0.91 us (1%)
    all_to_all x1, blocking collectives, local(): high_parts = lax.all_to_all(high_sums, EVERY, 0, 0)  18.6 us
    all_to_all x1, starting transfers between devices, local(): low_parts = lax.all_to_all(sums, EVERY, 0, 0)  12.9 us
    all_to_all x1, waiting for transfers between devices, local(): low_parts = lax.all_to_all(sums, EVERY, 0, 0)  9.55 us
    ppermute x5, starting transfers between devices, shifted(): return lax.ppermute(value, ('tm', 'col'), route)  7.09 us
    pallas_call x1, Pallas kernels, local(): pl.pallas_call(up_kernel, out_shape=(jax.ShapeDtypeStruct((2 + frames, 4...  3.87 us
    pallas_call x1, Pallas kernels, local(): pl.pallas_call(functools.partial(res_kernel, high_unit), out_shape=jax.Sh...  3.74 us
    pallas_call x1, Pallas kernels, local(): pl.pallas_call(functools.partial(fetch_kernel, low_unit), out_shape=(jax....  3.19 us
    ppermute x5, waiting for transfers between devices, shifted(): return lax.ppermute(value, ('tm', 'col'), route)  2.16 us
  transfers between devices with their start and end apart: 8, of which 4 were waited for; matrix products, arithmetic and copies ran while one was open for 0% of the time, Pallas kernels for 7%

profile of v3, /device:TPU:1, one launch (start us, length us, event | category | flops | bytes accessed | tf_op | source)
XLA Modules:
  0.0 66.7 jit_solution(11055405371371545026)
XLA Ops:
  0.0 0.9 %copy-done.1 = bf16[4,2,10,512]{3,1,2,0:T(2,128)(2,1)S(1)} copy-done((bf16[4,2,10,512]{3,1,2,0:T(2,128)(2,1)S(1)}, bf16[4,2,10,512]{3,1,2,0:T(2,128)(2,1)}, u32[]{:S(2)}) %copy-start.1) | copy-done | bytes 81944
  0.9 0.2 lay_out.1
  1.1 2.2 %collective-permute-start.4 = (bf16[128,512]{1,0:T(8,128)(2,1)S(1)}, bf16[128,512]{1,0:T(8,128)(2,1)S(1)}, u32[]{:S(2)}, u32[]{:S(2)}) collective-permute-start(bf16[128,512]{1,0:T(8,128)(2,1)S(1)} %get-tuple-element.23.x_ref.own_ref), channel_id=1, source_target_pairs={{0,64},{1,65},{2,66},{3,67},{4,68},{5,69},{6,70},{7,71},{8,72},{9,... | collective-permute-start | bytes 393224 | tf_op jit(solution)/shard_map/ppermute | solution.py:287
  3.3 2.1 %collective-permute-start.2 = (bf16[16,512]{1,0:T(8,128)(2,1)S(1)}, bf16[16,512]{1,0:T(8,128)(2,1)S(1)}, u32[]{:S(2)}, u32[]{:S(2)}) collective-permute-start(bf16[16,512]{1,0:T(8,128)(2,1)S(1)} %get-tuple-element.24), channel_id=1, source_target_pairs={{0,65},{1,64},{2,67},{3,66},{4,69},{5,68},{6,71},{7,70},{8,73},{9,... | collective-permute-start | bytes 49160 | tf_op jit(solution)/shard_map/ppermute | solution.py:287
  5.4 0.0 collective-permute-start
  5.4 2.7 %collective-permute-start.3 = (bf16[16,512]{1,0:T(8,128)(2,1)S(1)}, bf16[16,512]{1,0:T(8,128)(2,1)S(1)}, u32[]{:S(2)}, u32[]{:S(2)}) collective-permute-start(bf16[16,512]{1,0:T(8,128)(2,1)S(1)} %get-tuple-element.25), channel_id=1, source_target_pairs={{0,79},{1,66},{2,65},{3,68},{4,67},{5,70},{6,69},{7,72},{8,71},{9,... | collective-permute-start | bytes 49160 | tf_op jit(solution)/shard_map/ppermute | solution.py:287
  8.2 0.0 collective-permute-start.1
  8.2 1.0 %low_sums.1 = f32[256,128]{1,0:T(8,128)} custom-call(bf16[128,512]{1,0:T(8,128)(2,1)S(1)} %get-tuple-element.23.x_ref.own_ref), custom_call_target="tpu_custom_call" | custom-call | tf_op jit(solution)/shard_map/low_sums/pallas_call | solution.py:324
  9.2 1.0 %collective-permute-done.2.prev_core_ref = bf16[16,512]{1,0:T(8,128)(2,1)S(1)} collective-permute-done((bf16[16,512]{1,0:T(8,128)(2,1)S(1)}, bf16[16,512]{1,0:T(8,128)(2,1)S(1)}, u32[]{:S(2)}, u32[]{:S(2)}) %collective-permute-start.2) | collective-permute-done | bytes 16416 | tf_op jit(solution)/shard_map/ppermute | solution.py:287
  10.2 0.0 collective-permute-done.core_ref
  10.2 0.5 collective-permute-done.3.prev_chip_ref
  10.7 0.6 collective-permute-done.1.chip_ref
  11.4 0.0 collective-permute-done.4.prev_own_ref
  11.4 12.9 %all-to-all-start = ((f32[256,1,128]{2,1,0:T(1,128)}), f32[256,1,128]{2,1,0:T(1,128)S(1)}, u32[]{:S(2)}, u32[]{:S(2)}) async-start(f32[256,1,128]{2,1,0:T(1,128)} %bitcast.2), calls=%async_computation | async-start | bytes 262144 | tf_op jit(solution)/shard_map/all_to_all | solution.py:340
  24.3 0.5 pack.1
  24.7 1.5 %collective-permute-start.5 = (bf16[96,512]{1,0:T(8,128)(2,1)S(1)}, bf16[96,512]{1,0:T(8,128)(2,1)S(1)}, u32[]{:S(2)}, u32[]{:S(2)}) collective-permute-start(bf16[96,512]{1,0:T(8,128)(2,1)S(1)} %get-tuple-element.35), channel_id=1, source_target_pairs={{0,16},{16,32},{32,48},{48,0},{1,17},{17,33},{33,49},{49,1},{2,18}... | collective-permute-start | bytes 294920 | tf_op jit(solution)/shard_map/ppermute | solution.py:352
  26.2 1.3 %collective-permute-start.6 = (bf16[96,512]{1,0:T(8,128)(2,1)S(1)}, bf16[96,512]{1,0:T(8,128)(2,1)S(1)}, u32[]{:S(2)}, u32[]{:S(2)}) collective-permute-start(bf16[96,512]{1,0:T(8,128)(2,1)S(1)} %get-tuple-element.36), channel_id=1, source_target_pairs={{0,48},{16,0},{32,16},{48,32},{1,49},{17,1},{33,17},{49,33},{2,50}... | collective-permute-start | bytes 294920 | tf_op jit(solution)/shard_map/ppermute | solution.py:353
  27.5 9.6 %all-to-all-done = f32[256,1,128]{2,1,0:T(1,128)S(1)} async-done(((f32[256,1,128]{2,1,0:T(1,128)}), f32[256,1,128]{2,1,0:T(1,128)S(1)}, u32[]{:S(2)}, u32[]{:S(2)}) %all-to-all-start) | async-done | bytes 131104 | tf_op jit(solution)/shard_map/all_to_all | solution.py:340
  37.1 3.2 %fetch.1 = (f32[8,512]{1,0:T(8,128)S(1)}, bf16[3,3,3,512,256]{4,3,2,1,0:T(8,128)(2,1)S(1)}) custom-call(f32[256,128]{1,0:T(8,128)S(1)} %bitcast.16, f32[1,512]{1,0:T(1,128)} %bitcast.23, f32[1,512]{1,0:T(1,128)} %bitcast.24, f32[1,256]{1,0:T(1,128)} %bitcast.25, bf16[3,3,3,512,256]{4,3,2,1,0:T(8,128)(2,1)} %w_ref.2), custom_call_target="tpu_custom_call" | custom-call | tf_op jit(solution)/shard_map/fetch/pallas_call | solution.py:354
  40.3 0.0 copy-start
  40.3 0.0 copy-start.2
  40.3 0.0 copy-start.3
  40.3 0.0 copy-start.4
  40.3 0.0 collective-permute-done.5.above_ref
  40.3 0.0 collective-permute-done.6.below_ref
  40.3 3.9 %up.1 = (bf16[6,192,256]{2,1,0:T(8,128)(2,1)S(1)}, f32[256,128]{1,0:T(8,128)S(1)}, bf16[3,3,256,256]{3,2,1,0:T(8,128)(2,1)S(1)}) custom-call(f32[8,512]{1,0:T(8,128)S(1)} %get-tuple-element.27.coef_ref, bf16[128,512]{1,0:T(8,128)(2,1)S(1)} %get-tuple-element.33.now_ref, bf16[128,512]{1,0:T(8,128)(2,1)S(1)} %get-tuple-element.34.prev_ref, ...), custom_call_target="tpu_custom_call" | custom-call | tf_op jit(solution)/shard_map/up/pallas_call | solution.py:372
  44.2 18.6 %all_to_all.22 = f32[256,1,128]{2,1,0:T(1,128)S(1)} all-to-all(f32[256,1,128]{2,1,0:T(1,128)S(1)} %bitcast.18), channel_id=1, replica_groups=mesh['tm'=4,'row'=4,'col'=16] {'tm','row','col'}, dimensions={0} | all-to-all | bytes 262144 | tf_op jit(solution)/shard_map/all_to_all | solution.py:389
  62.8 0.0 copy-done
  62.8 0.0 copy-done.2
  62.8 0.0 copy-done.3
  62.8 0.0 copy-done.4
  62.8 3.7 %res.1 = bf16[4,20,4,256]{3,2,1,0:T(4,128)(2,1)} custom-call(f32[256,128]{1,0:T(8,128)S(1)} %bitcast.17, f32[1,256]{1,0:T(1,128)S(1)} %bitcast.20, f32[1,256]{1,0:T(1,128)S(1)} %bitcast.21, f32[1,256]{1,0:T(1,128)S(1)} %bitcast.22, bf16[6,192,256]{2,1,0:T(8,128)(2,1)S(1)} %get-tuple-element.39.hid_ref, bf16[720,192]{1,0:T(8,128)(2,1)S(1)} %copy-done, ...), custom_call_target="tpu_custom_call" | custom-call | tf_op jit(solution)/shard_map/res/pallas_call | solution.py:392
  (1 shorter events, 0.0 us)
Async XLA Ops:
  0.0 0.9 %copy-start.1 = (bf16[4,2,10,512]{3,1,2,0:T(2,128)(2,1)S(1)}, bf16[4,2,10,512]{3,1,2,0:T(2,128)(2,1)}, u32[]{:S(2)}) copy-start(bf16[4,2,10,512]{3,1,2,0:T(2,128)(2,1)} %param.10) | copy-start | bytes 245764
  1.1 10.3 %collective-permute-start.4 = (bf16[128,512]{1,0:T(8,128)(2,1)S(1)}, bf16[128,512]{1,0:T(8,128)(2,1)S(1)}, u32[]{:S(2)}, u32[]{:S(2)}) collective-permute-start(bf16[128,512]{1,0:T(8,128)(2,1)S(1)} %get-tuple-element.23.x_ref.own_ref), channel_id=1, source_target_pairs={{0,64},{1,65},{2,66},{3,67},{4,68},{5,69},{6,70},{7,71},{8,72},{9,... | collective-permute-start | bytes 393224 | tf_op jit(solution)/shard_map/ppermute | solution.py:287
  3.3 6.9 %collective-permute-start.2 = (bf16[16,512]{1,0:T(8,128)(2,1)S(1)}, bf16[16,512]{1,0:T(8,128)(2,1)S(1)}, u32[]{:S(2)}, u32[]{:S(2)}) collective-permute-start(bf16[16,512]{1,0:T(8,128)(2,1)S(1)} %get-tuple-element.24), channel_id=1, source_target_pairs={{0,65},{1,64},{2,67},{3,66},{4,69},{5,68},{6,71},{7,70},{8,73},{9,... | collective-permute-start | bytes 49160 | tf_op jit(solution)/shard_map/ppermute | solution.py:287
  5.4 4.8 %collective-permute-start = (bf16[16,512]{1,0:T(8,128)(2,1)S(1)}, bf16[16,512]{1,0:T(8,128)(2,1)S(1)}, u32[]{:S(2)}, u32[]{:S(2)}) collective-permute-start(bf16[16,512]{1,0:T(8,128)(2,1)S(1)} %get-tuple-element.24), channel_id=1, source_target_pairs={{0,1},{1,0},{2,3},{3,2},{4,5},{5,4},{6,7},{7,6},{8,9},{9,8},{10,11... | collective-permute-start | bytes 49160 | tf_op jit(solution)/shard_map/ppermute | solution.py:287
  5.4 5.3 %collective-permute-start.3 = (bf16[16,512]{1,0:T(8,128)(2,1)S(1)}, bf16[16,512]{1,0:T(8,128)(2,1)S(1)}, u32[]{:S(2)}, u32[]{:S(2)}) collective-permute-start(bf16[16,512]{1,0:T(8,128)(2,1)S(1)} %get-tuple-element.25), channel_id=1, source_target_pairs={{0,79},{1,66},{2,65},{3,68},{4,67},{5,70},{6,69},{7,72},{8,71},{9,... | collective-permute-start | bytes 49160 | tf_op jit(solution)/shard_map/ppermute | solution.py:287
  8.2 3.2 %collective-permute-start.1 = (bf16[16,512]{1,0:T(8,128)(2,1)S(1)}, bf16[16,512]{1,0:T(8,128)(2,1)S(1)}, u32[]{:S(2)}, u32[]{:S(2)}) collective-permute-start(bf16[16,512]{1,0:T(8,128)(2,1)S(1)} %get-tuple-element.25), channel_id=1, source_target_pairs={{0,15},{1,2},{2,1},{3,4},{4,3},{5,6},{6,5},{7,8},{8,7},{9,10},{10,... | collective-permute-start | bytes 49160 | tf_op jit(solution)/shard_map/ppermute | solution.py:287
  11.4 25.7 %all-to-all-start = ((f32[256,1,128]{2,1,0:T(1,128)}), f32[256,1,128]{2,1,0:T(1,128)S(1)}, u32[]{:S(2)}, u32[]{:S(2)}) async-start(f32[256,1,128]{2,1,0:T(1,128)} %bitcast.2), calls=%async_computation | async-start | bytes 262144 | tf_op jit(solution)/shard_map/all_to_all | solution.py:340
  24.7 15.6 %collective-permute-start.5 = (bf16[96,512]{1,0:T(8,128)(2,1)S(1)}, bf16[96,512]{1,0:T(8,128)(2,1)S(1)}, u32[]{:S(2)}, u32[]{:S(2)}) collective-permute-start(bf16[96,512]{1,0:T(8,128)(2,1)S(1)} %get-tuple-element.35), channel_id=1, source_target_pairs={{0,16},{16,32},{32,48},{48,0},{1,17},{17,33},{33,49},{49,1},{2,18}... | collective-permute-start | bytes 294920 | tf_op jit(solution)/shard_map/ppermute | solution.py:352
  26.2 14.1 %collective-permute-start.6 = (bf16[96,512]{1,0:T(8,128)(2,1)S(1)}, bf16[96,512]{1,0:T(8,128)(2,1)S(1)}, u32[]{:S(2)}, u32[]{:S(2)}) collective-permute-start(bf16[96,512]{1,0:T(8,128)(2,1)S(1)} %get-tuple-element.36), channel_id=1, source_target_pairs={{0,48},{16,0},{32,16},{48,32},{1,49},{17,1},{33,17},{49,33},{2,50}... | collective-permute-start | bytes 294920 | tf_op jit(solution)/shard_map/ppermute | solution.py:353
  40.3 22.6 %copy-start = (bf16[720,192]{1,0:T(8,128)(2,1)S(1)}, bf16[720,192]{1,0:T(8,128)(2,1)}, u32[]{:S(2)}) copy-start(bf16[720,192]{1,0:T(8,128)(2,1)} %constant.2.clone.pick_ref) | copy-start | bytes 829444
  40.3 22.5 %copy-start.2 = (f32[256]{0:T(256)S(1)}, f32[256]{0:T(256)}, u32[]{:S(2)}) copy-start(f32[256]{0:T(256)} %param.15) | copy-start | bytes 3076
  40.3 22.5 %copy-start.3 = (f32[256]{0:T(256)S(1)}, f32[256]{0:T(256)}, u32[]{:S(2)}) copy-start(f32[256]{0:T(256)} %param.16) | copy-start | bytes 3076
  40.3 22.5 %copy-start.4 = (f32[256]{0:T(256)S(1)}, f32[256]{0:T(256)}, u32[]{:S(2)}) copy-start(f32[256]{0:T(256)} %param.18) | copy-start | bytes 3076

commit v4 on v3

--- a/solution.py
+++ b/solution.py
@@ -61,10 +61,19 @@
     return x / (1.0 + jnp.exp(-x))
 
 
-def low_sums_kernel(x_ref, sums_ref):
+def low_sums_kernel(x_ref, w_ref, sums_ref, w_out_ref, rows_ref, sems):
+    weights = pltpu.make_async_copy(w_ref.at[:, 0], w_out_ref, sems.at[0])
+    weights.start()
     x = x_ref[...].astype(F32)
     row = packed_sums(jnp.sum(x, axis=0, keepdims=True), jnp.sum(x * x, axis=0, keepdims=True))
-    sums_ref[...] = jnp.broadcast_to(row, sums_ref.shape)
+    rows_ref[...] = jnp.broadcast_to(row, rows_ref.shape)
+    out = pltpu.make_async_copy(rows_ref, sums_ref, sems.at[1])
+    out.start()
+
+    @pl.when(lax.axis_index("tm") >= 0)
+    def _():
+        weights.wait()
+        out.wait()
 
 
 def lay_out_kernel(x_ref, own_ref, to_core_ref, to_chip_ref):
@@ -120,14 +129,30 @@
             ref[j * sent.shape[0] : (j + 1) * sent.shape[0]] = sent
 
 
+def position():
+    tm, row, col = (lax.axis_index(a) for a in EVERY)
+    return tm, row, col
+
+
+def activated(piece, scale, offset, valid):
+    col, last_col = lax.axis_index("col"), lax.axis_size("col") - 1
+    slot = lax.broadcasted_iota(jnp.int32, piece.shape, 0) % SLOTS
+    inside = (slot >= jnp.where(col > 0, 0, 1)) & (slot <= jnp.where(col < last_col, 11, 10))
+    return jnp.where(inside & valid, silu(piece.astype(F32) * scale + offset), 0.0).astype(BF16)
+
+
 def fetch_kernel(
     unit,
     parts_ref,
+    now_ref,
+    prev_ref,
     gain_ref,
     bias_ref,
     b_ref,
     w_ref,
     coef_ref,
+    act_ref,
+    act_prev_ref,
     w_out_ref,
     gain_buf,
     bias_buf,
@@ -137,82 +162,94 @@
 ):
     pairs = ((gain_ref, gain_buf), (bias_ref, bias_buf), (b_ref, b_buf))
     few = [pltpu.make_async_copy(ref, buf, small.at[k]) for k, (ref, buf) in enumerate(pairs)]
-    weights = [pltpu.make_async_copy(w_ref.at[a], w_out_ref.at[a], sems.at[a]) for a in range(3)]
+    weights = [pltpu.make_async_copy(w_ref.at[:, b + 1], w_out_ref.at[b], sems.at[b]) for b in range(2)]
     for copy in few + weights:
         copy.start()
     for copy in few:
         copy.wait()
-    now, before = affine(parts_ref[...], unit, gain_buf[...], bias_buf[...], lax.axis_index("tm"))
+    tm = lax.axis_index("tm")
+    now, before = affine(parts_ref[...], unit, gain_buf[...], bias_buf[...], tm)
     for k, row in enumerate(now + before):
         coef_ref[k : k + 1] = row
     coef_ref[4:5, : b_buf.shape[1]] = b_buf[...]
-    for copy in weights:
-        copy.wait()
-
-
-def position():
-    tm, row, col = (lax.axis_index(a) for a in EVERY)
-    return tm, row, col
+    act_ref[...] = activated(now_ref[...], *now, tm >= 0)
+    act_prev_ref[...] = activated(prev_ref[...], *before, tm > 0)
+
+    @pl.when(tm >= 0)
+    def _():
+        for copy in weights:
+            copy.wait()
 
 
 def up_kernel(
-    coef_ref, now_ref, prev_ref, above_ref, below_ref, w_ref, w_res_ref, hid_ref, sums_ref, w_res_out_ref, x_ref, acc_ref, sem
+    coef_ref,
+    act_ref,
+    act_prev_ref,
+    above_ref,
+    below_ref,
+    w_first_ref,
+    w_rest_ref,
+    w_res_ref,
+    hid_ref,
+    sums_ref,
+    w_res_out_ref,
+    x_ref,
+    acc_ref,
+    sem,
 ):
     ahead = pltpu.make_async_copy(w_res_ref.at[0], w_res_out_ref, sem)
     ahead.start()
     tm, row, col = position()
-    last_row, last_col = lax.axis_size("row") - 1, lax.axis_size("col") - 1
+    last_row = lax.axis_size("row") - 1
     scale, offset, scale_prev, offset_prev = (coef_ref[k : k + 1] for k in range(4))
     depth = scale.shape[-1]
-    line = prev_ref.shape[0] // 2
+    line = act_ref.shape[0] // 2
     span = line // SLOTS
     sent = above_ref.shape[0] // 2
-    slot = lax.broadcasted_iota(jnp.int32, (line, depth), 0) % SLOTS
-    inside = (slot >= jnp.where(col > 0, 0, 1)) & (slot <= jnp.where(col < last_col, 11, 10))
     up, down = row > 0, row < last_row
 
     def active(piece, a, b, valid):
         v = piece[...]
-        if v.shape[0] < line:
-            v = jnp.dot(widen(v.shape[0]), v, preferred_element_type=F32)
-        v = silu(v.astype(F32) * a + b)
-        return jnp.where(inside & valid, v, 0.0).astype(BF16)
+        wide = jnp.dot(widen(v.shape[0]), v, preferred_element_type=F32)
+        return activated(wide, a, b, valid)
 
     take = narrow(ROWS * SLOTS)
 
     def place_span(block, part, at, a, b, valid):
         rows = [
             active(above_ref.at[part], a, b, valid & up),
-            active(block.at[:line], a, b, valid),
-            active(block.at[line:], a, b, valid),
+            block[:line],
+            block[line:],
             active(below_ref.at[part], a, b, valid & down),
         ]
         for f in range(span):
             frame = jnp.concatenate([r[f * SLOTS : (f + 1) * SLOTS] for r in rows], axis=0)
             x_ref[at + f] = jnp.dot(take, frame, preferred_element_type=F32).astype(BF16)
 
-    place_span(prev_ref, slice(sent, 2 * sent), 0, scale_prev, offset_prev, tm > 0)
-    place_span(now_ref, slice(0, sent), span, scale, offset, tm >= 0)
-    acc_ref[...] = jnp.zeros_like(acc_ref)
+    place_span(act_prev_ref, slice(sent, 2 * sent), 0, scale_prev, offset_prev, tm > 0)
+    place_span(act_ref, slice(0, sent), span, scale, offset, tm >= 0)
+    acc_ref[0:2, SLOTS : SLOTS + ACROSS] = jnp.zeros((2, ACROSS, acc_ref.shape[-1]), F32)
 
     frames = 2 * span - 2
     size = frames * CELLS
-    width = w_ref.shape[-1]
+    width = w_first_ref.shape[-1]
     up_bias = coef_ref[4:5, :width]
     for b in range(3):
 
         @pl.when(tm >= 0)
         def _():
+            taps = w_first_ref if b == 0 else w_rest_ref.at[b - 1]
             x = jnp.concatenate([x_ref[a : a + frames].reshape(size, depth) for a in range(3)], axis=1)
             z = [
-                jnp.dot(x, w_ref[:, b, e].reshape(3 * depth, width), preferred_element_type=F32) for e in range(3)
+                jnp.dot(x, taps[:, e].reshape(3 * depth, width), preferred_element_type=F32) for e in range(3)
             ]
             even = pltpu.roll(z[0], 1, 0) + (z[1] + z[2])
             odd = (z[0] + z[1]) + pltpu.roll(z[2], size - 1, 0)
             for p in range(2):
                 at = SLOTS + ACROSS * ((b == 0 and p == 0) - (b == 2 and p == 1))
                 for q, u in ((0, even), (1, odd)):
-                    acc_ref[2 * p + q, at : at + size] += u
+                    k, rows = 2 * p + q, slice(at, at + size)
+                    acc_ref[k, rows] = u if b == 0 else acc_ref[k, rows] + u
 
     total = jnp.zeros((1, width), F32)
     square = jnp.zeros((1, width), F32)
@@ -321,14 +358,15 @@
         compiler_params=params(16),
         name="lay_out",
     )(features.transpose(0, 2, 1, 3))
-    sums = pl.pallas_call(
+    sums, w_first = pl.pallas_call(
         low_sums_kernel,
-        out_shape=jax.ShapeDtypeStruct((devices, LANES), F32),
-        in_specs=[VM],
-        out_specs=VM,
+        out_shape=(jax.ShapeDtypeStruct((devices, LANES), F32), jax.ShapeDtypeStruct((3, 3, depth, width), BF16)),
+        in_specs=[VM, HBM],
+        out_specs=(HBM, VM),
+        scratch_shapes=[pltpu.VMEM((devices, LANES), F32), pltpu.SemaphoreType.DMA((2,))],
         compiler_params=params(16),
         name="low_sums",
-    )(own)
+    )(own, in_hbm(w_up))
     prev_own = shifted(own, 1, lambda c: c)
     prev_chip = shifted(to_chip, 1, lambda c: (c - 1 + 2 * (c % 2)) % n_col)
     chip = shifted(to_chip, 0, lambda c: (c - 1 + 2 * (c % 2)) % n_col)
@@ -351,24 +389,26 @@
     )(own, core, chip, prev_own, prev_core, prev_chip)
     above = lax.ppermute(down, "row", [(i, (i + 1) % n_row) for i in range(n_row)])
     below = lax.ppermute(up, "row", [(i, (i - 1) % n_row) for i in range(n_row)])
-    coef, w_near = pl.pallas_call(
+    coef, act, act_prev, w_rest = pl.pallas_call(
         functools.partial(fetch_kernel, low_unit),
         out_shape=(
             jax.ShapeDtypeStruct((8, depth), F32),
-            jax.ShapeDtypeStruct((3, 3, 3, depth, width), BF16),
+            jax.ShapeDtypeStruct((block, depth), BF16),
+            jax.ShapeDtypeStruct((block, depth), BF16),
+            jax.ShapeDtypeStruct((2, 3, 3, depth, width), BF16),
         ),
-        in_specs=[VM] + [HBM] * 4,
-        out_specs=(VM,) * 2,
+        in_specs=[VM] * 3 + [HBM] * 4,
+        out_specs=(VM,) * 4,
         scratch_shapes=[
             pltpu.VMEM((1, depth), F32),
             pltpu.VMEM((1, depth), F32),
             pltpu.VMEM((1, width), F32),
             pltpu.SemaphoreType.DMA((3,)),
-            pltpu.SemaphoreType.DMA((3,)),
+            pltpu.SemaphoreType.DMA((2,)),
         ],
         compiler_params=params(16),
         name="fetch",
-    )(low_parts, in_hbm(gl), in_hbm(bl), in_hbm(bu), in_hbm(w_up))
+    )(low_parts, now, prev, in_hbm(gl), in_hbm(bl), in_hbm(bu), in_hbm(w_up))
     hidden, high_sums, w_res_near = pl.pallas_call(
         up_kernel,
         out_shape=(
@@ -376,7 +416,7 @@
             jax.ShapeDtypeStruct((devices, LANES), F32),
             jax.ShapeDtypeStruct((3, 3, width, width), BF16),
         ),
-        in_specs=[VM] * 6 + [HBM],
+        in_specs=[VM] * 7 + [HBM],
         out_specs=(VM,) * 3,
         scratch_shapes=[
             pltpu.VMEM((2 * frames, CELLS, depth), BF16),
@@ -385,7 +425,7 @@
         ],
         compiler_params=params(20),
         name="up",
-    )(coef, now, prev, above, below, w_near, in_hbm(w_res))
+    )(coef, act, act_prev, above, below, w_first, w_rest, in_hbm(w_res))
     high_parts = lax.all_to_all(high_sums, EVERY, 0, 0)
 
     area = 4 * height * across

time: 66.9 us -> 66.2 us (0.990)
  waiting for transfers between devices: 11.7 us -> 11 us
    ppermute x5, waiting for transfers between devices: 2.16 us -> 1.42 us  [shifted(): return lax.ppermute(value, ('tm', 'col'), route)]
    pallas_call x1, Pallas kernels: 1.01 us -> 1.74 us  [local(): pl.pallas_call(low_sums_kernel, out_shape=(jax.ShapeDtypeStruct((devices,...]
    pallas_call x1, Pallas kernels: 3.19 us -> 2.47 us  [local(): pl.pallas_call(functools.partial(fetch_kernel, low_unit), out_shape=(jax....]
where the time goes in v4:
time: 66.2 us; the launch traced here: 66 us
  starting transfers between devices  22.8 us (34%)
  blocking collectives  18.6 us (28%)
  Pallas kernels  12.3 us (19%)
  waiting for transfers between devices  11 us (17%)
  local copies, waits for them, and re-layouts  0.91 us (1%)
    all_to_all x1, blocking collectives, local(): high_parts = lax.all_to_all(high_sums, EVERY, 0, 0)  18.6 us
    all_to_all x1, starting transfers between devices, local(): low_parts = lax.all_to_all(sums, EVERY, 0, 0)  13 us
    all_to_all x1, waiting for transfers between devices, local(): low_parts = lax.all_to_all(sums, EVERY, 0, 0)  9.55 us
    ppermute x5, starting transfers between devices, shifted(): return lax.ppermute(value, ('tm', 'col'), route)  7.09 us
    pallas_call x1, Pallas kernels, local(): pl.pallas_call(functools.partial(res_kernel, high_unit), out_shape=jax.Sh...  3.74 us
    pallas_call x1, Pallas kernels, local(): pl.pallas_call(up_kernel, out_shape=(jax.ShapeDtypeStruct((2 + frames, 4...  3.7 us
    pallas_call x1, Pallas kernels, local(): pl.pallas_call(functools.partial(fetch_kernel, low_unit), out_shape=(jax....  2.47 us
    pallas_call x1, Pallas kernels, local(): pl.pallas_call(low_sums_kernel, out_shape=(jax.ShapeDtypeStruct((devices,...  1.74 us
  transfers between devices with their start and end apart: 8, of which 4 were waited for; matrix products, arithmetic and copies ran while one was open for 0% of the time, Pallas kernels for 7%

profile of v4, /device:TPU:1, one launch (start us, length us, event | category | flops | bytes accessed | tf_op | source)
XLA Modules:
  0.0 66.0 jit_solution(14019940625479409095)
XLA Ops:
  0.0 0.9 %copy-done.1 = bf16[4,2,10,512]{3,1,2,0:T(2,128)(2,1)S(1)} copy-done((bf16[4,2,10,512]{3,1,2,0:T(2,128)(2,1)S(1)}, bf16[4,2,10,512]{3,1,2,0:T(2,128)(2,1)}, u32[]{:S(2)}) %copy-start.1) | copy-done | bytes 81944
  0.9 0.2 lay_out.1
  1.1 2.2 %collective-permute-start.4 = (bf16[128,512]{1,0:T(8,128)(2,1)S(1)}, bf16[128,512]{1,0:T(8,128)(2,1)S(1)}, u32[]{:S(2)}, u32[]{:S(2)}) collective-permute-start(bf16[128,512]{1,0:T(8,128)(2,1)S(1)} %get-tuple-element.27.x_ref.own_ref), channel_id=1, source_target_pairs={{0,64},{1,65},{2,66},{3,67},{4,68},{5,69},{6,70},{7,71},{8,72},{9,... | collective-permute-start | bytes 393224 | tf_op jit(solution)/shard_map/ppermute | solution.py:324
  3.3 2.1 %collective-permute-start.2 = (bf16[16,512]{1,0:T(8,128)(2,1)S(1)}, bf16[16,512]{1,0:T(8,128)(2,1)S(1)}, u32[]{:S(2)}, u32[]{:S(2)}) collective-permute-start(bf16[16,512]{1,0:T(8,128)(2,1)S(1)} %get-tuple-element.29), channel_id=1, source_target_pairs={{0,65},{1,64},{2,67},{3,66},{4,69},{5,68},{6,71},{7,70},{8,73},{9,... | collective-permute-start | bytes 49160 | tf_op jit(solution)/shard_map/ppermute | solution.py:324
  5.4 0.0 collective-permute-start
  5.4 2.7 %collective-permute-start.3 = (bf16[16,512]{1,0:T(8,128)(2,1)S(1)}, bf16[16,512]{1,0:T(8,128)(2,1)S(1)}, u32[]{:S(2)}, u32[]{:S(2)}) collective-permute-start(bf16[16,512]{1,0:T(8,128)(2,1)S(1)} %get-tuple-element.30), channel_id=1, source_target_pairs={{0,79},{1,66},{2,65},{3,68},{4,67},{5,70},{6,69},{7,72},{8,71},{9,... | collective-permute-start | bytes 49160 | tf_op jit(solution)/shard_map/ppermute | solution.py:324
  8.2 0.0 collective-permute-start.1
  8.2 1.7 %low_sums.1 = (f32[256,128]{1,0:T(8,128)}, bf16[3,3,512,256]{3,2,1,0:T(8,128)(2,1)S(1)}) custom-call(bf16[128,512]{1,0:T(8,128)(2,1)S(1)} %get-tuple-element.27.x_ref.own_ref, bf16[3,3,3,512,256]{4,3,2,1,0:T(8,128)(2,1)} %w_ref.4), custom_call_target="tpu_custom_call" | custom-call | tf_op jit(solution)/shard_map/low_sums/pallas_call | solution.py:361
  9.9 0.3 collective-permute-done.2.prev_core_ref
  10.2 0.0 collective-permute-done.core_ref
  10.2 0.5 collective-permute-done.3.prev_chip_ref
  10.7 0.6 collective-permute-done.1.chip_ref
  11.4 0.0 collective-permute-done.4.prev_own_ref
  11.4 13.0 %all-to-all-start = ((f32[256,1,128]{2,1,0:T(1,128)}), f32[256,1,128]{2,1,0:T(1,128)S(1)}, u32[]{:S(2)}, u32[]{:S(2)}) async-start(f32[256,1,128]{2,1,0:T(1,128)} %bitcast.2), calls=%async_computation | async-start | bytes 262144 | tf_op jit(solution)/shard_map/all_to_all | solution.py:378
  24.3 0.5 pack.1
  24.8 1.5 %collective-permute-start.5 = (bf16[96,512]{1,0:T(8,128)(2,1)S(1)}, bf16[96,512]{1,0:T(8,128)(2,1)S(1)}, u32[]{:S(2)}, u32[]{:S(2)}) collective-permute-start(bf16[96,512]{1,0:T(8,128)(2,1)S(1)} %get-tuple-element.42), channel_id=1, source_target_pairs={{0,16},{16,32},{32,48},{48,0},{1,17},{17,33},{33,49},{49,1},{2,18}... | collective-permute-start | bytes 294920 | tf_op jit(solution)/shard_map/ppermute | solution.py:390
  26.3 1.3 %collective-permute-start.6 = (bf16[96,512]{1,0:T(8,128)(2,1)S(1)}, bf16[96,512]{1,0:T(8,128)(2,1)S(1)}, u32[]{:S(2)}, u32[]{:S(2)}) collective-permute-start(bf16[96,512]{1,0:T(8,128)(2,1)S(1)} %get-tuple-element.43), channel_id=1, source_target_pairs={{0,48},{16,0},{32,16},{48,32},{1,49},{17,1},{33,17},{49,33},{2,50}... | collective-permute-start | bytes 294920 | tf_op jit(solution)/shard_map/ppermute | solution.py:391
  27.6 9.6 %all-to-all-done = f32[256,1,128]{2,1,0:T(1,128)S(1)} async-done(((f32[256,1,128]{2,1,0:T(1,128)}), f32[256,1,128]{2,1,0:T(1,128)S(1)}, u32[]{:S(2)}, u32[]{:S(2)}) %all-to-all-start) | async-done | bytes 131104 | tf_op jit(solution)/shard_map/all_to_all | solution.py:378
  37.2 2.5 %fetch.1 = (f32[8,512]{1,0:T(8,128)S(1)}, bf16[128,512]{1,0:T(8,128)(2,1)S(1)}, bf16[128,512]{1,0:T(8,128)(2,1)S(1)}, bf16[2,3,3,512,256]{4,3,2,1,0:T(8,128)(2,1)S(1)}) custom-call(f32[256,128]{1,0:T(8,128)S(1)} %bitcast.16, bf16[128,512]{1,0:T(8,128)(2,1)S(1)} %get-tuple-element.37.now_ref, bf16[128,512]{1,0:T(8,128)(2,1)S(1)} %get-tuple-element.38.prev_ref, ...), custom_call_target="tpu_custom_call" | custom-call | tf_op jit(solution)/shard_map/fetch/pallas_call | solution.py:392
  39.6 0.0 collective-permute-done.5.above_ref
  39.6 0.0 collective-permute-done.6.below_ref
  39.7 0.0 copy-start
  39.7 0.0 copy-start.2
  39.7 0.0 copy-start.3
  39.7 0.0 copy-start.4
  39.7 3.7 %up.1 = (bf16[6,192,256]{2,1,0:T(8,128)(2,1)S(1)}, f32[256,128]{1,0:T(8,128)S(1)}, bf16[3,3,256,256]{3,2,1,0:T(8,128)(2,1)S(1)}) custom-call(f32[8,512]{1,0:T(8,128)S(1)} %get-tuple-element.39.coef_ref, bf16[128,512]{1,0:T(8,128)(2,1)S(1)} %get-tuple-element.40.act_ref, bf16[128,512]{1,0:T(8,128)(2,1)S(1)} %get-tuple-element.41.act_prev_ref, ...), custom_call_target="tpu_custom_call" | custom-call | tf_op jit(solution)/shard_map/up/pallas_call | solution.py:412
  43.4 18.6 %all_to_all.22 = f32[256,1,128]{2,1,0:T(1,128)S(1)} all-to-all(f32[256,1,128]{2,1,0:T(1,128)S(1)} %bitcast.18), channel_id=1, replica_groups=mesh['tm'=4,'row'=4,'col'=16] {'tm','row','col'}, dimensions={0} | all-to-all | bytes 262144 | tf_op jit(solution)/shard_map/all_to_all | solution.py:429
  62.0 0.0 copy-done
  62.0 0.0 copy-done.2
  62.0 0.0 copy-done.3
  62.0 0.0 copy-done.4
  62.1 3.7 %res.1 = bf16[4,20,4,256]{3,2,1,0:T(4,128)(2,1)} custom-call(f32[256,128]{1,0:T(8,128)S(1)} %bitcast.17, f32[1,256]{1,0:T(1,128)S(1)} %bitcast.20, f32[1,256]{1,0:T(1,128)S(1)} %bitcast.21, f32[1,256]{1,0:T(1,128)S(1)} %bitcast.22, bf16[6,192,256]{2,1,0:T(8,128)(2,1)S(1)} %get-tuple-element.47.hid_ref, bf16[720,192]{1,0:T(8,128)(2,1)S(1)} %copy-done, ...), custom_call_target="tpu_custom_call" | custom-call | tf_op jit(solution)/shard_map/res/pallas_call | solution.py:432
  (1 shorter events, 0.0 us)
Async XLA Ops:
  0.0 0.9 %copy-start.1 = (bf16[4,2,10,512]{3,1,2,0:T(2,128)(2,1)S(1)}, bf16[4,2,10,512]{3,1,2,0:T(2,128)(2,1)}, u32[]{:S(2)}) copy-start(bf16[4,2,10,512]{3,1,2,0:T(2,128)(2,1)} %param.10) | copy-start | bytes 245764
  1.1 10.3 %collective-permute-start.4 = (bf16[128,512]{1,0:T(8,128)(2,1)S(1)}, bf16[128,512]{1,0:T(8,128)(2,1)S(1)}, u32[]{:S(2)}, u32[]{:S(2)}) collective-permute-start(bf16[128,512]{1,0:T(8,128)(2,1)S(1)} %get-tuple-element.27.x_ref.own_ref), channel_id=1, source_target_pairs={{0,64},{1,65},{2,66},{3,67},{4,68},{5,69},{6,70},{7,71},{8,72},{9,... | collective-permute-start | bytes 393224 | tf_op jit(solution)/shard_map/ppermute | solution.py:324
  3.3 6.9 %collective-permute-start.2 = (bf16[16,512]{1,0:T(8,128)(2,1)S(1)}, bf16[16,512]{1,0:T(8,128)(2,1)S(1)}, u32[]{:S(2)}, u32[]{:S(2)}) collective-permute-start(bf16[16,512]{1,0:T(8,128)(2,1)S(1)} %get-tuple-element.29), channel_id=1, source_target_pairs={{0,65},{1,64},{2,67},{3,66},{4,69},{5,68},{6,71},{7,70},{8,73},{9,... | collective-permute-start | bytes 49160 | tf_op jit(solution)/shard_map/ppermute | solution.py:324
  5.4 4.8 %collective-permute-start = (bf16[16,512]{1,0:T(8,128)(2,1)S(1)}, bf16[16,512]{1,0:T(8,128)(2,1)S(1)}, u32[]{:S(2)}, u32[]{:S(2)}) collective-permute-start(bf16[16,512]{1,0:T(8,128)(2,1)S(1)} %get-tuple-element.29), channel_id=1, source_target_pairs={{0,1},{1,0},{2,3},{3,2},{4,5},{5,4},{6,7},{7,6},{8,9},{9,8},{10,11... | collective-permute-start | bytes 49160 | tf_op jit(solution)/shard_map/ppermute | solution.py:324
  5.4 5.3 %collective-permute-start.3 = (bf16[16,512]{1,0:T(8,128)(2,1)S(1)}, bf16[16,512]{1,0:T(8,128)(2,1)S(1)}, u32[]{:S(2)}, u32[]{:S(2)}) collective-permute-start(bf16[16,512]{1,0:T(8,128)(2,1)S(1)} %get-tuple-element.30), channel_id=1, source_target_pairs={{0,79},{1,66},{2,65},{3,68},{4,67},{5,70},{6,69},{7,72},{8,71},{9,... | collective-permute-start | bytes 49160 | tf_op jit(solution)/shard_map/ppermute | solution.py:324
  8.2 3.2 %collective-permute-start.1 = (bf16[16,512]{1,0:T(8,128)(2,1)S(1)}, bf16[16,512]{1,0:T(8,128)(2,1)S(1)}, u32[]{:S(2)}, u32[]{:S(2)}) collective-permute-start(bf16[16,512]{1,0:T(8,128)(2,1)S(1)} %get-tuple-element.30), channel_id=1, source_target_pairs={{0,15},{1,2},{2,1},{3,4},{4,3},{5,6},{6,5},{7,8},{8,7},{9,10},{10,... | collective-permute-start | bytes 49160 | tf_op jit(solution)/shard_map/ppermute | solution.py:324
  11.4 25.8 %all-to-all-start = ((f32[256,1,128]{2,1,0:T(1,128)}), f32[256,1,128]{2,1,0:T(1,128)S(1)}, u32[]{:S(2)}, u32[]{:S(2)}) async-start(f32[256,1,128]{2,1,0:T(1,128)} %bitcast.2), calls=%async_computation | async-start | bytes 262144 | tf_op jit(solution)/shard_map/all_to_all | solution.py:378
  24.8 14.8 %collective-permute-start.5 = (bf16[96,512]{1,0:T(8,128)(2,1)S(1)}, bf16[96,512]{1,0:T(8,128)(2,1)S(1)}, u32[]{:S(2)}, u32[]{:S(2)}) collective-permute-start(bf16[96,512]{1,0:T(8,128)(2,1)S(1)} %get-tuple-element.42), channel_id=1, source_target_pairs={{0,16},{16,32},{32,48},{48,0},{1,17},{17,33},{33,49},{49,1},{2,18}... | collective-permute-start | bytes 294920 | tf_op jit(solution)/shard_map/ppermute | solution.py:390
  26.3 13.3 %collective-permute-start.6 = (bf16[96,512]{1,0:T(8,128)(2,1)S(1)}, bf16[96,512]{1,0:T(8,128)(2,1)S(1)}, u32[]{:S(2)}, u32[]{:S(2)}) collective-permute-start(bf16[96,512]{1,0:T(8,128)(2,1)S(1)} %get-tuple-element.43), channel_id=1, source_target_pairs={{0,48},{16,0},{32,16},{48,32},{1,49},{17,1},{33,17},{49,33},{2,50}... | collective-permute-start | bytes 294920 | tf_op jit(solution)/shard_map/ppermute | solution.py:391
  39.7 22.4 %copy-start = (bf16[720,192]{1,0:T(8,128)(2,1)S(1)}, bf16[720,192]{1,0:T(8,128)(2,1)}, u32[]{:S(2)}) copy-start(bf16[720,192]{1,0:T(8,128)(2,1)} %constant.2.clone.pick_ref) | copy-start | bytes 829444
  39.7 22.4 %copy-start.2 = (f32[256]{0:T(256)S(1)}, f32[256]{0:T(256)}, u32[]{:S(2)}) copy-start(f32[256]{0:T(256)} %param.15) | copy-start | bytes 3076
  39.7 22.4 %copy-start.3 = (f32[256]{0:T(256)S(1)}, f32[256]{0:T(256)}, u32[]{:S(2)}) copy-start(f32[256]{0:T(256)} %param.16) | copy-start | bytes 3076
  39.7 22.4 %copy-start.4 = (f32[256]{0:T(256)S(1)}, f32[256]{0:T(256)}, u32[]{:S(2)}) copy-start(f32[256]{0:T(256)} %param.18) | copy-start | bytes 3076

commit v5 on v4

--- a/solution.py
+++ b/solution.py
@@ -58,7 +58,13 @@
 
 
 def silu(x):
-    return x / (1.0 + jnp.exp(-x))
+    half = 0.5 * x
+    return half + half * jnp.tanh(half)
+
+
+def by_twelve(n):
+    quotient = lax.shift_right_logical(n * 171, 11)
+    return quotient, n - 12 * quotient
 
 
 def low_sums_kernel(x_ref, w_ref, sums_ref, w_out_ref, rows_ref, sems):
@@ -98,13 +104,15 @@
 def narrow(rows):
     shape = (rows // 16 * 12, rows)
     to, source = (lax.broadcasted_iota(jnp.int32, shape, d) for d in range(2))
-    return (source == to // 12 * SLOTS + to % 12).astype(BF16)
+    quotient, rest = by_twelve(to)
+    return (source == quotient * SLOTS + rest).astype(BF16)
 
 
 def widen(rows):
     shape = (rows // 12 * 16, rows)
     to, source = (lax.broadcasted_iota(jnp.int32, shape, d) for d in range(2))
-    return ((to % SLOTS < 12) & (source == to // SLOTS * 12 + to % SLOTS)).astype(BF16)
+    slot = to & (SLOTS - 1)
+    return ((slot < 12) & (source == lax.shift_right_logical(to, 4) * 12 + slot)).astype(BF16)
 
 
 def pack_kernel(own_ref, core_ref, chip_ref, prev_own_ref, prev_core_ref, prev_chip_ref, now_ref, prev_ref, up_ref, down_ref):
@@ -114,7 +122,7 @@
     to = lax.broadcasted_iota(jnp.int32, shape, 0)
     source = lax.broadcasted_iota(jnp.int32, shape, 1)
     core_slot = jnp.where(lax.axis_index("col") % 2 == 0, 11, 0)
-    slot, k = to % SLOTS, to // SLOTS
+    slot, k = to & (SLOTS - 1), lax.shift_right_logical(to, 4)
     hit = (((slot == core_slot) & (source == k)) | ((slot == 11 - core_slot) & (source == 16 + k))).astype(BF16)
     take = narrow(line)
     for j, (own, core, chip, out) in enumerate(
@@ -136,7 +144,7 @@
 
 def activated(piece, scale, offset, valid):
     col, last_col = lax.axis_index("col"), lax.axis_size("col") - 1
-    slot = lax.broadcasted_iota(jnp.int32, piece.shape, 0) % SLOTS
+    slot = lax.broadcasted_iota(jnp.int32, piece.shape, 0) & (SLOTS - 1)
     inside = (slot >= jnp.where(col > 0, 0, 1)) & (slot <= jnp.where(col < last_col, 11, 10))
     return jnp.where(inside & valid, silu(piece.astype(F32) * scale + offset), 0.0).astype(BF16)
 
@@ -253,8 +261,8 @@
 
     total = jnp.zeros((1, width), F32)
     square = jnp.zeros((1, width), F32)
-    cell = lax.broadcasted_iota(jnp.int32, (span * CELLS, width), 0) % CELLS
-    r, c = cell // ACROSS, cell % ACROSS
+    line_of, c = by_twelve(lax.broadcasted_iota(jnp.int32, (span * CELLS, width), 0))
+    r = line_of & (ROWS - 1)
     mine = (r >= 1) & (r <= 2) & (c >= 1) & (c <= 10)
     for k in range(4):
         hidden = (acc_ref[k, SLOTS : SLOTS + size] + up_bias).astype(BF16)
@@ -286,9 +294,9 @@
     last_row, last_col = lax.axis_size("row") - 1, lax.axis_size("col") - 1
     (scale, offset), (scale_prev, offset_prev) = affine(parts_ref[...], unit, gain_ref[...], bias_ref[...], tm)
     width = scale.shape[-1]
-    cell = lax.broadcasted_iota(jnp.int32, (4 * CELLS, width), 0)
-    parity, r, slot = cell // CELLS, (cell // ACROSS) % ROWS, cell % ACROSS
-    y, x = 2 * (r - 1) + parity // 2, 2 * (slot - 1) + parity % 2
+    line_of, slot = by_twelve(lax.broadcasted_iota(jnp.int32, (4 * CELLS, width), 0))
+    parity, r = lax.shift_right_logical(line_of, 2), line_of & (ROWS - 1)
+    y, x = 2 * (r - 1) + lax.shift_right_logical(parity, 1), 2 * (slot - 1) + (parity & 1)
     inside = ((y >= 0) | (row > 0)) & ((y < 4) | (row < last_row)) & ((x >= 0) | (col > 0)) & ((x < 20) | (col < last_col))
     n_now = out_ref.shape[0]
     n_prev = hid_ref.shape[0] - n_now
@@ -368,13 +376,13 @@
         name="low_sums",
     )(own, in_hbm(w_up))
     prev_own = shifted(own, 1, lambda c: c)
+    prev_core = shifted(to_core, 1, lambda c: c ^ 1)
+    core = shifted(to_core, 0, lambda c: c ^ 1)
     prev_chip = shifted(to_chip, 1, lambda c: (c - 1 + 2 * (c % 2)) % n_col)
     chip = shifted(to_chip, 0, lambda c: (c - 1 + 2 * (c % 2)) % n_col)
-    prev_core = shifted(to_core, 1, lambda c: c ^ 1)
-    core = shifted(to_core, 0, lambda c: c ^ 1)
-    first = (core, chip, prev_core, prev_chip, prev_own)
+    first = (chip, core, prev_chip, prev_core, prev_own)
     sums, first = lax.optimization_barrier((sums, first))
-    core, chip, prev_core, prev_chip, prev_own = first
+    chip, core, prev_chip, prev_core, prev_own = first
     low_parts = lax.all_to_all(sums, EVERY, 0, 0)
     gl, bl, bu = gain_low.reshape(1, -1), bias_low.reshape(1, -1), b_up.reshape(1, -1)
     gh, bh, br = gain_high.reshape(1, -1), bias_high.reshape(1, -1), b_res.reshape(1, -1)

time: 66.2 us -> 65.7 us (level)
  waiting for transfers between devices: 11 us -> 9.6 us
  starting transfers between devices: 22.8 us -> 24.2 us
    ppermute x5, starting transfers between devices: 7.09 us -> 10.1 us  [shifted(): return lax.ppermute(value, ('tm', 'col'), route)]
    all_to_all x1, starting transfers between devices: 13 us -> 11.4 us  [local(): low_parts = lax.all_to_all(sums, EVERY, 0, 0)]
    ppermute x5, waiting for transfers between devices: 1.42 us -> 0.04 us  [shifted(): return lax.ppermute(value, ('tm', 'col'), route)]
  transfers between devices with their start and end apart: 8 -> 8, of which waited for: 4 -> 1; matrix products, arithmetic and copies ran while one was open for 0% -> 0% of each run, Pallas kernels for 7% -> 7%
where the time goes in v5:
time: 65.7 us; the launch traced here: 65.5 us
  starting transfers between devices  24.2 us (37%)
  blocking collectives  18.6 us (28%)
  Pallas kernels  12.1 us (18%)
  waiting for transfers between devices  9.6 us (15%)
  local copies, waits for them, and re-layouts  0.91 us (1%)
    all_to_all x1, blocking collectives, local(): high_parts = lax.all_to_all(high_sums, EVERY, 0, 0)  18.6 us
    all_to_all x1, starting transfers between devices, local(): low_parts = lax.all_to_all(sums, EVERY, 0, 0)  11.4 us
    ppermute x5, starting transfers between devices, shifted(): return lax.ppermute(value, ('tm', 'col'), route)  10.1 us
    all_to_all x1, waiting for transfers between devices, local(): low_parts = lax.all_to_all(sums, EVERY, 0, 0)  9.55 us
    pallas_call x1, Pallas kernels, local(): pl.pallas_call(functools.partial(res_kernel, high_unit), out_shape=jax.Sh...  3.66 us
    pallas_call x1, Pallas kernels, local(): pl.pallas_call(up_kernel, out_shape=(jax.ShapeDtypeStruct((2 + frames, 4...  3.53 us
    pallas_call x1, Pallas kernels, local(): pl.pallas_call(functools.partial(fetch_kernel, low_unit), out_shape=(jax....  2.47 us
    pallas_call x1, Pallas kernels, local(): pl.pallas_call(low_sums_kernel, out_shape=(jax.ShapeDtypeStruct((devices,...  1.74 us
  transfers between devices with their start and end apart: 8, of which 1 were waited for; matrix products, arithmetic and copies ran while one was open for 0% of the time, Pallas kernels for 7%

profile of v5, /device:TPU:1, one launch (start us, length us, event | category | flops | bytes accessed | tf_op | source)
XLA Modules:
  0.0 65.5 jit_solution(11063042042445646120)
XLA Ops:
  0.0 0.9 %copy-done.1 = bf16[4,2,10,512]{3,1,2,0:T(2,128)(2,1)S(1)} copy-done((bf16[4,2,10,512]{3,1,2,0:T(2,128)(2,1)S(1)}, bf16[4,2,10,512]{3,1,2,0:T(2,128)(2,1)}, u32[]{:S(2)}) %copy-start.1) | copy-done | bytes 81944
  0.9 0.2 lay_out.1
  1.1 2.2 %collective-permute-start.4 = (bf16[128,512]{1,0:T(8,128)(2,1)S(1)}, bf16[128,512]{1,0:T(8,128)(2,1)S(1)}, u32[]{:S(2)}, u32[]{:S(2)}) collective-permute-start(bf16[128,512]{1,0:T(8,128)(2,1)S(1)} %get-tuple-element.27.x_ref.own_ref), channel_id=1, source_target_pairs={{0,64},{1,65},{2,66},{3,67},{4,68},{5,69},{6,70},{7,71},{8,72},{9,... | collective-permute-start | bytes 393224 | tf_op jit(solution)/shard_map/ppermute | solution.py:332
  3.3 3.5 %collective-permute-start.2 = (bf16[16,512]{1,0:T(8,128)(2,1)S(1)}, bf16[16,512]{1,0:T(8,128)(2,1)S(1)}, u32[]{:S(2)}, u32[]{:S(2)}) collective-permute-start(bf16[16,512]{1,0:T(8,128)(2,1)S(1)} %get-tuple-element.29), channel_id=1, source_target_pairs={{0,79},{1,66},{2,65},{3,68},{4,67},{5,70},{6,69},{7,72},{8,71},{9,... | collective-permute-start | bytes 49160 | tf_op jit(solution)/shard_map/ppermute | solution.py:332
  6.8 0.0 collective-permute-start
  6.8 4.4 %collective-permute-start.3 = (bf16[16,512]{1,0:T(8,128)(2,1)S(1)}, bf16[16,512]{1,0:T(8,128)(2,1)S(1)}, u32[]{:S(2)}, u32[]{:S(2)}) collective-permute-start(bf16[16,512]{1,0:T(8,128)(2,1)S(1)} %get-tuple-element.30), channel_id=1, source_target_pairs={{0,65},{1,64},{2,67},{3,66},{4,69},{5,68},{6,71},{7,70},{8,73},{9,... | collective-permute-start | bytes 49160 | tf_op jit(solution)/shard_map/ppermute | solution.py:332
  11.2 0.0 collective-permute-start.1
  11.2 1.7 %low_sums.1 = (f32[256,128]{1,0:T(8,128)}, bf16[3,3,512,256]{3,2,1,0:T(8,128)(2,1)S(1)}) custom-call(bf16[128,512]{1,0:T(8,128)(2,1)S(1)} %get-tuple-element.27.x_ref.own_ref, bf16[3,3,3,512,256]{4,3,2,1,0:T(8,128)(2,1)} %w_ref.4), custom_call_target="tpu_custom_call" | custom-call | tf_op jit(solution)/shard_map/low_sums/pallas_call | solution.py:369
  12.9 0.0 collective-permute-done.2.prev_chip_ref
  12.9 0.0 collective-permute-done.chip_ref
  12.9 0.0 collective-permute-done.3.prev_core_ref
  13.0 0.0 collective-permute-done.1.core_ref
  13.0 0.0 collective-permute-done.4.prev_own_ref
  13.0 11.4 %all-to-all-start = ((f32[256,1,128]{2,1,0:T(1,128)}), f32[256,1,128]{2,1,0:T(1,128)S(1)}, u32[]{:S(2)}, u32[]{:S(2)}) async-start(f32[256,1,128]{2,1,0:T(1,128)} %bitcast.2), calls=%async_computation | async-start | bytes 262144 | tf_op jit(solution)/shard_map/all_to_all | solution.py:386
  24.3 0.5 pack.1
  24.8 1.5 %collective-permute-start.5 = (bf16[96,512]{1,0:T(8,128)(2,1)S(1)}, bf16[96,512]{1,0:T(8,128)(2,1)S(1)}, u32[]{:S(2)}, u32[]{:S(2)}) collective-permute-start(bf16[96,512]{1,0:T(8,128)(2,1)S(1)} %get-tuple-element.42), channel_id=1, source_target_pairs={{0,16},{16,32},{32,48},{48,0},{1,17},{17,33},{33,49},{49,1},{2,18}... | collective-permute-start | bytes 294920 | tf_op jit(solution)/shard_map/ppermute | solution.py:398
  26.3 1.3 %collective-permute-start.6 = (bf16[96,512]{1,0:T(8,128)(2,1)S(1)}, bf16[96,512]{1,0:T(8,128)(2,1)S(1)}, u32[]{:S(2)}, u32[]{:S(2)}) collective-permute-start(bf16[96,512]{1,0:T(8,128)(2,1)S(1)} %get-tuple-element.43), channel_id=1, source_target_pairs={{0,48},{16,0},{32,16},{48,32},{1,49},{17,1},{33,17},{49,33},{2,50}... | collective-permute-start | bytes 294920 | tf_op jit(solution)/shard_map/ppermute | solution.py:399
  27.6 9.6 %all-to-all-done = f32[256,1,128]{2,1,0:T(1,128)S(1)} async-done(((f32[256,1,128]{2,1,0:T(1,128)}), f32[256,1,128]{2,1,0:T(1,128)S(1)}, u32[]{:S(2)}, u32[]{:S(2)}) %all-to-all-start) | async-done | bytes 131104 | tf_op jit(solution)/shard_map/all_to_all | solution.py:386
  37.2 2.5 %fetch.1 = (f32[8,512]{1,0:T(8,128)S(1)}, bf16[128,512]{1,0:T(8,128)(2,1)S(1)}, bf16[128,512]{1,0:T(8,128)(2,1)S(1)}, bf16[2,3,3,512,256]{4,3,2,1,0:T(8,128)(2,1)S(1)}) custom-call(f32[256,128]{1,0:T(8,128)S(1)} %bitcast.16, bf16[128,512]{1,0:T(8,128)(2,1)S(1)} %get-tuple-element.37.now_ref, bf16[128,512]{1,0:T(8,128)(2,1)S(1)} %get-tuple-element.38.prev_ref, ...), custom_call_target="tpu_custom_call" | custom-call | tf_op jit(solution)/shard_map/fetch/pallas_call | solution.py:400
  39.6 0.0 collective-permute-done.5.above_ref
  39.6 0.0 collective-permute-done.6.below_ref
  39.7 0.0 copy-start
  39.7 0.0 copy-start.2
  39.7 0.0 copy-start.3
  39.7 0.0 copy-start.4
  39.7 3.5 %up.1 = (bf16[6,192,256]{2,1,0:T(8,128)(2,1)S(1)}, f32[256,128]{1,0:T(8,128)S(1)}, bf16[3,3,256,256]{3,2,1,0:T(8,128)(2,1)S(1)}) custom-call(f32[8,512]{1,0:T(8,128)S(1)} %get-tuple-element.39.coef_ref, bf16[128,512]{1,0:T(8,128)(2,1)S(1)} %get-tuple-element.40.act_ref, bf16[128,512]{1,0:T(8,128)(2,1)S(1)} %get-tuple-element.41.act_prev_ref, ...), custom_call_target="tpu_custom_call" | custom-call | tf_op jit(solution)/shard_map/up/pallas_call | solution.py:420
  43.2 18.6 %all_to_all.22 = f32[256,1,128]{2,1,0:T(1,128)S(1)} all-to-all(f32[256,1,128]{2,1,0:T(1,128)S(1)} %bitcast.18), channel_id=1, replica_groups=mesh['tm'=4,'row'=4,'col'=16] {'tm','row','col'}, dimensions={0} | all-to-all | bytes 262144 | tf_op jit(solution)/shard_map/all_to_all | solution.py:437
  61.9 0.0 copy-done
  61.9 0.0 copy-done.2
  61.9 0.0 copy-done.3
  61.9 0.0 copy-done.4
  61.9 3.7 %res.1 = bf16[4,20,4,256]{3,2,1,0:T(4,128)(2,1)} custom-call(f32[256,128]{1,0:T(8,128)S(1)} %bitcast.17, f32[1,256]{1,0:T(1,128)S(1)} %bitcast.20, f32[1,256]{1,0:T(1,128)S(1)} %bitcast.21, f32[1,256]{1,0:T(1,128)S(1)} %bitcast.22, bf16[6,192,256]{2,1,0:T(8,128)(2,1)S(1)} %get-tuple-element.47.hid_ref, bf16[720,192]{1,0:T(8,128)(2,1)S(1)} %copy-done, ...), custom_call_target="tpu_custom_call" | custom-call | tf_op jit(solution)/shard_map/res/pallas_call | solution.py:440
  (1 shorter events, 0.0 us)
Async XLA Ops:
  0.0 0.9 %copy-start.1 = (bf16[4,2,10,512]{3,1,2,0:T(2,128)(2,1)S(1)}, bf16[4,2,10,512]{3,1,2,0:T(2,128)(2,1)}, u32[]{:S(2)}) copy-start(bf16[4,2,10,512]{3,1,2,0:T(2,128)(2,1)} %param.10) | copy-start | bytes 245764
  1.1 11.9 %collective-permute-start.4 = (bf16[128,512]{1,0:T(8,128)(2,1)S(1)}, bf16[128,512]{1,0:T(8,128)(2,1)S(1)}, u32[]{:S(2)}, u32[]{:S(2)}) collective-permute-start(bf16[128,512]{1,0:T(8,128)(2,1)S(1)} %get-tuple-element.27.x_ref.own_ref), channel_id=1, source_target_pairs={{0,64},{1,65},{2,66},{3,67},{4,68},{5,69},{6,70},{7,71},{8,72},{9,... | collective-permute-start | bytes 393224 | tf_op jit(solution)/shard_map/ppermute | solution.py:332
  3.3 9.6 %collective-permute-start.2 = (bf16[16,512]{1,0:T(8,128)(2,1)S(1)}, bf16[16,512]{1,0:T(8,128)(2,1)S(1)}, u32[]{:S(2)}, u32[]{:S(2)}) collective-permute-start(bf16[16,512]{1,0:T(8,128)(2,1)S(1)} %get-tuple-element.29), channel_id=1, source_target_pairs={{0,79},{1,66},{2,65},{3,68},{4,67},{5,70},{6,69},{7,72},{8,71},{9,... | collective-permute-start | bytes 49160 | tf_op jit(solution)/shard_map/ppermute | solution.py:332
  6.8 6.1 %collective-permute-start = (bf16[16,512]{1,0:T(8,128)(2,1)S(1)}, bf16[16,512]{1,0:T(8,128)(2,1)S(1)}, u32[]{:S(2)}, u32[]{:S(2)}) collective-permute-start(bf16[16,512]{1,0:T(8,128)(2,1)S(1)} %get-tuple-element.29), channel_id=1, source_target_pairs={{0,15},{1,2},{2,1},{3,4},{4,3},{5,6},{6,5},{7,8},{8,7},{9,10},{10,... | collective-permute-start | bytes 49160 | tf_op jit(solution)/shard_map/ppermute | solution.py:332
  6.8 6.2 %collective-permute-start.3 = (bf16[16,512]{1,0:T(8,128)(2,1)S(1)}, bf16[16,512]{1,0:T(8,128)(2,1)S(1)}, u32[]{:S(2)}, u32[]{:S(2)}) collective-permute-start(bf16[16,512]{1,0:T(8,128)(2,1)S(1)} %get-tuple-element.30), channel_id=1, source_target_pairs={{0,65},{1,64},{2,67},{3,66},{4,69},{5,68},{6,71},{7,70},{8,73},{9,... | collective-permute-start | bytes 49160 | tf_op jit(solution)/shard_map/ppermute | solution.py:332
  11.2 1.8 %collective-permute-start.1 = (bf16[16,512]{1,0:T(8,128)(2,1)S(1)}, bf16[16,512]{1,0:T(8,128)(2,1)S(1)}, u32[]{:S(2)}, u32[]{:S(2)}) collective-permute-start(bf16[16,512]{1,0:T(8,128)(2,1)S(1)} %get-tuple-element.30), channel_id=1, source_target_pairs={{0,1},{1,0},{2,3},{3,2},{4,5},{5,4},{6,7},{7,6},{8,9},{9,8},{10,11... | collective-permute-start | bytes 49160 | tf_op jit(solution)/shard_map/ppermute | solution.py:332
  13.0 24.2 %all-to-all-start = ((f32[256,1,128]{2,1,0:T(1,128)}), f32[256,1,128]{2,1,0:T(1,128)S(1)}, u32[]{:S(2)}, u32[]{:S(2)}) async-start(f32[256,1,128]{2,1,0:T(1,128)} %bitcast.2), calls=%async_computation | async-start | bytes 262144 | tf_op jit(solution)/shard_map/all_to_all | solution.py:386
  24.8 14.8 %collective-permute-start.5 = (bf16[96,512]{1,0:T(8,128)(2,1)S(1)}, bf16[96,512]{1,0:T(8,128)(2,1)S(1)}, u32[]{:S(2)}, u32[]{:S(2)}) collective-permute-start(bf16[96,512]{1,0:T(8,128)(2,1)S(1)} %get-tuple-element.42), channel_id=1, source_target_pairs={{0,16},{16,32},{32,48},{48,0},{1,17},{17,33},{33,49},{49,1},{2,18}... | collective-permute-start | bytes 294920 | tf_op jit(solution)/shard_map/ppermute | solution.py:398
  26.3 13.3 %collective-permute-start.6 = (bf16[96,512]{1,0:T(8,128)(2,1)S(1)}, bf16[96,512]{1,0:T(8,128)(2,1)S(1)}, u32[]{:S(2)}, u32[]{:S(2)}) collective-permute-start(bf16[96,512]{1,0:T(8,128)(2,1)S(1)} %get-tuple-element.43), channel_id=1, source_target_pairs={{0,48},{16,0},{32,16},{48,32},{1,49},{17,1},{33,17},{49,33},{2,50}... | collective-permute-start | bytes 294920 | tf_op jit(solution)/shard_map/ppermute | solution.py:399
  39.7 22.2 %copy-start = (bf16[720,192]{1,0:T(8,128)(2,1)S(1)}, bf16[720,192]{1,0:T(8,128)(2,1)}, u32[]{:S(2)}) copy-start(bf16[720,192]{1,0:T(8,128)(2,1)} %constant.2.clone.pick_ref) | copy-start | bytes 829444
  39.7 22.2 %copy-start.2 = (f32[256]{0:T(256)S(1)}, f32[256]{0:T(256)}, u32[]{:S(2)}) copy-start(f32[256]{0:T(256)} %param.15) | copy-start | bytes 3076
  39.7 22.2 %copy-start.3 = (f32[256]{0:T(256)S(1)}, f32[256]{0:T(256)}, u32[]{:S(2)}) copy-start(f32[256]{0:T(256)} %param.16) | copy-start | bytes 3076
  39.7 22.2 %copy-start.4 = (f32[256]{0:T(256)S(1)}, f32[256]{0:T(256)}, u32[]{:S(2)}) copy-start(f32[256]{0:T(256)} %param.18) | copy-start | bytes 3076

commit v6 on v5

--- a/solution.py
+++ b/solution.py
@@ -108,13 +108,6 @@
     return (source == quotient * SLOTS + rest).astype(BF16)
 
 
-def widen(rows):
-    shape = (rows // 12 * 16, rows)
-    to, source = (lax.broadcasted_iota(jnp.int32, shape, d) for d in range(2))
-    slot = to & (SLOTS - 1)
-    return ((slot < 12) & (source == lax.shift_right_logical(to, 4) * 12 + slot)).astype(BF16)
-
-
 def pack_kernel(own_ref, core_ref, chip_ref, prev_own_ref, prev_core_ref, prev_chip_ref, now_ref, prev_ref, up_ref, down_ref):
     rows = own_ref.shape[0]
     line = rows // 2
@@ -124,7 +117,6 @@
     core_slot = jnp.where(lax.axis_index("col") % 2 == 0, 11, 0)
     slot, k = to & (SLOTS - 1), lax.shift_right_logical(to, 4)
     hit = (((slot == core_slot) & (source == k)) | ((slot == 11 - core_slot) & (source == 16 + k))).astype(BF16)
-    take = narrow(line)
     for j, (own, core, chip, out) in enumerate(
         ((own_ref, core_ref, chip_ref, now_ref), (prev_own_ref, prev_core_ref, prev_chip_ref, prev_ref))
     ):
@@ -133,8 +125,7 @@
         block = (own[...].astype(F32) + moved).astype(BF16)
         out[...] = block
         for ref, half in ((up_ref, block[:line]), (down_ref, block[line:])):
-            sent = jnp.dot(take, half, preferred_element_type=F32).astype(BF16)
-            ref[j * sent.shape[0] : (j + 1) * sent.shape[0]] = sent
+            ref[j * line : (j + 1) * line] = half
 
 
 def position():
@@ -217,9 +208,7 @@
     up, down = row > 0, row < last_row
 
     def active(piece, a, b, valid):
-        v = piece[...]
-        wide = jnp.dot(widen(v.shape[0]), v, preferred_element_type=F32)
-        return activated(wide, a, b, valid)
+        return activated(piece[...], a, b, valid)
 
     take = narrow(ROWS * SLOTS)
 
@@ -388,8 +377,7 @@
     gh, bh, br = gain_high.reshape(1, -1), bias_high.reshape(1, -1), b_res.reshape(1, -1)
     now, prev, up, down = pl.pallas_call(
         pack_kernel,
-        out_shape=(jax.ShapeDtypeStruct((block, depth), BF16),) * 2
-        + (jax.ShapeDtypeStruct((block // 16 * 12, depth), BF16),) * 2,
+        out_shape=(jax.ShapeDtypeStruct((block, depth), BF16),) * 4,
         in_specs=[VM] * 6,
         out_specs=(VM,) * 4,
         compiler_params=params(16),

time: 65.7 us -> 65.4 us (level)
  no operation moved by 1% of the time
where the time goes in v6:
time: 65.4 us; the launch traced here: 65.2 us
  starting transfers between devices  24.2 us (37%)
  blocking collectives  18.6 us (28%)
  Pallas kernels  11.5 us (18%)
  waiting for transfers between devices  9.87 us (15%)
  local copies, waits for them, and re-layouts  0.91 us (1%)
    all_to_all x1, blocking collectives, local(): high_parts = lax.all_to_all(high_sums, EVERY, 0, 0)  18.6 us
    all_to_all x1, starting transfers between devices, local(): low_parts = lax.all_to_all(sums, EVERY, 0, 0)  11.4 us
    ppermute x5, starting transfers between devices, shifted(): return lax.ppermute(value, ('tm', 'col'), route)  10.1 us
    all_to_all x1, waiting for transfers between devices, local(): low_parts = lax.all_to_all(sums, EVERY, 0, 0)  9.82 us
    pallas_call x1, Pallas kernels, local(): pl.pallas_call(functools.partial(res_kernel, high_unit), out_shape=jax.Sh...  3.66 us
    pallas_call x1, Pallas kernels, local(): pl.pallas_call(up_kernel, out_shape=(jax.ShapeDtypeStruct((2 + frames, 4...  3.23 us
    pallas_call x1, Pallas kernels, local(): pl.pallas_call(functools.partial(fetch_kernel, low_unit), out_shape=(jax....  2.47 us
    pallas_call x1, Pallas kernels, local(): pl.pallas_call(low_sums_kernel, out_shape=(jax.ShapeDtypeStruct((devices,...  1.74 us
  transfers between devices with their start and end apart: 8, of which 1 were waited for; matrix products, arithmetic and copies ran while one was open for 0% of the time, Pallas kernels for 7%

profile of v6, /device:TPU:1, one launch (start us, length us, event | category | flops | bytes accessed | tf_op | source)
XLA Modules:
  0.0 65.2 jit_solution(12320789126493640511)
XLA Ops:
  0.0 0.9 %copy-done.1 = bf16[4,2,10,512]{3,1,2,0:T(2,128)(2,1)S(1)} copy-done((bf16[4,2,10,512]{3,1,2,0:T(2,128)(2,1)S(1)}, bf16[4,2,10,512]{3,1,2,0:T(2,128)(2,1)}, u32[]{:S(2)}) %copy-start.1) | copy-done | bytes 81944
  0.9 0.2 lay_out.1
  1.1 2.2 %collective-permute-start.4 = (bf16[128,512]{1,0:T(8,128)(2,1)S(1)}, bf16[128,512]{1,0:T(8,128)(2,1)S(1)}, u32[]{:S(2)}, u32[]{:S(2)}) collective-permute-start(bf16[128,512]{1,0:T(8,128)(2,1)S(1)} %get-tuple-element.27.x_ref.own_ref), channel_id=1, source_target_pairs={{0,64},{1,65},{2,66},{3,67},{4,68},{5,69},{6,70},{7,71},{8,72},{9,... | collective-permute-start | bytes 393224 | tf_op jit(solution)/shard_map/ppermute | solution.py:321
  3.3 3.5 %collective-permute-start.2 = (bf16[16,512]{1,0:T(8,128)(2,1)S(1)}, bf16[16,512]{1,0:T(8,128)(2,1)S(1)}, u32[]{:S(2)}, u32[]{:S(2)}) collective-permute-start(bf16[16,512]{1,0:T(8,128)(2,1)S(1)} %get-tuple-element.29), channel_id=1, source_target_pairs={{0,79},{1,66},{2,65},{3,68},{4,67},{5,70},{6,69},{7,72},{8,71},{9,... | collective-permute-start | bytes 49160 | tf_op jit(solution)/shard_map/ppermute | solution.py:321
  6.8 0.0 collective-permute-start
  6.8 4.4 %collective-permute-start.3 = (bf16[16,512]{1,0:T(8,128)(2,1)S(1)}, bf16[16,512]{1,0:T(8,128)(2,1)S(1)}, u32[]{:S(2)}, u32[]{:S(2)}) collective-permute-start(bf16[16,512]{1,0:T(8,128)(2,1)S(1)} %get-tuple-element.30), channel_id=1, source_target_pairs={{0,65},{1,64},{2,67},{3,66},{4,69},{5,68},{6,71},{7,70},{8,73},{9,... | collective-permute-start | bytes 49160 | tf_op jit(solution)/shard_map/ppermute | solution.py:321
  11.2 0.0 collective-permute-start.1
  11.2 1.7 %low_sums.1 = (f32[256,128]{1,0:T(8,128)}, bf16[3,3,512,256]{3,2,1,0:T(8,128)(2,1)S(1)}) custom-call(bf16[128,512]{1,0:T(8,128)(2,1)S(1)} %get-tuple-element.27.x_ref.own_ref, bf16[3,3,3,512,256]{4,3,2,1,0:T(8,128)(2,1)} %w_ref.4), custom_call_target="tpu_custom_call" | custom-call | tf_op jit(solution)/shard_map/low_sums/pallas_call | solution.py:358
  12.9 0.0 collective-permute-done.2.prev_chip_ref
  12.9 0.0 collective-permute-done.chip_ref
  12.9 0.0 collective-permute-done.3.prev_core_ref
  13.0 0.0 collective-permute-done.1.core_ref
  13.0 0.0 collective-permute-done.4.prev_own_ref
  13.0 11.4 %all-to-all-start = ((f32[256,1,128]{2,1,0:T(1,128)}), f32[256,1,128]{2,1,0:T(1,128)S(1)}, u32[]{:S(2)}, u32[]{:S(2)}) async-start(f32[256,1,128]{2,1,0:T(1,128)} %bitcast.2), calls=%async_computation | async-start | bytes 262144 | tf_op jit(solution)/shard_map/all_to_all | solution.py:375
  24.3 0.2 pack.1
  24.6 1.5 %collective-permute-start.5 = (bf16[128,512]{1,0:T(8,128)(2,1)S(1)}, bf16[128,512]{1,0:T(8,128)(2,1)S(1)}, u32[]{:S(2)}, u32[]{:S(2)}) collective-permute-start(bf16[128,512]{1,0:T(8,128)(2,1)S(1)} %get-tuple-element.42), channel_id=1, source_target_pairs={{0,16},{16,32},{32,48},{48,0},{1,17},{17,33},{33,49},{49,1},{2,18}... | collective-permute-start | bytes 393224 | tf_op jit(solution)/shard_map/ppermute | solution.py:386
  26.0 1.3 %collective-permute-start.6 = (bf16[128,512]{1,0:T(8,128)(2,1)S(1)}, bf16[128,512]{1,0:T(8,128)(2,1)S(1)}, u32[]{:S(2)}, u32[]{:S(2)}) collective-permute-start(bf16[128,512]{1,0:T(8,128)(2,1)S(1)} %get-tuple-element.43), channel_id=1, source_target_pairs={{0,48},{16,0},{32,16},{48,32},{1,49},{17,1},{33,17},{49,33},{2,50}... | collective-permute-start | bytes 393224 | tf_op jit(solution)/shard_map/ppermute | solution.py:387
  27.3 9.8 %all-to-all-done = f32[256,1,128]{2,1,0:T(1,128)S(1)} async-done(((f32[256,1,128]{2,1,0:T(1,128)}), f32[256,1,128]{2,1,0:T(1,128)S(1)}, u32[]{:S(2)}, u32[]{:S(2)}) %all-to-all-start) | async-done | bytes 131104 | tf_op jit(solution)/shard_map/all_to_all | solution.py:375
  37.2 2.5 %fetch.1 = (f32[8,512]{1,0:T(8,128)S(1)}, bf16[128,512]{1,0:T(8,128)(2,1)S(1)}, bf16[128,512]{1,0:T(8,128)(2,1)S(1)}, bf16[2,3,3,512,256]{4,3,2,1,0:T(8,128)(2,1)S(1)}) custom-call(f32[256,128]{1,0:T(8,128)S(1)} %bitcast.16, bf16[128,512]{1,0:T(8,128)(2,1)S(1)} %get-tuple-element.37.now_ref, bf16[128,512]{1,0:T(8,128)(2,1)S(1)} %get-tuple-element.38.prev_ref, ...), custom_call_target="tpu_custom_call" | custom-call | tf_op jit(solution)/shard_map/fetch/pallas_call | solution.py:388
  39.6 0.0 collective-permute-done.5.above_ref
  39.6 0.0 collective-permute-done.6.below_ref
  39.7 0.0 copy-start
  39.7 0.0 copy-start.2
  39.7 0.0 copy-start.3
  39.7 0.0 copy-start.4
  39.7 3.2 %up.1 = (bf16[6,192,256]{2,1,0:T(8,128)(2,1)S(1)}, f32[256,128]{1,0:T(8,128)S(1)}, bf16[3,3,256,256]{3,2,1,0:T(8,128)(2,1)S(1)}) custom-call(f32[8,512]{1,0:T(8,128)S(1)} %get-tuple-element.39.coef_ref, bf16[128,512]{1,0:T(8,128)(2,1)S(1)} %get-tuple-element.40.act_ref, bf16[128,512]{1,0:T(8,128)(2,1)S(1)} %get-tuple-element.41.act_prev_ref, ...), custom_call_target="tpu_custom_call" | custom-call | tf_op jit(solution)/shard_map/up/pallas_call | solution.py:408
  42.9 18.6 %all_to_all.22 = f32[256,1,128]{2,1,0:T(1,128)S(1)} all-to-all(f32[256,1,128]{2,1,0:T(1,128)S(1)} %bitcast.18), channel_id=1, replica_groups=mesh['tm'=4,'row'=4,'col'=16] {'tm','row','col'}, dimensions={0} | all-to-all | bytes 262144 | tf_op jit(solution)/shard_map/all_to_all | solution.py:425
  61.6 0.0 copy-done
  61.6 0.0 copy-done.2
  61.6 0.0 copy-done.3
  61.6 0.0 copy-done.4
  61.6 3.7 %res.1 = bf16[4,20,4,256]{3,2,1,0:T(4,128)(2,1)} custom-call(f32[256,128]{1,0:T(8,128)S(1)} %bitcast.17, f32[1,256]{1,0:T(1,128)S(1)} %bitcast.20, f32[1,256]{1,0:T(1,128)S(1)} %bitcast.21, f32[1,256]{1,0:T(1,128)S(1)} %bitcast.22, bf16[6,192,256]{2,1,0:T(8,128)(2,1)S(1)} %get-tuple-element.47.hid_ref, bf16[720,192]{1,0:T(8,128)(2,1)S(1)} %copy-done, ...), custom_call_target="tpu_custom_call" | custom-call | tf_op jit(solution)/shard_map/res/pallas_call | solution.py:428
  (1 shorter events, 0.0 us)
Async XLA Ops:
  0.0 0.9 %copy-start.1 = (bf16[4,2,10,512]{3,1,2,0:T(2,128)(2,1)S(1)}, bf16[4,2,10,512]{3,1,2,0:T(2,128)(2,1)}, u32[]{:S(2)}) copy-start(bf16[4,2,10,512]{3,1,2,0:T(2,128)(2,1)} %param.10) | copy-start | bytes 245764
  1.1 11.9 %collective-permute-start.4 = (bf16[128,512]{1,0:T(8,128)(2,1)S(1)}, bf16[128,512]{1,0:T(8,128)(2,1)S(1)}, u32[]{:S(2)}, u32[]{:S(2)}) collective-permute-start(bf16[128,512]{1,0:T(8,128)(2,1)S(1)} %get-tuple-element.27.x_ref.own_ref), channel_id=1, source_target_pairs={{0,64},{1,65},{2,66},{3,67},{4,68},{5,69},{6,70},{7,71},{8,72},{9,... | collective-permute-start | bytes 393224 | tf_op jit(solution)/shard_map/ppermute | solution.py:321
  3.3 9.6 %collective-permute-start.2 = (bf16[16,512]{1,0:T(8,128)(2,1)S(1)}, bf16[16,512]{1,0:T(8,128)(2,1)S(1)}, u32[]{:S(2)}, u32[]{:S(2)}) collective-permute-start(bf16[16,512]{1,0:T(8,128)(2,1)S(1)} %get-tuple-element.29), channel_id=1, source_target_pairs={{0,79},{1,66},{2,65},{3,68},{4,67},{5,70},{6,69},{7,72},{8,71},{9,... | collective-permute-start | bytes 49160 | tf_op jit(solution)/shard_map/ppermute | solution.py:321
  6.8 6.1 %collective-permute-start = (bf16[16,512]{1,0:T(8,128)(2,1)S(1)}, bf16[16,512]{1,0:T(8,128)(2,1)S(1)}, u32[]{:S(2)}, u32[]{:S(2)}) collective-permute-start(bf16[16,512]{1,0:T(8,128)(2,1)S(1)} %get-tuple-element.29), channel_id=1, source_target_pairs={{0,15},{1,2},{2,1},{3,4},{4,3},{5,6},{6,5},{7,8},{8,7},{9,10},{10,... | collective-permute-start | bytes 49160 | tf_op jit(solution)/shard_map/ppermute | solution.py:321
  6.8 6.2 %collective-permute-start.3 = (bf16[16,512]{1,0:T(8,128)(2,1)S(1)}, bf16[16,512]{1,0:T(8,128)(2,1)S(1)}, u32[]{:S(2)}, u32[]{:S(2)}) collective-permute-start(bf16[16,512]{1,0:T(8,128)(2,1)S(1)} %get-tuple-element.30), channel_id=1, source_target_pairs={{0,65},{1,64},{2,67},{3,66},{4,69},{5,68},{6,71},{7,70},{8,73},{9,... | collective-permute-start | bytes 49160 | tf_op jit(solution)/shard_map/ppermute | solution.py:321
  11.2 1.8 %collective-permute-start.1 = (bf16[16,512]{1,0:T(8,128)(2,1)S(1)}, bf16[16,512]{1,0:T(8,128)(2,1)S(1)}, u32[]{:S(2)}, u32[]{:S(2)}) collective-permute-start(bf16[16,512]{1,0:T(8,128)(2,1)S(1)} %get-tuple-element.30), channel_id=1, source_target_pairs={{0,1},{1,0},{2,3},{3,2},{4,5},{5,4},{6,7},{7,6},{8,9},{9,8},{10,11... | collective-permute-start | bytes 49160 | tf_op jit(solution)/shard_map/ppermute | solution.py:321
  13.0 24.2 %all-to-all-start = ((f32[256,1,128]{2,1,0:T(1,128)}), f32[256,1,128]{2,1,0:T(1,128)S(1)}, u32[]{:S(2)}, u32[]{:S(2)}) async-start(f32[256,1,128]{2,1,0:T(1,128)} %bitcast.2), calls=%async_computation | async-start | bytes 262144 | tf_op jit(solution)/shard_map/all_to_all | solution.py:375
  24.6 15.1 %collective-permute-start.5 = (bf16[128,512]{1,0:T(8,128)(2,1)S(1)}, bf16[128,512]{1,0:T(8,128)(2,1)S(1)}, u32[]{:S(2)}, u32[]{:S(2)}) collective-permute-start(bf16[128,512]{1,0:T(8,128)(2,1)S(1)} %get-tuple-element.42), channel_id=1, source_target_pairs={{0,16},{16,32},{32,48},{48,0},{1,17},{17,33},{33,49},{49,1},{2,18}... | collective-permute-start | bytes 393224 | tf_op jit(solution)/shard_map/ppermute | solution.py:386
  26.0 13.6 %collective-permute-start.6 = (bf16[128,512]{1,0:T(8,128)(2,1)S(1)}, bf16[128,512]{1,0:T(8,128)(2,1)S(1)}, u32[]{:S(2)}, u32[]{:S(2)}) collective-permute-start(bf16[128,512]{1,0:T(8,128)(2,1)S(1)} %get-tuple-element.43), channel_id=1, source_target_pairs={{0,48},{16,0},{32,16},{48,32},{1,49},{17,1},{33,17},{49,33},{2,50}... | collective-permute-start | bytes 393224 | tf_op jit(solution)/shard_map/ppermute | solution.py:387
  39.7 21.9 %copy-start = (bf16[720,192]{1,0:T(8,128)(2,1)S(1)}, bf16[720,192]{1,0:T(8,128)(2,1)}, u32[]{:S(2)}) copy-start(bf16[720,192]{1,0:T(8,128)(2,1)} %constant.2.clone.pick_ref) | copy-start | bytes 829444
  39.7 21.9 %copy-start.2 = (f32[256]{0:T(256)S(1)}, f32[256]{0:T(256)}, u32[]{:S(2)}) copy-start(f32[256]{0:T(256)} %param.15) | copy-start | bytes 3076
  39.7 21.9 %copy-start.3 = (f32[256]{0:T(256)S(1)}, f32[256]{0:T(256)}, u32[]{:S(2)}) copy-start(f32[256]{0:T(256)} %param.16) | copy-start | bytes 3076
  39.7 21.9 %copy-start.4 = (f32[256]{0:T(256)S(1)}, f32[256]{0:T(256)}, u32[]{:S(2)}) copy-start(f32[256]{0:T(256)} %param.18) | copy-start | bytes 3076
